TPU v7x, 32 devices: a whole 2x2x4 slice. The times are simulated.
32 devices in a mesh: dp: 2 (over core), expert: 16 (over z, y, x).
Axes of the slice: x: 2, y: 2, z: 4, core: 2. Of those that a mesh axis runs over, the one named last changes fastest.
Arguments:
- tokens_in: bfloat16 [12288, 1280], P(('dp', 'expert')), may hold values from -6 to 6
- lengths: int32 [32], P(('dp', 'expert')), may hold values from 48 to 384, as said below
- key_keep: int32 [12288], P(('dp', 'expert')), may hold values 0 or 1
- routes: int32 [12288, 7], P(('dp', 'expert')), may hold values from 0 to 15, all different within a row; in each aligned block of 384 rows (0 to 383, 384 to 767, ...) at most 189 rows name the same one
- cotangent: bfloat16 [12288, 1280], P(('dp', 'expert')), may hold values from -6 to 6
- attention_in: float32 [3, 1280, 1280], P(None, None, ('dp', 'expert')), may hold values from -0.15625 to 0.15625
- attention_in_momentum: float32 [3, 1280, 1280], P(None, None, ('dp', 'expert'))
- attention_in_average: float32 [3, 1280, 1280], P(None, None, ('dp', 'expert')), may hold values from -0.15625 to 0.15625
- attention_out: float32 [1280, 1280], P(None, ('dp', 'expert')), may hold values from -1.25 to 1.25
- attention_out_momentum: float32 [1280, 1280], P(None, ('dp', 'expert'))
- attention_out_average: float32 [1280, 1280], P(None, ('dp', 'expert')), may hold values from -1.25 to 1.25
- shared_in: float32 [2, 1280, 896], P(None, ('dp', 'expert')), may hold values from -0.15625 to 0.15625
- shared_in_momentum: float32 [2, 1280, 896], P(None, ('dp', 'expert'))
- shared_in_average: float32 [2, 1280, 896], P(None, ('dp', 'expert')), may hold values from -0.15625 to 0.15625
- shared_down: float32 [896, 1280], P(None, ('dp', 'expert')), may hold values from -0.375 to 0.375
- shared_down_momentum: float32 [896, 1280], P(None, ('dp', 'expert'))
- shared_down_average: float32 [896, 1280], P(None, ('dp', 'expert')), may hold values from -0.375 to 0.375
- router: float32 [1280, 16], P(('dp', 'expert')), may hold values from -0.078125 to 0.078125
- router_momentum: float32 [1280, 16], P(('dp', 'expert'))
- router_average: float32 [1280, 16], P(('dp', 'expert')), may hold values from -0.078125 to 0.078125
- norm_gains: float32 [2, 1280], P(None, ('dp', 'expert')), may hold values from 0.5 to 1.5
- norm_gains_momentum: float32 [2, 1280], P(None, ('dp', 'expert'))
- norm_gains_average: float32 [2, 1280], P(None, ('dp', 'expert')), may hold values from 0.5 to 1.5
- expert_in: float32 [16, 2, 1280, 896], P('expert', None, 'dp'), may hold values from -0.15625 to 0.15625
- expert_in_momentum: float32 [16, 2, 1280, 896], P('expert', None, 'dp')
- expert_in_average: float32 [16, 2, 1280, 896], P('expert', None, 'dp'), may hold values from -0.15625 to 0.15625
- expert_down: float32 [16, 896, 1280], P('expert', 'dp'), may hold values from -0.75 to 0.75
- expert_down_momentum: float32 [16, 896, 1280], P('expert', 'dp')
- expert_down_average: float32 [16, 896, 1280], P('expert', 'dp'), may hold values from -0.75 to 0.75
Outputs:
- output: bfloat16 [12288, 1280], P(('dp', 'expert'))
- input_grad: float32 [12288, 1280], P(('dp', 'expert'))
- new_attention_in: float32 [3, 1280, 1280], P(None, None, ('dp', 'expert'))
- new_attention_in_momentum: float32 [3, 1280, 1280], P(None, None, ('dp', 'expert'))
- new_attention_in_average: float32 [3, 1280, 1280], P(None, None, ('dp', 'expert'))
- new_attention_out: float32 [1280, 1280], P(None, ('dp', 'expert'))
- new_attention_out_momentum: float32 [1280, 1280], P(None, ('dp', 'expert'))
- new_attention_out_average: float32 [1280, 1280], P(None, ('dp', 'expert'))
- new_shared_in: float32 [2, 1280, 896], P(None, ('dp', 'expert'))
- new_shared_in_momentum: float32 [2, 1280, 896], P(None, ('dp', 'expert'))
- new_shared_in_average: float32 [2, 1280, 896], P(None, ('dp', 'expert'))
- new_shared_down: float32 [896, 1280], P(None, ('dp', 'expert'))
- new_shared_down_momentum: float32 [896, 1280], P(None, ('dp', 'expert'))
- new_shared_down_average: float32 [896, 1280], P(None, ('dp', 'expert'))
- new_router: float32 [1280, 16], P(('dp', 'expert'))
- new_router_momentum: float32 [1280, 16], P(('dp', 'expert'))
- new_router_average: float32 [1280, 16], P(('dp', 'expert'))
- new_norm_gains: float32 [2, 1280], P(None, ('dp', 'expert'))
- new_norm_gains_momentum: float32 [2, 1280], P(None, ('dp', 'expert'))
- new_norm_gains_average: float32 [2, 1280], P(None, ('dp', 'expert'))
- new_expert_in: float32 [16, 2, 1280, 896], P('expert', None, 'dp')
- new_expert_in_momentum: float32 [16, 2, 1280, 896], P('expert', None, 'dp')
- new_expert_in_average: float32 [16, 2, 1280, 896], P('expert', None, 'dp')
- new_expert_down: float32 [16, 896, 1280], P('expert', 'dp')
- new_expert_down_momentum: float32 [16, 896, 1280], P('expert', 'dp')
- new_expert_down_average: float32 [16, 896, 1280], P('expert', 'dp')
Inputs may be any that keep to these rules, and one draw needn't show every extreme that they name: `lengths`: every sequence has at least 48 used tokens, and some sequence uses all 384. `routes`: the 7 experts of a token differ; among the rows of one device at most 189 name one expert, a bound that some block reaches.
All inputs are finite; a program needn't handle non-finite values. No bound on the sum of `key_keep` on one device may be relied on, other than what follows from the above.
Results may differ from a plain program's by a relative error of at most 0.015.
The roundings to bfloat16 on the way count: a program that leaves them out, or rounds other values in their place, can miss the bound.
Values may be sent and summed in bfloat16 or wider, within the bound.
A program may use at most 320 MiB of HBM per device.

v0:
```python
import jax
import jax.numpy as jnp
from jax import lax
from jax.sharding import PartitionSpec as P

HD = 128
STEP = 4


eps_norm = 1e-06
theta_base = 10000.0
momentum_decay = 0.9
mask_fill = -1e30
rate_attention_in = 2e-05
rate_attention_out = 0.002
rate_shared_in = 3e-05
rate_shared_down = 0.0002
rate_router = 1.5e-05
rate_gains = 0.0002
rate_expert_in = 0.0004
rate_expert_down = 0.008


def rope_tables(length, head_width):
    half_width = head_width // 2
    frequency = theta_base ** (-(jnp.arange(half_width, dtype=jnp.float32) * 2.0 / head_width))
    angles = jnp.arange(length, dtype=jnp.float32)[:, None] * frequency[None, :]
    return (jnp.cos(angles)[:, None, :], jnp.sin(angles)[:, None, :])


def rotate(values, cosine, sine_table):
    half_width = values.shape[-1] // 2
    front_half = values[..., :half_width]
    back_half = values[..., half_width:]
    return jnp.concatenate(
        [
            front_half * cosine - back_half * sine_table,
            back_half * cosine + front_half * sine_table,
        ],
        axis=-1,
    )


def unrotate(values, cosine, sine_table):
    half_width = values.shape[-1] // 2
    front_half = values[..., :half_width]
    back_half = values[..., half_width:]
    return jnp.concatenate(
        [
            front_half * cosine + back_half * sine_table,
            back_half * cosine - front_half * sine_table,
        ],
        axis=-1,
    )


def allowed_keys(length, keep_flags):
    amount = keep_flags.shape[0]
    position = jnp.arange(amount)
    causal = position[None, :] <= position[:, None]
    usable = (position < length) & (keep_flags == 1)
    return causal & (usable[None, :] | (position[None, :] == position[:, None]))


def silu_parts(values):
    logistic = jax.nn.sigmoid(values)
    return (values * logistic, logistic * (1.0 + values * (1.0 - logistic)))


def advance(weight, moment, average, gradient, step_rate):
    moment_new = momentum_decay * moment + gradient
    weight_new = weight - step_rate * (gradient + momentum_decay * moment_new)
    average_new = average + (weight_new - average) / (STEP + 1)
    return (weight_new, moment_new, average_new)


def local(
    tokens_in,
    lengths,
    key_keep,
    routes,
    cotangent,
    attention_in,
    attention_in_momentum,
    attention_in_average,
    attention_out,
    attention_out_momentum,
    attention_out_average,
    shared_in,
    shared_in_momentum,
    shared_in_average,
    shared_down,
    shared_down_momentum,
    shared_down_average,
    router,
    router_momentum,
    router_average,
    norm_gains,
    norm_gains_momentum,
    norm_gains_average,
    expert_in,
    expert_in_momentum,
    expert_in_average,
    expert_down,
    expert_down_momentum,
    expert_down_average,
):
    dense = (
        lax.all_gather(attention_in.astype(jnp.bfloat16), ("dp", "expert"), axis=2, tiled=True),
        lax.all_gather(attention_out.astype(jnp.bfloat16), ("dp", "expert"), axis=1, tiled=True),
        lax.all_gather(shared_in.astype(jnp.bfloat16), ("dp", "expert"), axis=1, tiled=True),
        lax.all_gather(shared_down.astype(jnp.bfloat16), ("dp", "expert"), axis=1, tiled=True),
        lax.all_gather(router.astype(jnp.bfloat16), ("dp", "expert"), axis=0, tiled=True),
        lax.all_gather(norm_gains.astype(jnp.bfloat16), ("dp", "expert"), axis=1, tiled=True),
    )
    weights_in, weights_out, shared_pair, shared_back, router_low, gains_low = dense
    experts_pair, experts_back = (
        lax.all_gather(expert_in.astype(jnp.bfloat16), "dp", axis=2, tiled=True),
        lax.all_gather(expert_down.astype(jnp.bfloat16), "dp", axis=1, tiled=True),
    )
    tokens = tokens_in.shape[0]
    model_width = tokens_in.shape[1]
    head_count = model_width // HD
    top_count = routes.shape[1]
    experts = router_low.shape[1]
    capacity = 9 * tokens * top_count // (8 * experts)
    scaling = HD ** (-0.5)
    inputs = tokens_in.astype(jnp.float32)
    gain_one = gains_low[0].astype(jnp.float32)
    gain_two = gains_low[1].astype(jnp.float32)
    rstd_one = lax.rsqrt(jnp.mean(inputs * inputs, axis=-1, keepdims=True) + eps_norm)
    normed_one = (inputs * rstd_one * gain_one).astype(jnp.bfloat16)
    projected = jnp.einsum(
        "td,mde->mte", normed_one, weights_in, preferred_element_type=jnp.float32
    )
    cosine, sine_table = rope_tables(tokens, HD)
    split_shape = (tokens, head_count, HD)
    query = rotate(projected[0].reshape(split_shape), cosine, sine_table).astype(jnp.bfloat16)
    key_rot = rotate(projected[1].reshape(split_shape), cosine, sine_table).astype(jnp.bfloat16)
    value = projected[2].reshape(split_shape).astype(jnp.bfloat16)
    allowed = allowed_keys(lengths[0], key_keep)[None]

    def attention_scores():
        raw = (
            jnp.einsum("qhd,khd->hqk", query, key_rot, preferred_element_type=jnp.float32) * scaling
        )
        return jnp.where(allowed, raw, mask_fill)

    scores = attention_scores()
    row_top = jnp.max(scores, axis=-1, keepdims=True)
    exps = jnp.exp(scores - row_top)
    totals = jnp.sum(exps, axis=-1, keepdims=True)
    log_total = row_top + jnp.log(totals)
    attended = jnp.einsum(
        "hqk,khd->qhd",
        (exps / totals).astype(jnp.bfloat16),
        value,
        preferred_element_type=jnp.float32,
    )
    attended = attended.reshape(tokens, model_width).astype(jnp.bfloat16)
    branch = jnp.dot(attended, weights_out, preferred_element_type=jnp.float32)
    hidden = inputs + branch
    rstd_two = lax.rsqrt(jnp.mean(hidden * hidden, axis=-1, keepdims=True) + eps_norm)
    normed_two = (hidden * rstd_two * gain_two).astype(jnp.bfloat16)
    logits = jnp.dot(normed_two, router_low, preferred_element_type=jnp.float32)
    chosen = jnp.take_along_axis(logits, routes, axis=1)
    chosen_top = jnp.max(chosen, axis=-1, keepdims=True)
    chosen_exps = jnp.exp(chosen - chosen_top)
    gating = chosen_exps / jnp.sum(chosen_exps, axis=-1, keepdims=True)
    position = jnp.arange(tokens, dtype=jnp.int32)
    usable = position < lengths[0]
    gating_live = gating * usable[:, None].astype(jnp.float32)
    shared_gate = jnp.dot(normed_two, shared_pair[0], preferred_element_type=jnp.float32)
    shared_up = jnp.dot(normed_two, shared_pair[1], preferred_element_type=jnp.float32)
    shared_silu, shared_slope = silu_parts(shared_gate)
    shared_hidden = (shared_silu * shared_up).astype(jnp.bfloat16)
    shared_result = jnp.dot(shared_hidden, shared_back, preferred_element_type=jnp.float32)
    ids_flat = routes.reshape(tokens * top_count)
    live_flat = jnp.repeat(usable, top_count)
    chosen_hot = (
        (ids_flat[:, None] == jnp.arange(experts, dtype=jnp.int32)[None, :]) & live_flat[:, None]
    ).astype(jnp.int32)
    slot_index = jnp.sum((jnp.cumsum(chosen_hot, axis=0) - chosen_hot) * chosen_hot, axis=1)
    target = jnp.where(live_flat, ids_flat * capacity + slot_index, experts * capacity)
    slot_table = jnp.full((experts * capacity,), tokens * top_count, jnp.int32)
    slot_table = slot_table.at[target].set(
        jnp.arange(tokens * top_count, dtype=jnp.int32), mode="drop"
    )
    owner_rows = slot_table // top_count
    rows_padded = jnp.concatenate([normed_two, jnp.zeros((1, model_width), jnp.bfloat16)], axis=0)
    outgoing = rows_padded[owner_rows].reshape(experts, 1, capacity, model_width)
    received = lax.all_to_all(outgoing, "expert", split_axis=0, concat_axis=1, tiled=True)
    gate_rows = jnp.einsum(
        "ensd,edf->ensf", received, experts_pair[:, 0], preferred_element_type=jnp.float32
    )
    up_rows = jnp.einsum(
        "ensd,edf->ensf", received, experts_pair[:, 1], preferred_element_type=jnp.float32
    )
    silu_rows, slope_rows = silu_parts(gate_rows)
    inner = (silu_rows * up_rows).astype(jnp.bfloat16)
    result_rows = jnp.einsum(
        "ensf,efd->ensd", inner, experts_back, preferred_element_type=jnp.float32
    ).astype(jnp.bfloat16)
    back_rows = lax.all_to_all(result_rows, "expert", split_axis=1, concat_axis=0, tiled=True)
    returned_flat = jnp.concatenate(
        [
            back_rows.reshape(experts * capacity, model_width),
            jnp.zeros((1, model_width), jnp.bfloat16),
        ],
        axis=0,
    )
    picked = returned_flat[target].reshape(tokens, top_count, model_width).astype(jnp.float32)
    routed = jnp.einsum("tk,tkd->td", gating_live, picked)
    output = (hidden + shared_result + routed).astype(jnp.bfloat16)
    grad_out = cotangent.astype(jnp.float32)
    grad_shared_down = jnp.dot(shared_hidden.T, cotangent, preferred_element_type=jnp.float32)
    grad_shared_hidden = jnp.dot(cotangent, shared_back.T, preferred_element_type=jnp.float32)
    grad_shared_gate = (grad_shared_hidden * shared_up * shared_slope).astype(jnp.bfloat16)
    grad_shared_up = (grad_shared_hidden * shared_silu).astype(jnp.bfloat16)
    grad_shared_in = jnp.stack(
        [
            jnp.dot(normed_two.T, grad_shared_gate, preferred_element_type=jnp.float32),
            jnp.dot(normed_two.T, grad_shared_up, preferred_element_type=jnp.float32),
        ],
        axis=0,
    )
    grad_normed_two = jnp.dot(
        grad_shared_gate, shared_pair[0].T, preferred_element_type=jnp.float32
    ) + jnp.dot(grad_shared_up, shared_pair[1].T, preferred_element_type=jnp.float32)
    grad_gating = jnp.einsum("td,tkd->tk", grad_out, picked) * usable[:, None].astype(jnp.float32)
    grad_chosen = gating * (grad_gating - jnp.sum(gating * grad_gating, axis=-1, keepdims=True))
    route_hot = (routes[:, :, None] == jnp.arange(experts, dtype=jnp.int32)[None, None, :]).astype(
        jnp.float32
    )
    grad_logits = jnp.einsum("tk,tke->te", grad_chosen, route_hot).astype(jnp.bfloat16)
    grad_router = jnp.dot(normed_two.T, grad_logits, preferred_element_type=jnp.float32)
    grad_normed_two = grad_normed_two + jnp.dot(
        grad_logits, router_low.T, preferred_element_type=jnp.float32
    )
    grad_padded = jnp.concatenate([grad_out, jnp.zeros((1, model_width), jnp.float32)], axis=0)
    gating_padded = jnp.concatenate(
        [gating_live.reshape(tokens * top_count), jnp.zeros((1,), jnp.float32)], axis=0
    )
    to_send = (grad_padded[owner_rows] * gating_padded[slot_table][:, None]).astype(jnp.bfloat16)
    arrived = lax.all_to_all(
        to_send.reshape(experts, 1, capacity, model_width),
        "expert",
        split_axis=0,
        concat_axis=1,
        tiled=True,
    )
    gate_rows = jnp.einsum(
        "ensd,edf->ensf", received, experts_pair[:, 0], preferred_element_type=jnp.float32
    )
    up_rows = jnp.einsum(
        "ensd,edf->ensf", received, experts_pair[:, 1], preferred_element_type=jnp.float32
    )
    silu_rows, slope_rows = silu_parts(gate_rows)
    inner = (silu_rows * up_rows).astype(jnp.bfloat16)
    grad_expert_down = jnp.einsum(
        "ensf,ensd->efd", inner, arrived, preferred_element_type=jnp.float32
    )
    grad_inner = jnp.einsum(
        "ensd,efd->ensf", arrived, experts_back, preferred_element_type=jnp.float32
    )
    grad_gate_rows = (grad_inner * up_rows * slope_rows).astype(jnp.bfloat16)
    grad_up_rows = (grad_inner * silu_rows).astype(jnp.bfloat16)
    grad_expert_in = jnp.stack(
        [
            jnp.einsum(
                "ensd,ensf->edf", received, grad_gate_rows, preferred_element_type=jnp.float32
            ),
            jnp.einsum(
                "ensd,ensf->edf", received, grad_up_rows, preferred_element_type=jnp.float32
            ),
        ],
        axis=1,
    )
    grad_rows = (
        jnp.einsum(
            "ensf,edf->ensd", grad_gate_rows, experts_pair[:, 0], preferred_element_type=jnp.float32
        )
        + jnp.einsum(
            "ensf,edf->ensd", grad_up_rows, experts_pair[:, 1], preferred_element_type=jnp.float32
        )
    ).astype(jnp.bfloat16)
    returned_grad = lax.all_to_all(
        grad_rows, "expert", split_axis=1, concat_axis=0, tiled=True
    ).reshape(experts * capacity, model_width)
    grad_normed_two = grad_normed_two.at[owner_rows].add(
        returned_grad.astype(jnp.float32), mode="drop"
    )
    scaled_two = grad_normed_two * gain_two
    grad_gain_two = jnp.sum(grad_normed_two * hidden * rstd_two, axis=0)
    grad_hidden = (
        grad_out
        + rstd_two * scaled_two
        - hidden * rstd_two**3 * jnp.mean(scaled_two * hidden, axis=-1, keepdims=True)
    )
    grad_branch = grad_hidden.astype(jnp.bfloat16)
    grad_attention_out = jnp.dot(attended.T, grad_branch, preferred_element_type=jnp.float32)
    grad_attended = (
        jnp.dot(grad_branch, weights_out.T, preferred_element_type=jnp.float32)
        .astype(jnp.bfloat16)
        .reshape(split_shape)
    )
    probs = jnp.exp(attention_scores() - log_total)
    grad_probs = jnp.einsum(
        "qhd,khd->hqk", grad_attended, value, preferred_element_type=jnp.float32
    )
    grad_scores = (
        probs * (grad_probs - jnp.sum(probs * grad_probs, axis=-1, keepdims=True))
    ).astype(jnp.bfloat16)
    grad_query = (
        jnp.einsum("hqk,khd->qhd", grad_scores, key_rot, preferred_element_type=jnp.float32)
        * scaling
    )
    grad_key = (
        jnp.einsum("hqk,qhd->khd", grad_scores, query, preferred_element_type=jnp.float32) * scaling
    )
    grad_value = jnp.einsum(
        "hqk,qhd->khd",
        probs.astype(jnp.bfloat16),
        grad_attended,
        preferred_element_type=jnp.float32,
    )
    grad_projected = jnp.stack(
        [
            unrotate(grad_query, cosine, sine_table),
            unrotate(grad_key, cosine, sine_table),
            grad_value,
        ],
        axis=0,
    )
    grad_projected = grad_projected.reshape(3, tokens, model_width).astype(jnp.bfloat16)
    grad_attention_in = jnp.einsum(
        "td,mte->mde", normed_one, grad_projected, preferred_element_type=jnp.float32
    )
    grad_normed_one = jnp.einsum(
        "mte,mde->td", grad_projected, weights_in, preferred_element_type=jnp.float32
    )
    scaled_one = grad_normed_one * gain_one
    grad_gain_one = jnp.sum(grad_normed_one * inputs * rstd_one, axis=0)
    input_grad = (
        grad_hidden
        + rstd_one * scaled_one
        - inputs * rstd_one**3 * jnp.mean(scaled_one * inputs, axis=-1, keepdims=True)
    )
    grad_gains = jnp.stack([grad_gain_one, grad_gain_two], axis=0)
    summed_in, summed_out, summed_shared_in, summed_shared_down, summed_router, summed_gains = (
        lax.psum_scatter(grad_attention_in, ("dp", "expert"), scatter_dimension=2, tiled=True),
        lax.psum_scatter(grad_attention_out, ("dp", "expert"), scatter_dimension=1, tiled=True),
        lax.psum_scatter(grad_shared_in, ("dp", "expert"), scatter_dimension=1, tiled=True),
        lax.psum_scatter(grad_shared_down, ("dp", "expert"), scatter_dimension=1, tiled=True),
        lax.psum_scatter(grad_router, ("dp", "expert"), scatter_dimension=0, tiled=True),
        lax.psum_scatter(grad_gains, ("dp", "expert"), scatter_dimension=1, tiled=True),
    )
    summed_expert_in, summed_expert_down = (
        lax.psum_scatter(
            grad_expert_in.astype(jnp.bfloat16), "dp", scatter_dimension=2, tiled=True
        ).astype(jnp.float32),
        lax.psum_scatter(
            grad_expert_down.astype(jnp.bfloat16), "dp", scatter_dimension=1, tiled=True
        ).astype(jnp.float32),
    )
    upd_attn_in = advance(
        attention_in, attention_in_momentum, attention_in_average, summed_in, rate_attention_in
    )
    upd_attn_out = advance(
        attention_out, attention_out_momentum, attention_out_average, summed_out, rate_attention_out
    )
    upd_shared_in = advance(
        shared_in, shared_in_momentum, shared_in_average, summed_shared_in, rate_shared_in
    )
    upd_shared_down = advance(
        shared_down, shared_down_momentum, shared_down_average, summed_shared_down, rate_shared_down
    )
    upd_router = advance(router, router_momentum, router_average, summed_router, rate_router)
    upd_gains = advance(
        norm_gains, norm_gains_momentum, norm_gains_average, summed_gains, rate_gains
    )
    upd_expert_in = advance(
        expert_in, expert_in_momentum, expert_in_average, summed_expert_in, rate_expert_in
    )
    upd_expert_down = advance(
        expert_down, expert_down_momentum, expert_down_average, summed_expert_down, rate_expert_down
    )
    return (
        output,
        input_grad,
        upd_attn_in[0],
        upd_attn_in[1],
        upd_attn_in[2],
        upd_attn_out[0],
        upd_attn_out[1],
        upd_attn_out[2],
        upd_shared_in[0],
        upd_shared_in[1],
        upd_shared_in[2],
        upd_shared_down[0],
        upd_shared_down[1],
        upd_shared_down[2],
        upd_router[0],
        upd_router[1],
        upd_router[2],
        upd_gains[0],
        upd_gains[1],
        upd_gains[2],
        upd_expert_in[0],
        upd_expert_in[1],
        upd_expert_in[2],
        upd_expert_down[0],
        upd_expert_down[1],
        upd_expert_down[2],
    )


def solution(mesh):
    in_specs = (
        P(("dp", "expert"), None),
        P(("dp", "expert")),
        P(("dp", "expert")),
        P(("dp", "expert"), None),
        P(("dp", "expert"), None),
        P(None, None, ("dp", "expert")),
        P(None, None, ("dp", "expert")),
        P(None, None, ("dp", "expert")),
        P(None, ("dp", "expert")),
        P(None, ("dp", "expert")),
        P(None, ("dp", "expert")),
        P(None, ("dp", "expert"), None),
        P(None, ("dp", "expert"), None),
        P(None, ("dp", "expert"), None),
        P(None, ("dp", "expert")),
        P(None, ("dp", "expert")),
        P(None, ("dp", "expert")),
        P(("dp", "expert"), None),
        P(("dp", "expert"), None),
        P(("dp", "expert"), None),
        P(None, ("dp", "expert")),
        P(None, ("dp", "expert")),
        P(None, ("dp", "expert")),
        P("expert", None, "dp", None),
        P("expert", None, "dp", None),
        P("expert", None, "dp", None),
        P("expert", "dp", None),
        P("expert", "dp", None),
        P("expert", "dp", None),
    )
    out_specs = (
        P(("dp", "expert"), None),
        P(("dp", "expert"), None),
        P(None, None, ("dp", "expert")),
        P(None, None, ("dp", "expert")),
        P(None, None, ("dp", "expert")),
        P(None, ("dp", "expert")),
        P(None, ("dp", "expert")),
        P(None, ("dp", "expert")),
        P(None, ("dp", "expert"), None),
        P(None, ("dp", "expert"), None),
        P(None, ("dp", "expert"), None),
        P(None, ("dp", "expert")),
        P(None, ("dp", "expert")),
        P(None, ("dp", "expert")),
        P(("dp", "expert"), None),
        P(("dp", "expert"), None),
        P(("dp", "expert"), None),
        P(None, ("dp", "expert")),
        P(None, ("dp", "expert")),
        P(None, ("dp", "expert")),
        P("expert", None, "dp", None),
        P("expert", None, "dp", None),
        P("expert", None, "dp", None),
        P("expert", "dp", None),
        P("expert", "dp", None),
        P("expert", "dp", None),
    )
    return jax.shard_map(local, mesh=mesh, in_specs=in_specs, out_specs=out_specs, check_vma=False)
```

profile of v0, /device:TPU:0, one launch (start us, length us, event | category | flops | bytes accessed | tf_op | source)
XLA Modules:
  0.0 2034.9 jit_solution(15622376803231870734)
XLA Ops:
  15.3 69.9 %all-gather = bf16[32,40,2]{1,2,0:T(2,128)(2,1)S(1)} all-gather(bf16[1,40,2]{1,2,0:T(2,128)(2,1)S(1)} %convert_bitcast_fusion.2), channel_id=1, replica_groups=mesh['dp'=2,'expert'=16] {'dp','expert'}, dimensions={0}, use_global_device_ids=true | all-gather | bytes 5280 | tf_op jit(solution)/shard_map/all_gather | solution.py:114
  92.2 13.5 scatter_custom_fusion
  164.6 14.3 gather_fusion
  198.2 241.1 %all-gather.1 = bf16[32,40,16]{1,2,0:T(8,128)(2,1)S(1)} all-gather(bf16[1,40,16]{1,2,0:T(8,128)(2,1)S(1)} %convert_bitcast_fusion.1), channel_id=1, replica_groups=mesh['dp'=2,'expert'=16] {'dp','expert'}, dimensions={0}, use_global_device_ids=true | all-gather | bytes 42240 | tf_op jit(solution)/shard_map/all_gather | solution.py:113
  441.3 15.3 gather_fusion.2
  456.6 14.6 gather.22
  471.6 20.9 %gather_fusion.4 = f32[2688]{0:T(1024)S(1)} fusion(f32[384,16]{0,1:T(8,128)S(1)} %fusion.104, s32[2688]{0:T(1024)S(1)} %reshape.519), kind=kCustom, calls=%fused_computation.4 | custom fusion | bytes 43008 | tf_op jit(solution)/shard_map/jit(take_along_axis)/gather | solution.py:166
  493.9 17.4 gather_fusion.3
  548.2 14.1 fusion.10
  562.3 13.1 fusion.12
  575.4 112.1 %all-to-all-done.2 = bf16[16,1,189,1280]{3,2,1,0:T(8,128)(2,1)} async-done(((bf16[16,1,189,1280]{3,2,1,0:T(8,128)(2,1)}), bf16[16,1,189,1280]{3,2,1,0:T(8,128)(2,1)}, u32[]{:S(2)}, u32[]{:S(2)}) %all-to-all-start.2) | async-done | bytes 7741472 | tf_op jit(solution)/shard_map/all_to_all | solution.py:245
  687.5 21.8 %multiply_convert_fusion.1 = (bf16[16,189,896]{2,1,0:T(8,128)(2,1)}, bf16[16,189,896]{2,1,0:T(8,128)(2,1)}, bf16[16,189,896]{2,1,0:T(8,128)(2,1)}) fusion(f32[16,189,896]{2,1,0:T(8,128)} %fusion.12, f32[16,189,896]{2,1,0:T(8,128)} %fusion.10, bf16[1,896,1280]{2,1,0:T(8,128)(2,1)} %all-gather.19.cloned.1.call-done, bf16[16,1,189,1280]{3,2,1,0:T(8,128)(2,1)} %all-to-all-done.2), kind=kOutput, calls=%fused_computation.10 | convolution fusion | flops 6976972800 | bytes 47968256 | tf_op jit(solution)/shard_map/ensd,efd->ensf/dot_general | solution.py:263
  709.3 13.1 convert_bitcast_fusion
  722.4 38.7 %all-to-all-start.1 = ((bf16[1,16,189,1280]{3,2,0,1:T(8,128)(2,1)}), bf16[1,16,189,1280]{3,2,0,1:T(8,128)(2,1)}, u32[]{:S(2)}, u32[]{:S(2)}) async-start(bf16[1,16,189,1280]{3,2,0,1:T(8,128)(2,1)} %convert_bitcast_fusion), calls=%async_computation.1 | async-start | bytes 15728640 | tf_op jit(solution)/shard_map/all_to_all | solution.py:204
  761.1 14.4 fusion.47
  775.6 16.8 fusion.14
  792.3 127.8 %all-to-all-done.1 = bf16[1,16,189,1280]{3,2,0,1:T(8,128)(2,1)} async-done(((bf16[1,16,189,1280]{3,2,0,1:T(8,128)(2,1)}), bf16[1,16,189,1280]{3,2,0,1:T(8,128)(2,1)}, u32[]{:S(2)}, u32[]{:S(2)}) %all-to-all-start.1) | async-done | bytes 7741472 | tf_op jit(solution)/shard_map/all_to_all | solution.py:204
  920.2 46.2 %all-to-all-start.3 = ((bf16[1,16,189,1280]{3,2,0,1:T(8,128)(2,1)}), bf16[1,16,189,1280]{3,2,0,1:T(8,128)(2,1)}, u32[]{:S(2)}, u32[]{:S(2)}) async-start(bf16[1,16,189,1280]{3,2,0,1:T(8,128)(2,1)} %fusion.14), calls=%async_computation.3 | async-start | bytes 15728640 | tf_op jit(solution)/shard_map/all_to_all | solution.py:287
  966.4 12.6 fusion.25
  979.1 12.3 fusion.28
  991.4 12.3 fusion.31
  1027.8 19.5 gather_fusion.1
  1065.6 61.0 %all-to-all-done.3 = bf16[1,16,189,1280]{3,2,0,1:T(8,128)(2,1)} async-done(((bf16[1,16,189,1280]{3,2,0,1:T(8,128)(2,1)}), bf16[1,16,189,1280]{3,2,0,1:T(8,128)(2,1)}, u32[]{:S(2)}, u32[]{:S(2)}) %all-to-all-start.3) | async-done | bytes 7741472 | tf_op jit(solution)/shard_map/all_to_all | solution.py:287
  1126.6 12.3 reshape.537
  1140.9 30.4 %scatter_fusion = f32[384,1280]{1,0:T(8,128)S(1)} fusion(f32[384,1280]{1,0:T(8,128)S(1)} %convolution_add_fusion, s32[3024]{0:T(1024)S(1)} %copy-done.58, f32[3024,1280]{1,0:T(8,128)} %reshape.537), kind=kCustom, calls=%fused_computation.6 | custom fusion | flops 3870720 | bytes 46460736 | tf_op jit(solution)/shard_map/scatter-add | solution.py:290
  1224.3 12.1 convolution_bitcast_fusion
  1238.7 47.8 %reduce-scatter.16.cloned.1.call-done = f32[2,40,896]{2,1,0:T(8,128)} async-done(((f32[2,1280,896]{2,1,0:T(8,128)}), f32[2,40,896]{2,1,0:T(8,128)}) %reduce-scatter.16.cloned.1.call-update) | async-done | bytes 286736 | tf_op jit(solution)/shard_map/reduce_scatter | solution.py:353
  1288.5 16.8 reduce-scatter.20.cloned.1.call-done
  1342.0 40.9 %all-reduce.5 = f32[2,1280]{1,0:T(2,128)S(1)} all-reduce(f32[2,1280]{1,0:T(2,128)S(1)} %pad_maximum_fusion.14), channel_id=7, replica_groups=mesh['dp'=2,'expert'=16] {'dp','expert'}, use_global_device_ids=true, to_apply=%region_22.23.clone | all-reduce | flops 2560 | bytes 20480
  1393.2 55.5 %all-reduce.8.cloned.1.call-done = f32[1280,16]{0,1:T(8,128)} async-done(((f32[1280,16]{0,1:T(8,128)}), f32[1280,16]{0,1:T(8,128)}) %all-reduce.8.cloned.1.call-update) | async-done | bytes 81936
  1450.1 154.7 %reduce-scatter.14.cloned.1.call-done = f32[1280,40]{0,1:T(8,128)} async-done(((f32[1280,1280]{0,1:T(8,128)}), f32[1280,40]{0,1:T(8,128)}) %reduce-scatter.14.cloned.1.call-update) | async-done | bytes 204816 | tf_op jit(solution)/shard_map/reduce_scatter | solution.py:352
  1606.8 418.4 %reduce-scatter.12.cloned.1.call-done = f32[3,1280,40]{1,2,0:T(8,128)} async-done(((f32[3,1280,1280]{1,2,0:T(8,128)}), f32[3,1280,40]{1,2,0:T(8,128)}) %reduce-scatter.12.cloned.1.call-update) | async-done | bytes 614416 | tf_op jit(solution)/shard_map/reduce_scatter | solution.py:351
  (340 shorter events, 287.0 us)
Async XLA Ops:
  7.2 78.2 %copy-start.6 = (bf16[384,1280]{1,0:T(8,128)(2,1)S(1)}, bf16[384,1280]{1,0:T(8,128)(2,1)}, u32[]{:S(2)}) copy-start(bf16[384,1280]{1,0:T(8,128)(2,1)} %param.29) | copy-start | bytes 2949124
  7.2 100.6 %all-gather.9.cloned.1.call-start = ((), (), s32[]{:S(2)}) async-start(), calls=%async_computation.10 | async-start | bytes 10137600 | tf_op jit(solution)/shard_map/all_gather | solution.py:109
  9.2 150.2 %all-gather.11.cloned.1.call-start = ((), (), s32[]{:S(2)}) async-start(), calls=%async_computation.11 | async-start | bytes 3379200 | tf_op jit(solution)/shard_map/all_gather | solution.py:110
  10.9 514.0 %all-gather.13.cloned.1.call-start = ((), (), s32[]{:S(2)}) async-start(), calls=%async_computation.12 | async-start | bytes 4730880 | tf_op jit(solution)/shard_map/all_gather | solution.py:111
  85.5 78.2 %copy-start.46 = (f32[1280]{0:T(1024)}, f32[1280]{0:T(1024)S(1)}, u32[]{:S(2)}) copy-start(f32[1280]{0:T(1024)S(1)} %get-tuple-element.32) | copy-start | bytes 15364
  164.5 378.0 %copy-start.4 = (bf16[384,1280]{1,0:T(8,128)(2,1)}, bf16[384,1280]{1,0:T(8,128)(2,1)S(1)}, u32[]{:S(2)}) copy-start(bf16[384,1280]{1,0:T(8,128)(2,1)S(1)} %multiply_convert_fusion.5) | copy-start | bytes 2949124
  185.8 334.3 %all-to-all-start = ((bf16[16,1,189,1280]{3,2,1,0:T(8,128)(2,1)}), bf16[16,1,189,1280]{3,2,1,0:T(8,128)(2,1)}, u32[]{:S(2)}, u32[]{:S(2)}) async-start(bf16[16,1,189,1280]{3,2,1,0:T(8,128)(2,1)} %bitcast.213), calls=%async_computation | async-start | bytes 15728640 | tf_op jit(solution)/shard_map/all_to_all | solution.py:192
  190.6 340.6 %all-gather.15.cloned.1.call-start = ((), (), s32[]{:S(2)}) async-start(), calls=%async_computation.13 | async-start | bytes 2365440 | tf_op jit(solution)/shard_map/all_gather | solution.py:112
  191.4 356.8 %all-gather.17.cloned.1.call-start = ((), (), s32[]{:S(2)}) async-start(), calls=%async_computation.14 | async-start | bytes 6881280 | tf_op jit(solution)/shard_map/all_gather | solution.py:118
  195.4 380.0 %all-gather.19.cloned.1.call-start = ((), (), s32[]{:S(2)}) async-start(), calls=%async_computation.15 | async-start | bytes 3440640 | tf_op jit(solution)/shard_map/all_gather | solution.py:119
  520.1 167.4 %all-to-all-start.2 = ((bf16[16,1,189,1280]{3,2,1,0:T(8,128)(2,1)}), bf16[16,1,189,1280]{3,2,1,0:T(8,128)(2,1)}, u32[]{:S(2)}, u32[]{:S(2)}) async-start(bf16[16,1,189,1280]{3,2,1,0:T(8,128)(2,1)} %fusion.1), calls=%async_computation.2 | async-start | bytes 15728640 | tf_op jit(solution)/shard_map/all_to_all | solution.py:245
  524.8 712.0 %reduce-scatter.22.cloned.1.call-start = ((), (), s32[]{:S(2)}) async-start(), calls=%async_computation.22 | async-start | bytes 4730880
  539.9 746.5 %reduce-scatter.16.cloned.1.call-start = ((), (), s32[]{:S(2)}) async-start(), calls=%async_computation.18 | async-start | bytes 9461760 | tf_op jit(solution)/shard_map/reduce_scatter | solution.py:353
  575.4 133.9 %copy-start.75 = (bf16[1,896,1280]{2,1,0:T(8,128)(2,1)S(1)}, bf16[1,896,1280]{2,1,0:T(8,128)(2,1)}, u32[]{:S(2)}) copy-start(bf16[1,896,1280]{2,1,0:T(8,128)(2,1)} %all-gather.19.cloned.1.call-done) | copy-start | bytes 6881284
  722.4 53.1 %slice-start.2 = ((s8[4587520]{0:T(1024)(128)(4,1)}), s8[393216]{0:T(1024)(128)(4,1)S(1)}, s32[]{:S(2)}) async-start(s8[4587520]{0:T(1024)(128)(4,1)} %bitcast.229), calls=%async_computation.25 | async-start | bytes 786432
  722.4 197.7 %all-to-all-start.1 = ((bf16[1,16,189,1280]{3,2,0,1:T(8,128)(2,1)}), bf16[1,16,189,1280]{3,2,0,1:T(8,128)(2,1)}, u32[]{:S(2)}, u32[]{:S(2)}) async-start(bf16[1,16,189,1280]{3,2,0,1:T(8,128)(2,1)} %convert_bitcast_fusion), calls=%async_computation.1 | async-start | bytes 15728640 | tf_op jit(solution)/shard_map/all_to_all | solution.py:204
  920.2 206.4 %all-to-all-start.3 = ((bf16[1,16,189,1280]{3,2,0,1:T(8,128)(2,1)}), bf16[1,16,189,1280]{3,2,0,1:T(8,128)(2,1)}, u32[]{:S(2)}, u32[]{:S(2)}) async-start(bf16[1,16,189,1280]{3,2,0,1:T(8,128)(2,1)} %fusion.14), calls=%async_computation.3 | async-start | bytes 15728640 | tf_op jit(solution)/shard_map/all_to_all | solution.py:287
  966.4 339.0 %reduce-scatter.20.cloned.1.call-start = ((), (), s32[]{:S(2)}) async-start(), calls=%async_computation.20 | async-start | bytes 3440640 | tf_op jit(solution)/shard_map/reduce_scatter | solution.py:362
  979.0 342.8 %reduce-scatter.18.cloned.1.call-start = ((), (), s32[]{:S(2)}) async-start(), calls=%async_computation.19 | async-start | bytes 6881280 | tf_op jit(solution)/shard_map/reduce_scatter | solution.py:359
  1006.4 442.3 %all-reduce.8.cloned.1.call-start = ((), (), s32[]{:S(2)}) async-start(), calls=%async_computation.21 | async-start | bytes 163840
  1065.6 73.3 %copy-start.40 = (bf16[1280,16]{0,1:T(8,128)(2,1)S(1)}, bf16[1280,16]{0,1:T(8,128)(2,1)}, u32[]{:S(2)}) copy-start(bf16[1280,16]{0,1:T(8,128)(2,1)} %copy-done.39) | copy-start | bytes 122884
  1177.8 427.1 %reduce-scatter.14.cloned.1.call-start = ((), (), s32[]{:S(2)}) async-start(), calls=%async_computation.17 | async-start | bytes 6758400 | tf_op jit(solution)/shard_map/reduce_scatter | solution.py:352
  1184.3 840.8 %reduce-scatter.12.cloned.1.call-start = ((), (), s32[]{:S(2)}) async-start(), calls=%async_computation.16 | async-start | bytes 20275200 | tf_op jit(solution)/shard_map/reduce_scatter | solution.py:351
  1236.4 50.0 %copy-start.32 = (f32[2,40,896]{2,1,0:T(8,128)S(1)}, f32[2,40,896]{2,1,0:T(8,128)}, u32[]{:S(2)}) copy-start(f32[2,40,896]{2,1,0:T(8,128)} %param.40) | copy-start | bytes 860164
  1332.7 50.2 %copy-start.71 = (f32[2,40]{1,0:T(2,128)S(1)}, f32[2,40]{1,0:T(2,128)}, u32[]{:S(2)}) copy-start(f32[2,40]{1,0:T(2,128)} %param.49) | copy-start | bytes 964
  1332.7 50.2 %copy-start.72 = (f32[2,40]{1,0:T(2,128)S(1)}, f32[2,40]{1,0:T(2,128)}, u32[]{:S(2)}) copy-start(f32[2,40]{1,0:T(2,128)} %param.51) | copy-start | bytes 964
  1332.7 50.2 %copy-start.73 = (f32[2,40]{1,0:T(2,128)S(1)}, f32[2,40]{1,0:T(2,128)}, u32[]{:S(2)}) copy-start(f32[2,40]{1,0:T(2,128)} %param.50) | copy-start | bytes 964
  1391.4 57.3 %copy-start.63 = (f32[40,16]{0,1:T(8,128)S(1)}, f32[40,16]{0,1:T(8,128)}, u32[]{:S(2)}) copy-start(f32[40,16]{0,1:T(8,128)} %param.46) | copy-start | bytes 7684
  1391.4 57.3 %copy-start.68 = (f32[40,16]{0,1:T(8,128)S(1)}, f32[40,16]{0,1:T(8,128)}, u32[]{:S(2)}) copy-start(f32[40,16]{0,1:T(8,128)} %param.48) | copy-start | bytes 7684
  1391.4 57.3 %copy-start.69 = (f32[40,16]{0,1:T(8,128)S(1)}, f32[40,16]{0,1:T(8,128)}, u32[]{:S(2)}) copy-start(f32[40,16]{0,1:T(8,128)} %param.47) | copy-start | bytes 7684
  1391.4 213.4 %copy-start.33 = (f32[1280,40]{0,1:T(8,128)S(1)}, f32[1280,40]{0,1:T(8,128)}, u32[]{:S(2)}) copy-start(f32[1280,40]{0,1:T(8,128)} %param.37) | copy-start | bytes 614404
  1391.4 213.4 %copy-start.45 = (f32[1280,40]{0,1:T(8,128)S(1)}, f32[1280,40]{0,1:T(8,128)}, u32[]{:S(2)}) copy-start(f32[1280,40]{0,1:T(8,128)} %param.39) | copy-start | bytes 614404
  (67 other events, 502.9 us)
Sparse Core Ops, SparseCore 0:
  11.5 86.4 all-gather.8
  101.4 57.9 all-gather.10
  162.9 156.3 all-gather.12
  322.6 88.4 all-gather.14
  413.1 12.8 all-gather.16
  428.0 12.0 all-gather.18
  540.1 297.9 reduce-scatter.21
  840.3 446.0 reduce-scatter.15
  1289.3 16.0 reduce-scatter.19
  1308.2 13.6 reduce-scatter.17
  1328.0 120.6 all-reduce.7
  1450.9 153.9 reduce-scatter.13
  1607.2 417.9 reduce-scatter.11
where the time goes:
time: 2040 us; the launch traced here: 2030 us
  waiting for transfers between devices  1010 us (50%)
  blocking collectives  352 us (17%)
  matrix products  232 us (11%)
  local copies, waits for them, and re-layouts  209 us (10%)
  other arithmetic  117 us (6%)
  starting transfers between devices  95.6 us (5%)
    reduce_scatter x1, waiting for transfers between devices, local(): lax.psum_scatter(grad_attention_in, ('dp', 'expert'), scatter_dimension=2...  418 us
    all_gather x1, blocking collectives, local(): lax.all_gather(router.astype(jnp.bfloat16), ('dp', 'expert'), axis=0, til...  241 us
    reduce_scatter x1, waiting for transfers between devices, local(): lax.psum_scatter(grad_attention_out, ('dp', 'expert'), scatter_dimension=...  155 us
    all_to_all x1, waiting for transfers between devices, local(): lax.all_to_all(result_rows, 'expert', split_axis=1, concat_axis=0, tiled=...  128 us
    all_to_all x1, waiting for transfers between devices, local(): lax.all_to_all(to_send.reshape(experts, 1, capacity, model_width), 'exper...  112 us
    all_gather x1, blocking collectives, local(): lax.all_gather(norm_gains.astype(jnp.bfloat16), ('dp', 'expert'), axis=1,...  69.9 us
    all_to_all x1, waiting for transfers between devices, local(): lax.all_to_all(grad_rows, 'expert', split_axis=1, concat_axis=0, tiled=True)  61 us
    unnamed x15, waiting for transfers between devices  55.7 us
  transfers between devices with their start and end apart: 17, of which 10 were waited for; matrix products, arithmetic and copies ran while one was open for 27% of the time, Pallas kernels for 0%

commit v1 on v0

v1 whole, which is shorter than its diff:
```python
import jax
import jax.numpy as jnp
from jax import lax
from jax.sharding import PartitionSpec as P

HD = 128
STEP = 4


eps_norm = 1e-06
theta_base = 10000.0
momentum_decay = 0.9
mask_fill = -1e30
rate_attention_in = 2e-05
rate_attention_out = 0.002
rate_shared_in = 3e-05
rate_shared_down = 0.0002
rate_router = 1.5e-05
rate_gains = 0.0002
rate_expert_in = 0.0004
rate_expert_down = 0.008


def rope_tables(length, head_width):
    half_width = head_width // 2
    frequency = theta_base ** (-(jnp.arange(half_width, dtype=jnp.float32) * 2.0 / head_width))
    angles = jnp.arange(length, dtype=jnp.float32)[:, None] * frequency[None, :]
    return (jnp.cos(angles)[:, None, :], jnp.sin(angles)[:, None, :])


def rotate(values, cosine, sine_table):
    half_width = values.shape[-1] // 2
    front_half = values[..., :half_width]
    back_half = values[..., half_width:]
    return jnp.concatenate(
        [
            front_half * cosine - back_half * sine_table,
            back_half * cosine + front_half * sine_table,
        ],
        axis=-1,
    )


def unrotate(values, cosine, sine_table):
    half_width = values.shape[-1] // 2
    front_half = values[..., :half_width]
    back_half = values[..., half_width:]
    return jnp.concatenate(
        [
            front_half * cosine + back_half * sine_table,
            back_half * cosine - front_half * sine_table,
        ],
        axis=-1,
    )


def allowed_keys(length, keep_flags):
    amount = keep_flags.shape[0]
    position = jnp.arange(amount)
    causal = position[None, :] <= position[:, None]
    usable = (position < length) & (keep_flags == 1)
    return causal & (usable[None, :] | (position[None, :] == position[:, None]))


def silu_parts(values):
    logistic = jax.nn.sigmoid(values)
    return (values * logistic, logistic * (1.0 + values * (1.0 - logistic)))


def advance(weight, moment, average, gradient, step_rate):
    moment_new = momentum_decay * moment + gradient
    weight_new = weight - step_rate * (gradient + momentum_decay * moment_new)
    average_new = average + (weight_new - average) / (STEP + 1)
    return (weight_new, moment_new, average_new)


def dot_nn(a, b):
    return lax.dot_general(a, b, (((1,), (0,)), ((), ())), preferred_element_type=jnp.float32)


def dot_nt(a, b):
    return lax.dot_general(a, b, (((1,), (1,)), ((), ())), preferred_element_type=jnp.float32)


def dot_tn(a, b):
    return lax.dot_general(a, b, (((0,), (0,)), ((), ())), preferred_element_type=jnp.float32)


PLANE = 4


class Grid:
    def __init__(self, experts):
        self.experts = experts
        self.line = experts // PLANE
        here = lax.axis_index("expert")
        self.core = lax.axis_index("dp")
        self.at_line = here // PLANE
        self.at_plane = here % PLANE

    def shift(self, block, amount):
        pairs = [
            (i, ((i // PLANE + amount) % self.line) * PLANE + i % PLANE)
            for i in range(self.experts)
        ]
        return lax.ppermute(block, "expert", pairs)

    def swap(self, block, flip):
        pairs = [(i, (i // PLANE) * PLANE + ((i % PLANE) ^ flip)) for i in range(self.experts)]
        return lax.ppermute(block, "expert", pairs)

    def line_gather(self, block):
        found = [block] + [None] * (self.line - 1)
        for i in range(1, self.line // 2 + 1):
            found[i] = self.shift(found[i - 1], 1)
        last = block
        for i in range(1, (self.line - 1) // 2 + 1):
            last = self.shift(last, -1)
            found[self.line - i] = last
        return found


def halves(array, axis, index):
    mine = lax.dynamic_index_in_dim(array, index, axis, keepdims=False)
    other = lax.dynamic_index_in_dim(array, 1 - index, axis, keepdims=False)
    return mine, other


def add_low(a, b):
    return (a.astype(jnp.float32) + b.astype(jnp.float32)).astype(jnp.bfloat16)


def scatter_sum(grid, grads, splits):
    rows, columns = grads.shape
    block = rows // (2 * grid.experts)
    parts = grads.reshape(2, grid.line, 2, 2, block, columns)
    mine, other = halves(parts, 0, grid.core)
    total = add_low(mine, lax.ppermute(other, "dp", [(0, 1), (1, 0)]))
    bit_y, bit_x = grid.at_plane // 2, grid.at_plane % 2

    def over_y(array, axis):
        mine, other = halves(array, axis, bit_y)
        return add_low(mine, grid.swap(other, 2))

    def over_x(array, axis):
        mine, other = halves(array, axis, bit_x)
        return add_low(mine, grid.swap(other, 1))

    def over_line(array):
        def pick(offset):
            index = lax.rem(grid.at_line + offset + grid.line, grid.line)
            return lax.dynamic_index_in_dim(array, index, 0, keepdims=False)

        half, rest = grid.line // 2, (grid.line - 1) // 2
        low = pick(-half)
        for i in range(half, 0, -1):
            low = add_low(pick(-(i - 1)), grid.shift(low, -1))
        if rest:
            high = pick(rest)
            for i in range(rest, 0, -1):
                got = grid.shift(high, 1)
                if i > 1:
                    high = add_low(pick(i - 1), got)
            low = add_low(low, got)
        return low

    out = []
    start = 0
    for order, width in enumerate(splits):
        piece = lax.slice_in_dim(total, start, start + width, axis=4)
        start += width
        if order == 0:
            piece = over_x(over_y(over_line(piece), 0), 0)
        elif order == 1:
            piece = over_y(over_line(over_x(piece, 2)), 0)
        else:
            piece = over_line(over_x(over_y(piece, 1), 1))
        out.append(piece)
    return jnp.concatenate(out, axis=1)


def local(
    tokens_in,
    lengths,
    key_keep,
    routes,
    cotangent,
    attention_in,
    attention_in_momentum,
    attention_in_average,
    attention_out,
    attention_out_momentum,
    attention_out_average,
    shared_in,
    shared_in_momentum,
    shared_in_average,
    shared_down,
    shared_down_momentum,
    shared_down_average,
    router,
    router_momentum,
    router_average,
    norm_gains,
    norm_gains_momentum,
    norm_gains_average,
    expert_in,
    expert_in_momentum,
    expert_in_average,
    expert_down,
    expert_down_momentum,
    expert_down_average,
):
    low = jnp.bfloat16
    full = jnp.float32
    tokens = tokens_in.shape[0]
    model_width = tokens_in.shape[1]
    head_count = model_width // HD
    top_count = routes.shape[1]
    block_rows = router.shape[0]
    experts = router.shape[1]
    hidden_width = shared_in.shape[2]
    grid = Grid(experts)
    capacity = 9 * tokens * top_count // (8 * experts)
    slots = -(-capacity // 16) * 16
    scaling = HD ** (-0.5)
    extra_width = -(-(experts + 2) // 128) * 128

    pack_one = jnp.concatenate(
        [attention_in[m].astype(low).T for m in range(3)]
        + [
            router.astype(low),
            norm_gains.astype(low).T,
            jnp.zeros((block_rows, extra_width - experts - 2), low),
        ],
        axis=1,
    )
    pack_two = jnp.concatenate(
        [
            attention_out.astype(low).T,
            shared_in[0].astype(low),
            shared_in[1].astype(low),
            shared_down.astype(low).T,
        ],
        axis=1,
    )
    all_one = lax.all_gather(pack_one, ("dp", "expert"), axis=0, tiled=True)
    all_two = lax.all_gather(pack_two, ("dp", "expert"), axis=0, tiled=True)
    turned_in = [all_one[:, m * model_width : (m + 1) * model_width] for m in range(3)]
    extra = all_one[:, 3 * model_width :]
    router_low = extra[:, :experts]
    gains = extra[:, experts : experts + 2].astype(full).T
    gain_one, gain_two = gains[0], gains[1]
    turned_out = all_two[:, :model_width]
    at = model_width
    shared_pair = [all_two[:, at + m * hidden_width : at + (m + 1) * hidden_width] for m in range(2)]
    turned_down = all_two[:, at + 2 * hidden_width :]
    expert_pair = lax.all_gather(expert_in[0].astype(low), "dp", axis=1, tiled=True)
    expert_back = lax.all_gather(expert_down[0].astype(low), "dp", axis=0, tiled=True)

    position = jnp.arange(tokens, dtype=jnp.int32)
    usable = position < lengths[0]
    named = jnp.any(
        routes.T[None, :, :] == jnp.arange(experts, dtype=jnp.int32)[:, None, None], axis=1
    )
    member = named & usable[None, :]
    earlier = (position[:, None] < position[None, :]).astype(low)
    counted = dot_nn(member.astype(low), earlier)
    slot_of = jnp.where(member, counted, -1.0)
    line_slots = grid.line_gather(slot_of)
    wanted = grid.at_line * PLANE + (grid.at_plane ^ jnp.arange(PLANE, dtype=jnp.int32))
    choose = (wanted[:, None] == jnp.arange(experts, dtype=jnp.int32)[None, :]).astype(low)
    slot_ids = jnp.arange(slots, dtype=jnp.int32).astype(full)
    places = []
    for r in range(grid.line):
        chosen_slots = dot_nn(choose, line_slots[r].astype(low))
        places.append(
            (chosen_slots[:, None, :] == slot_ids[None, :, None])
            .astype(low)
            .reshape(PLANE * slots, tokens)
        )

    def dispatch(line_rows):
        rows = dot_nn(places_now, line_rows).astype(low)
        return [rows[:slots]] + [
            grid.swap(rows[q * slots : (q + 1) * slots], q) for q in range(1, PLANE)
        ]

    line_grads = grid.line_gather(cotangent)
    grads_in = []
    for r in range(grid.line):
        places_now = places[r]
        grads_in.append(dispatch(line_grads[r]))

    inputs = tokens_in.astype(full)
    rstd_one = lax.rsqrt(jnp.mean(inputs * inputs, axis=-1, keepdims=True) + eps_norm)
    normed_one = (inputs * rstd_one * gain_one).astype(low)
    projected = [dot_nt(normed_one, turned_in[m]) for m in range(3)]
    cosine, sine_table = rope_tables(tokens, HD)
    split_shape = (tokens, head_count, HD)
    query = rotate(projected[0].reshape(split_shape), cosine, sine_table).astype(low)
    key_rot = rotate(projected[1].reshape(split_shape), cosine, sine_table).astype(low)
    value = projected[2].reshape(split_shape).astype(low)
    allowed = allowed_keys(lengths[0], key_keep)[None]

    def attention_scores():
        raw = jnp.einsum("qhd,khd->hqk", query, key_rot, preferred_element_type=full) * scaling
        return jnp.where(allowed, raw, mask_fill)

    scores = attention_scores()
    row_top = jnp.max(scores, axis=-1, keepdims=True)
    exps = jnp.exp(scores - row_top)
    totals = jnp.sum(exps, axis=-1, keepdims=True)
    log_total = row_top + jnp.log(totals)
    attended = jnp.einsum(
        "hqk,khd->qhd", (exps / totals).astype(low), value, preferred_element_type=full
    )
    attended = attended.reshape(tokens, model_width).astype(low)
    hidden = inputs + dot_nt(attended, turned_out)
    rstd_two = lax.rsqrt(jnp.mean(hidden * hidden, axis=-1, keepdims=True) + eps_norm)
    normed_two = (hidden * rstd_two * gain_two).astype(low)

    logits = lax.dot_general(
        router_low, normed_two, (((0,), (1,)), ((), ())), preferred_element_type=full
    )
    logits = jnp.where(named, logits, mask_fill)
    logit_exps = jnp.exp(logits - jnp.max(logits, axis=0, keepdims=True))
    gating = logit_exps / jnp.sum(logit_exps, axis=0, keepdims=True)
    gating_live = jnp.where(member, gating, 0.0)
    at_slot = slot_of[:, None, :] == slot_ids[None, :, None]
    slot_gates = jnp.sum(jnp.where(at_slot, gating_live[:, None, :], 0.0), axis=2)
    offsets = jnp.arange(grid.line, dtype=jnp.int32)
    source_line = (grid.at_line - offsets + grid.line) % grid.line
    sources = (source_line[:, None] * PLANE + (grid.at_plane ^ jnp.arange(PLANE))[None, :]).reshape(
        experts
    )
    order = (sources[:, None] == jnp.arange(experts, dtype=jnp.int32)[None, :]).astype(full)
    gates_in = lax.all_to_all(slot_gates, "expert", split_axis=0, concat_axis=0, tiled=True)
    gates_in = jnp.dot(order, gates_in, precision=lax.Precision.HIGHEST)

    line_rows = grid.line_gather(normed_two)
    kept = []
    grads_back, results_back, gate_grads = [], [], []
    for r in range(grid.line):
        places_now = places[r]
        rows = jnp.concatenate(dispatch(line_rows[r]), axis=0)
        grad_rows = jnp.concatenate(grads_in[r], axis=0).astype(full)
        gate_col = gates_in[r * PLANE : (r + 1) * PLANE].reshape(PLANE * slots, 1)
        gate_rows = dot_nn(rows, expert_pair[0])
        up_rows = dot_nn(rows, expert_pair[1])
        silu_rows, slope_rows = silu_parts(gate_rows)
        inner = (silu_rows * up_rows).astype(low)
        result_rows = dot_nn(inner, expert_back)
        gate_grads.append(jnp.sum(result_rows * grad_rows, axis=1).reshape(PLANE, slots))
        sent_results = (result_rows * gate_col).astype(low)
        gated = (grad_rows * gate_col).astype(low)
        grad_inner = dot_nt(gated, expert_back)
        grad_gate_rows = (grad_inner * up_rows * slope_rows).astype(low)
        grad_up_rows = (grad_inner * silu_rows).astype(low)
        sent_grads = (
            dot_nt(grad_gate_rows, expert_pair[0]) + dot_nt(grad_up_rows, expert_pair[1])
        ).astype(low)
        kept.append((rows, inner, gated, grad_gate_rows, grad_up_rows))
        grads_back.append(sent_grads)
        results_back.append(sent_results)

    def collect(blocks):
        total = None
        for r in range(grid.line):
            back = jnp.concatenate(
                [blocks[r][:slots]]
                + [
                    grid.swap(blocks[r][q * slots : (q + 1) * slots], q) for q in range(1, PLANE)
                ],
                axis=0,
            )
            part = dot_tn(places[r], back)
            if r:
                part = grid.shift(part.astype(low), -r).astype(full)
            total = part if total is None else total + part
        return total

    routed_grad = collect(grads_back)
    gate_grads = jnp.dot(
        order.T, jnp.concatenate(gate_grads, axis=0), precision=lax.Precision.HIGHEST
    )
    gate_grads = lax.all_to_all(gate_grads, "expert", split_axis=0, concat_axis=0, tiled=True)
    grad_gating = jnp.sum(jnp.where(at_slot, gate_grads[:, :, None], 0.0), axis=1)
    grad_chosen = gating * (grad_gating - jnp.sum(gating * grad_gating, axis=0, keepdims=True))
    grad_logits = grad_chosen.astype(low)
    grad_router = lax.dot_general(
        normed_two, grad_logits, (((0,), (1,)), ((), ())), preferred_element_type=full
    )

    grad_out = cotangent.astype(full)
    shared_gate = dot_nn(normed_two, shared_pair[0])
    shared_up = dot_nn(normed_two, shared_pair[1])
    shared_silu, shared_slope = silu_parts(shared_gate)
    shared_hidden = (shared_silu * shared_up).astype(low)
    shared_result = dot_nt(shared_hidden, turned_down)
    grad_shared_hidden = dot_nn(cotangent, turned_down)
    grad_shared_gate = (grad_shared_hidden * shared_up * shared_slope).astype(low)
    grad_shared_up = (grad_shared_hidden * shared_silu).astype(low)
    grad_normed_two = dot_nt(grad_shared_gate, shared_pair[0]) + dot_nt(
        grad_shared_up, shared_pair[1]
    )
    grad_normed_two = grad_normed_two + lax.dot_general(
        grad_logits, router_low, (((0,), (1,)), ((), ())), preferred_element_type=full
    )

    grad_normed_two = grad_normed_two + routed_grad
    scaled_two = grad_normed_two * gain_two
    grad_gain_two = jnp.sum(grad_normed_two * hidden * rstd_two, axis=0)
    grad_hidden = (
        grad_out
        + rstd_two * scaled_two
        - hidden * rstd_two**3 * jnp.mean(scaled_two * hidden, axis=-1, keepdims=True)
    )
    grad_branch = grad_hidden.astype(low)
    grads_two = jnp.concatenate(
        [
            dot_tn(grad_branch, attended).astype(low),
            dot_tn(normed_two, grad_shared_gate).astype(low),
            dot_tn(normed_two, grad_shared_up).astype(low),
            dot_tn(cotangent, shared_hidden).astype(low),
        ],
        axis=1,
    )
    units = grads_two.shape[1] // 128
    first = 3 * units // 8
    summed_two = scatter_sum(
        grid, grads_two, ((units - 2 * first) * 128, first * 128, first * 128)
    ).astype(full)

    grad_attended = dot_nn(grad_branch, turned_out).astype(low).reshape(split_shape)
    probs = jnp.exp(attention_scores() - log_total)
    grad_probs = jnp.einsum("qhd,khd->hqk", grad_attended, value, preferred_element_type=full)
    grad_scores = (
        probs * (grad_probs - jnp.sum(probs * grad_probs, axis=-1, keepdims=True))
    ).astype(low)
    grad_query = (
        jnp.einsum("hqk,khd->qhd", grad_scores, key_rot, preferred_element_type=full) * scaling
    )
    grad_key = (
        jnp.einsum("hqk,qhd->khd", grad_scores, query, preferred_element_type=full) * scaling
    )
    grad_value = jnp.einsum(
        "hqk,qhd->khd", probs.astype(low), grad_attended, preferred_element_type=full
    )
    grad_projected = [
        part.reshape(tokens, model_width).astype(low)
        for part in (
            unrotate(grad_query, cosine, sine_table),
            unrotate(grad_key, cosine, sine_table),
            grad_value,
        )
    ]
    grad_normed_one = (
        dot_nn(grad_projected[0], turned_in[0])
        + dot_nn(grad_projected[1], turned_in[1])
        + dot_nn(grad_projected[2], turned_in[2])
    )
    scaled_one = grad_normed_one * gain_one
    grad_gain_one = jnp.sum(grad_normed_one * inputs * rstd_one, axis=0)
    input_grad = (
        grad_hidden
        + rstd_one * scaled_one
        - inputs * rstd_one**3 * jnp.mean(scaled_one * inputs, axis=-1, keepdims=True)
    )
    grads_one = jnp.concatenate(
        [dot_tn(part, normed_one).astype(low) for part in grad_projected]
        + [
            grad_router.astype(low),
            jnp.stack([grad_gain_one, grad_gain_two], axis=1).astype(low),
            jnp.zeros((model_width, extra_width - experts - 2), low),
        ],
        axis=1,
    )
    units = grads_one.shape[1] // 128
    first = 3 * units // 8
    summed_one = scatter_sum(
        grid, grads_one, ((units - 2 * first) * 128, first * 128, first * 128)
    ).astype(full)

    output = (hidden + shared_result + collect(results_back)).astype(low)

    rows, inner, gated, grad_gate_rows, grad_up_rows = [
        jnp.concatenate(parts, axis=0) for parts in zip(*kept)
    ]
    grad_expert_down = dot_tn(inner, gated).astype(low)
    grad_expert_in = jnp.stack(
        [dot_tn(rows, grad_gate_rows).astype(low), dot_tn(rows, grad_up_rows).astype(low)], axis=0
    )
    summed_expert_in = lax.psum_scatter(
        grad_expert_in, "dp", scatter_dimension=1, tiled=True
    ).astype(full)[None]
    summed_expert_down = lax.psum_scatter(
        grad_expert_down, "dp", scatter_dimension=0, tiled=True
    ).astype(full)[None]

    summed_in = jnp.stack(
        [summed_one[:, m * model_width : (m + 1) * model_width].T for m in range(3)], axis=0
    )
    summed_extra = summed_one[:, 3 * model_width :]
    summed_router = summed_extra[:, :experts]
    summed_gains = summed_extra[:, experts : experts + 2].T
    summed_out = summed_two[:, :model_width].T
    summed_shared_in = jnp.stack(
        [summed_two[:, at + m * hidden_width : at + (m + 1) * hidden_width] for m in range(2)],
        axis=0,
    )
    summed_shared_down = summed_two[:, at + 2 * hidden_width :].T
    upd_attn_in = advance(
        attention_in, attention_in_momentum, attention_in_average, summed_in, rate_attention_in
    )
    upd_attn_out = advance(
        attention_out, attention_out_momentum, attention_out_average, summed_out, rate_attention_out
    )
    upd_shared_in = advance(
        shared_in, shared_in_momentum, shared_in_average, summed_shared_in, rate_shared_in
    )
    upd_shared_down = advance(
        shared_down, shared_down_momentum, shared_down_average, summed_shared_down, rate_shared_down
    )
    upd_router = advance(router, router_momentum, router_average, summed_router, rate_router)
    upd_gains = advance(
        norm_gains, norm_gains_momentum, norm_gains_average, summed_gains, rate_gains
    )
    upd_expert_in = advance(
        expert_in, expert_in_momentum, expert_in_average, summed_expert_in, rate_expert_in
    )
    upd_expert_down = advance(
        expert_down, expert_down_momentum, expert_down_average, summed_expert_down, rate_expert_down
    )
    return (
        output,
        input_grad,
        upd_attn_in[0],
        upd_attn_in[1],
        upd_attn_in[2],
        upd_attn_out[0],
        upd_attn_out[1],
        upd_attn_out[2],
        upd_shared_in[0],
        upd_shared_in[1],
        upd_shared_in[2],
        upd_shared_down[0],
        upd_shared_down[1],
        upd_shared_down[2],
        upd_router[0],
        upd_router[1],
        upd_router[2],
        upd_gains[0],
        upd_gains[1],
        upd_gains[2],
        upd_expert_in[0],
        upd_expert_in[1],
        upd_expert_in[2],
        upd_expert_down[0],
        upd_expert_down[1],
        upd_expert_down[2],
    )


def solution(mesh):
    in_specs = (
        P(("dp", "expert"), None),
        P(("dp", "expert")),
        P(("dp", "expert")),
        P(("dp", "expert"), None),
        P(("dp", "expert"), None),
        P(None, None, ("dp", "expert")),
        P(None, None, ("dp", "expert")),
        P(None, None, ("dp", "expert")),
        P(None, ("dp", "expert")),
        P(None, ("dp", "expert")),
        P(None, ("dp", "expert")),
        P(None, ("dp", "expert"), None),
        P(None, ("dp", "expert"), None),
        P(None, ("dp", "expert"), None),
        P(None, ("dp", "expert")),
        P(None, ("dp", "expert")),
        P(None, ("dp", "expert")),
        P(("dp", "expert"), None),
        P(("dp", "expert"), None),
        P(("dp", "expert"), None),
        P(None, ("dp", "expert")),
        P(None, ("dp", "expert")),
        P(None, ("dp", "expert")),
        P("expert", None, "dp", None),
        P("expert", None, "dp", None),
        P("expert", None, "dp", None),
        P("expert", "dp", None),
        P("expert", "dp", None),
        P("expert", "dp", None),
    )
    out_specs = (
        P(("dp", "expert"), None),
        P(("dp", "expert"), None),
        P(None, None, ("dp", "expert")),
        P(None, None, ("dp", "expert")),
        P(None, None, ("dp", "expert")),
        P(None, ("dp", "expert")),
        P(None, ("dp", "expert")),
        P(None, ("dp", "expert")),
        P(None, ("dp", "expert"), None),
        P(None, ("dp", "expert"), None),
        P(None, ("dp", "expert"), None),
        P(None, ("dp", "expert")),
        P(None, ("dp", "expert")),
        P(None, ("dp", "expert")),
        P(("dp", "expert"), None),
        P(("dp", "expert"), None),
        P(("dp", "expert"), None),
        P(None, ("dp", "expert")),
        P(None, ("dp", "expert")),
        P(None, ("dp", "expert")),
        P("expert", None, "dp", None),
        P("expert", None, "dp", None),
        P("expert", None, "dp", None),
        P("expert", "dp", None),
        P("expert", "dp", None),
        P("expert", "dp", None),
    )
    return jax.shard_map(local, mesh=mesh, in_specs=in_specs, out_specs=out_specs, check_vma=False)
```

time: 2040 us -> 1160 us (0.57)
  waiting for transfers between devices: 1010 us -> 475 us
  blocking collectives: 352 us -> 0 us
  local copies, waits for them, and re-layouts: 209 us -> 161 us
  starting transfers between devices: 95.6 us -> 131 us
  matrix products: 232 us -> 266 us
    reduce_scatter x5 -> x2, waiting for transfers between devices: 647 us -> 0.01 us  [the longest x1 0.01 us: local(): lax.psum_scatter(grad_expert_down, 'dp', scatter_dimension=0, tiled=True)]
    ppermute x0 -> x95, waiting for transfers between devices: none -> 421 us  [the longest x33 247 us: shift(): return lax.ppermute(block, 'expert', pairs)]
    all_gather x2 -> x0, blocking collectives: 311 us -> none  [the longest x1 241 us: local(): lax.all_gather(router.astype(jnp.bfloat16), ('dp', 'expert'), axis=0, til...]
    all_to_all x4 -> x2, waiting for transfers between devices: 301 us -> 5.31 us  [the longest x1 3.57 us: local(): lax.all_to_all(slot_gates, 'expert', split_axis=0, concat_axis=0, tiled=T...]
    ppermute x0 -> x95, starting transfers between devices: none -> 121 us  [the longest x60 78.9 us: swap(): return lax.ppermute(block, 'expert', pairs)]
    gather x10 -> x0, local copies, waits for them, and re-layouts: 103 us -> none  [the longest x2 29.9 us: local(): grad_padded[owner_rows] * gating_padded[slot_table][:, None]]
    all_to_all x4 -> x2, starting transfers between devices: 94.5 us -> 8.64 us  [the longest x1 5.14 us: local(): lax.all_to_all(slot_gates, 'expert', split_axis=0, concat_axis=0, tiled=T...]
    concatenate x3 -> x6, local copies, waits for them, and re-layouts: 8.18 us -> 73 us  [the longest x2 55.7 us: local(): jnp.concatenate([dot_tn(part, normed_one).astype(low) for part in grad_pr...]
  transfers between devices with their start and end apart: 17 -> 103, of which waited for: 10 -> 40; matrix products, arithmetic and copies ran while one was open for 27% -> 40% of each run, Pallas kernels for 0% -> 0%
where the time goes in v1:
time: 1160 us; the launch traced here: 1150 us
  waiting for transfers between devices  475 us (41%)
  matrix products  266 us (23%)
  local copies, waits for them, and re-layouts  161 us (14%)
  starting transfers between devices  131 us (11%)
  other arithmetic  99 us (9%)
  between operations  17.7 us (2%)
    ppermute x33, waiting for transfers between devices, shift(): return lax.ppermute(block, 'expert', pairs)  247 us
    ppermute x60, waiting for transfers between devices, swap(): return lax.ppermute(block, 'expert', pairs)  174 us
    dot_general x32, matrix products, dot_nn(): lax.dot_general(a, b, (((1,), (0,)), ((), ())), preferred_element_type=jn...  104 us
    ppermute x60, starting transfers between devices, swap(): return lax.ppermute(block, 'expert', pairs)  78.9 us
    dot_general x18, matrix products, dot_tn(): lax.dot_general(a, b, (((0,), (0,)), ((), ())), preferred_element_type=jn...  77.6 us
    dot_general x19, matrix products, dot_nt(): lax.dot_general(a, b, (((1,), (1,)), ((), ())), preferred_element_type=jn...  66.9 us
    concatenate x2, local copies, waits for them, and re-layouts, local(): jnp.concatenate([dot_tn(part, normed_one).astype(low) for part in grad_pr...  55.7 us
    all_gather x1, waiting for transfers between devices, local(): all_two = lax.all_gather(pack_two, ('dp', 'expert'), axis=0, tiled=True)  47.3 us
  transfers between devices with their start and end apart: 103, of which 40 were waited for; matrix products, arithmetic and copies ran while one was open for 40% of the time, Pallas kernels for 0%

profile of v1, /device:TPU:0, one launch (start us, length us, event | category | flops | bytes accessed | tf_op | source)
XLA Modules:
  0.0 1148.7 jit_solution(3679602337041853288)
XLA Ops:
  31.6 48.3 %collective-permute-done.6 = bf16[16,384]{1,0:T(8,128)(2,1)S(1)} collective-permute-done((bf16[16,384]{1,0:T(8,128)(2,1)}, bf16[16,384]{1,0:T(8,128)(2,1)S(1)}, u32[]{:S(2)}, u32[]{:S(2)}) %collective-permute-start.6) | collective-permute-done | bytes 12320 | tf_op jit(solution)/shard_map/ppermute | solution.py:106
  102.0 38.4 %collective-permute-done.40 = bf16[384,1280]{1,0:T(8,128)(2,1)S(1)} collective-permute-done((bf16[384,1280]{1,0:T(8,128)(2,1)}, bf16[384,1280]{1,0:T(8,128)(2,1)S(1)}, u32[]{:S(2)}, u32[]{:S(2)}) %collective-permute-start.40) | collective-permute-done | bytes 983072 | tf_op jit(solution)/shard_map/ppermute | solution.py:106
  184.3 47.3 %all-gather.9.cloned.1.call-done = bf16[1280,3968]{1,0:T(8,128)(2,1)} async-done(((bf16[40,3968]{1,0:T(8,128)(2,1)}), bf16[1280,3968]{1,0:T(8,128)(2,1)}) %all-gather.9.cloned.1.call-update) | async-done | bytes 10158096 | tf_op jit(solution)/shard_map/all_gather | solution.py:247
  281.8 11.6 %collective-permute-done.7 = bf16[384,1280]{1,0:T(8,128)(2,1)} collective-permute-done((bf16[384,1280]{1,0:T(8,128)(2,1)S(1)}, bf16[384,1280]{1,0:T(8,128)(2,1)}, u32[]{:S(2)}, u32[]{:S(2)}) %collective-permute-start.7) | collective-permute-done | bytes 983072 | tf_op jit(solution)/shard_map/ppermute | solution.py:106
  307.4 7.6 collective-permute-done.25
  323.6 17.7 %collective-permute-done.9 = bf16[192,1280]{1,0:T(8,128)(2,1)S(1)} collective-permute-done((bf16[192,1280]{1,0:T(8,128)(2,1)}, bf16[192,1280]{1,0:T(8,128)(2,1)S(1)}, u32[]{:S(2)}, u32[]{:S(2)}) %collective-permute-start.9) | collective-permute-done | bytes 491552 | tf_op jit(solution)/shard_map/ppermute | solution.py:110
  355.4 13.7 %collective-permute-done.16 = bf16[384,1280]{1,0:T(8,128)(2,1)S(1)} collective-permute-done((bf16[384,1280]{1,0:T(8,128)(2,1)}, bf16[384,1280]{1,0:T(8,128)(2,1)S(1)}, u32[]{:S(2)}, u32[]{:S(2)}) %collective-permute-start.16) | collective-permute-done | bytes 983072 | tf_op jit(solution)/shard_map/ppermute | solution.py:106
  388.2 14.2 %collective-permute-done.18 = bf16[192,1280]{1,0:T(8,128)(2,1)} collective-permute-done((bf16[192,1280]{1,0:T(8,128)(2,1)}, bf16[192,1280]{1,0:T(8,128)(2,1)}, u32[]{:S(2)}, u32[]{:S(2)}) %collective-permute-start.18) | collective-permute-done | bytes 491552 | tf_op jit(solution)/shard_map/ppermute | solution.py:110
  409.1 6.8 multiply_convert_fusion.14
  431.3 6.7 collective-permute-done.26
  439.4 17.2 %collective-permute-done.27 = bf16[192,1280]{1,0:T(8,128)(2,1)} collective-permute-done((bf16[192,1280]{1,0:T(8,128)(2,1)}, bf16[192,1280]{1,0:T(8,128)(2,1)}, u32[]{:S(2)}, u32[]{:S(2)}) %collective-permute-start.27) | collective-permute-done | bytes 491552 | tf_op jit(solution)/shard_map/ppermute | solution.py:110
  461.1 7.1 multiply_convert_fusion.13
  523.9 13.7 %fusion.53 = bf16[896,1280]{1,0:T(8,128)(2,1)} fusion(bf16[768,1280]{1,0:T(8,128)(2,1)} %get-tuple-element.320, bf16[768,1280]{1,0:T(8,128)(2,1)} %get-tuple-element.318, bf16[768,1280]{1,0:T(8,128)(2,1)} %get-tuple-element.316, bf16[768,1280]{1,0:T(8,128)(2,1)} %get-tuple-element.322, bf16[768,896]{1,0:T(8,128)(2,1)} %copy-done.154, ...), kind=kOutput, calls=%fused_computation.92 | convolution fusion | flops 7101054976 | bytes 15663104 | tf_op jit(solution)/shard_map/dot_general | solution.py:86
  537.8 7.1 multiply_convert_fusion.11
  576.3 6.9 multiply_convert_fusion.5
  583.2 12.0 %fusion.61 = bf16[1,1280,896]{2,1,0:T(8,128)(2,1)} fusion(bf16[3072,1280]{1,0:T(8,128)(2,1)S(1)} %bitcast.424, bf16[768,896]{1,0:T(8,128)(2,1)} %get-tuple-element.193, bf16[768,896]{1,0:T(8,128)(2,1)} %copy-done.142, bf16[768,896]{1,0:T(8,128)(2,1)} %copy-done.141, bf16[768,896]{1,0:T(8,128)(2,1)} %copy-done.140), kind=kOutput, calls=%fused_computation.112 | convolution fusion | flops 7069597696 | bytes 15663104 | tf_op jit(solution)/shard_map/dot_general | solution.py:86
  610.6 18.9 %collective-permute-done.56 = bf16[192,1280]{1,0:T(8,128)(2,1)S(1)} collective-permute-done((bf16[192,1280]{1,0:T(8,128)(2,1)S(1)}, bf16[192,1280]{1,0:T(8,128)(2,1)S(1)}, u32[]{:S(2)}, u32[]{:S(2)}) %collective-permute-start.56) | collective-permute-done | bytes 491552 | tf_op jit(solution)/shard_map/ppermute | solution.py:110
  633.2 17.4 %collective-permute-done.60 = bf16[192,1280]{1,0:T(8,128)(2,1)S(1)} collective-permute-done((bf16[192,1280]{1,0:T(8,128)(2,1)S(1)}, bf16[192,1280]{1,0:T(8,128)(2,1)S(1)}, u32[]{:S(2)}, u32[]{:S(2)}) %collective-permute-start.60) | collective-permute-done | bytes 491552 | tf_op jit(solution)/shard_map/ppermute | solution.py:110
  654.1 22.8 %collective-permute-done.12 = bf16[192,1280]{1,0:T(8,128)(2,1)S(1)} collective-permute-done((bf16[192,1280]{1,0:T(8,128)(2,1)S(1)}, bf16[192,1280]{1,0:T(8,128)(2,1)S(1)}, u32[]{:S(2)}, u32[]{:S(2)}) %collective-permute-start.12) | collective-permute-done | bytes 491552 | tf_op jit(solution)/shard_map/ppermute | solution.py:110
  689.5 16.4 %collective-permute-done.30 = bf16[192,1280]{1,0:T(8,128)(2,1)S(1)} collective-permute-done((bf16[192,1280]{1,0:T(8,128)(2,1)S(1)}, bf16[192,1280]{1,0:T(8,128)(2,1)S(1)}, u32[]{:S(2)}, u32[]{:S(2)}) %collective-permute-start.30) | collective-permute-done | bytes 491552 | tf_op jit(solution)/shard_map/ppermute | solution.py:110
  714.2 14.8 %collective-permute-done.49 = bf16[192,1280]{1,0:T(8,128)(2,1)S(1)} collective-permute-done((bf16[192,1280]{1,0:T(8,128)(2,1)S(1)}, bf16[192,1280]{1,0:T(8,128)(2,1)S(1)}, u32[]{:S(2)}, u32[]{:S(2)}) %collective-permute-start.49) | collective-permute-done | bytes 491552 | tf_op jit(solution)/shard_map/ppermute | solution.py:110
  732.5 28.8 %collective-permute-done.58 = bf16[384,1280]{1,0:T(8,128)(2,1)S(1)} collective-permute-done((bf16[384,1280]{1,0:T(8,128)(2,1)S(1)}, bf16[384,1280]{1,0:T(8,128)(2,1)S(1)}, u32[]{:S(2)}, u32[]{:S(2)}) %collective-permute-start.58) | collective-permute-done | bytes 983072 | tf_op jit(solution)/shard_map/ppermute | solution.py:106
  788.9 14.1 %copy.287 = bf16[1280,3968]{1,0:T(8,128)(2,1)} copy(bf16[1280,3968]{0,1:T(8,128)(2,1)} %pad_maximum_fusion) | data formatting | bytes 20316160 | tf_op jit(solution)/shard_map/concatenate | solution.py:419
  843.9 41.6 %concatenate.125 = bf16[1280,3968]{0,1:T(8,128)(2,1)} concatenate(bf16[1280,1280]{0,1:T(8,128)(2,1)} %convolution_convert_fusion.3, bf16[1280,1280]{0,1:T(8,128)(2,1)} %convolution_convert_fusion.2, bf16[1280,1280]{0,1:T(8,128)(2,1)S(1)} %convolution_convert_fusion.1, bf16[1280,16]{0,1:T(8,128)(2,1)S(1)} %copy-done.104, bf16[1280,1]{0,1:T(2,128)(2,1)S(1)} %stack.40, ...), dimensions={1} | concatenate | bytes 20316160 | tf_op jit(solution)/shard_map/concatenate | solution.py:469
  885.6 14.1 %copy.282 = bf16[1280,3968]{1,0:T(8,128)(2,1)} copy(bf16[1280,3968]{0,1:T(8,128)(2,1)} %concatenate.125) | data formatting | bytes 20316160 | tf_op jit(solution)/shard_map/concatenate | solution.py:469
  907.9 11.7 %fusion.64 = bf16[1,1280,896]{2,1,0:T(8,128)(2,1)S(1)} fusion(bf16[3072,1280]{1,0:T(8,128)(2,1)} %constant_dynamic-update-slice_fusion, bf16[768,896]{1,0:T(8,128)(2,1)S(1)} %copy-done.139, bf16[768,896]{1,0:T(8,128)(2,1)S(1)} %copy-done.137, bf16[768,896]{1,0:T(8,128)(2,1)S(1)} %copy-done.135, bf16[768,896]{1,0:T(8,128)(2,1)S(1)} %copy-done.133), kind=kOutput, calls=%fused_computation.113 | convolution fusion | flops 7069597696 | bytes 15663104 | tf_op jit(solution)/shard_map/dot_general | solution.py:86
  922.2 50.3 %collective-permute-done.23 = bf16[384,1280]{1,0:T(8,128)(2,1)} collective-permute-done((bf16[384,1280]{1,0:T(8,128)(2,1)}, bf16[384,1280]{1,0:T(8,128)(2,1)}, u32[]{:S(2)}, u32[]{:S(2)}) %collective-permute-start.23) | collective-permute-done | bytes 983072 | tf_op jit(solution)/shard_map/ppermute | solution.py:106
  1008.6 10.1 collective-permute-done.80
  1018.8 7.3 collective-permute-done.64
  1030.8 11.1 collective-permute-done.81
  1058.4 9.4 collective-permute-done.74
  1131.0 10.6 multiply_add_fusion
  (789 shorter events, 555.4 us)
Async XLA Ops:
  7.2 136.9 %all-gather.7.cloned.1.call-start = ((), (), s32[]{:S(2)}) async-start(), calls=%async_computation.4 | async-start | bytes 10475520 | tf_op jit(solution)/shard_map/all_gather | solution.py:246
  10.9 220.6 %all-gather.9.cloned.1.call-start = ((), (), s32[]{:S(2)}) async-start(), calls=%async_computation.5 | async-start | bytes 10475520 | tf_op jit(solution)/shard_map/all_gather | solution.py:247
  11.9 258.4 %all-gather.11.cloned.1.call-start = ((), (), s32[]{:S(2)}) async-start(), calls=%async_computation.8 | async-start | bytes 6881280 | tf_op jit(solution)/shard_map/all_gather | solution.py:257
  15.9 283.4 %all-gather.13.cloned.1.call-start = ((), (), s32[]{:S(2)}) async-start(), calls=%async_computation.9 | async-start | bytes 3440640 | tf_op jit(solution)/shard_map/all_gather | solution.py:258
  15.9 77.8 %collective-permute-start.36 = (bf16[384,1280]{1,0:T(8,128)(2,1)}, bf16[384,1280]{1,0:T(8,128)(2,1)}, u32[]{:S(2)}, u32[]{:S(2)}) collective-permute-start(bf16[384,1280]{1,0:T(8,128)(2,1)} %param.33), channel_id=1, source_target_pairs={{0,4},{1,5},{2,6},{3,7},{4,8},{5,9},{6,10},{7,11},{8,12},{9,13},{1... | collective-permute-start | bytes 2949128 | tf_op jit(solution)/shard_map/ppermute | solution.py:106
  19.0 78.0 %collective-permute-start.44 = (bf16[384,1280]{1,0:T(8,128)(2,1)}, bf16[384,1280]{1,0:T(8,128)(2,1)}, u32[]{:S(2)}, u32[]{:S(2)}) collective-permute-start(bf16[384,1280]{1,0:T(8,128)(2,1)} %param.33), channel_id=1, source_target_pairs={{0,12},{1,13},{2,14},{3,15},{4,0},{5,1},{6,2},{7,3},{8,4},{9,5},{1... | collective-permute-start | bytes 2949128 | tf_op jit(solution)/shard_map/ppermute | solution.py:106
  22.6 57.3 %collective-permute-start.6 = (bf16[16,384]{1,0:T(8,128)(2,1)}, bf16[16,384]{1,0:T(8,128)(2,1)S(1)}, u32[]{:S(2)}, u32[]{:S(2)}) collective-permute-start(bf16[16,384]{1,0:T(8,128)(2,1)} %get-tuple-element.310), channel_id=1, source_target_pairs={{0,4},{1,5},{2,6},{3,7},{4,8},{5,9},{6,10},{7,11},{8,12},{9,13},{1... | collective-permute-start | bytes 36872 | tf_op jit(solution)/shard_map/ppermute | solution.py:106
  22.6 61.6 %collective-permute-start.24 = (bf16[16,384]{1,0:T(8,128)(2,1)}, bf16[16,384]{1,0:T(8,128)(2,1)}, u32[]{:S(2)}, u32[]{:S(2)}) collective-permute-start(bf16[16,384]{1,0:T(8,128)(2,1)} %get-tuple-element.311), channel_id=1, source_target_pairs={{0,12},{1,13},{2,14},{3,15},{4,0},{5,1},{6,2},{7,3},{8,4},{9,5},{1... | collective-permute-start | bytes 36872 | tf_op jit(solution)/shard_map/ppermute | solution.py:106
  90.5 206.8 %collective-permute-start.33 = (bf16[192,1280]{1,0:T(8,128)(2,1)}, bf16[192,1280]{1,0:T(8,128)(2,1)}, u32[]{:S(2)}, u32[]{:S(2)}) collective-permute-start(bf16[192,1280]{1,0:T(8,128)(2,1)} %get-tuple-element.269), channel_id=1, source_target_pairs={{0,1},{1,0},{2,3},{3,2},{4,5},{5,4},{6,7},{7,6},{8,9},{9,8},{10,11... | collective-permute-start | bytes 1474568 | tf_op jit(solution)/shard_map/ppermute | solution.py:110
  92.2 206.2 %collective-permute-start.34 = (bf16[192,1280]{1,0:T(8,128)(2,1)}, bf16[192,1280]{1,0:T(8,128)(2,1)}, u32[]{:S(2)}, u32[]{:S(2)}) collective-permute-start(bf16[192,1280]{1,0:T(8,128)(2,1)} %get-tuple-element.268), channel_id=1, source_target_pairs={{0,2},{1,3},{2,0},{3,1},{4,6},{5,7},{6,4},{7,5},{8,10},{9,11},{10,... | collective-permute-start | bytes 1474568 | tf_op jit(solution)/shard_map/ppermute | solution.py:110
  266.7 105.7 %collective-permute-start.37 = (bf16[192,1280]{1,0:T(8,128)(2,1)}, bf16[192,1280]{1,0:T(8,128)(2,1)}, u32[]{:S(2)}, u32[]{:S(2)}) collective-permute-start(bf16[192,1280]{1,0:T(8,128)(2,1)} %get-tuple-element.273), channel_id=1, source_target_pairs={{0,1},{1,0},{2,3},{3,2},{4,5},{5,4},{6,7},{7,6},{8,9},{9,8},{10,11... | collective-permute-start | bytes 1474568 | tf_op jit(solution)/shard_map/ppermute | solution.py:110
  297.3 76.4 %collective-permute-start.38 = (bf16[192,1280]{1,0:T(8,128)(2,1)}, bf16[192,1280]{1,0:T(8,128)(2,1)}, u32[]{:S(2)}, u32[]{:S(2)}) collective-permute-start(bf16[192,1280]{1,0:T(8,128)(2,1)} %get-tuple-element.272), channel_id=1, source_target_pairs={{0,2},{1,3},{2,0},{3,1},{4,6},{5,7},{6,4},{7,5},{8,10},{9,11},{10,... | collective-permute-start | bytes 1474568 | tf_op jit(solution)/shard_map/ppermute | solution.py:110
  320.1 54.4 %collective-permute-start.39 = (bf16[192,1280]{1,0:T(8,128)(2,1)S(1)}, bf16[192,1280]{1,0:T(8,128)(2,1)S(1)}, u32[]{:S(2)}, u32[]{:S(2)}) collective-permute-start(bf16[192,1280]{1,0:T(8,128)(2,1)S(1)} %copy-done.67), channel_id=1, source_target_pairs={{0,3},{1,2},{2,1},{3,0},{4,7},{5,6},{6,5},{7,4},{8,11},{9,10},{10,... | collective-permute-start | bytes 1474568 | tf_op jit(solution)/shard_map/ppermute | solution.py:110
  341.3 126.9 %collective-permute-start.45 = (bf16[192,1280]{1,0:T(8,128)(2,1)}, bf16[192,1280]{1,0:T(8,128)(2,1)}, u32[]{:S(2)}, u32[]{:S(2)}) collective-permute-start(bf16[192,1280]{1,0:T(8,128)(2,1)} %get-tuple-element.281), channel_id=1, source_target_pairs={{0,1},{1,0},{2,3},{3,2},{4,5},{5,4},{6,7},{7,6},{8,9},{9,8},{10,11... | collective-permute-start | bytes 1474568 | tf_op jit(solution)/shard_map/ppermute | solution.py:110
  369.1 99.2 %collective-permute-start.46 = (bf16[192,1280]{1,0:T(8,128)(2,1)}, bf16[192,1280]{1,0:T(8,128)(2,1)}, u32[]{:S(2)}, u32[]{:S(2)}) collective-permute-start(bf16[192,1280]{1,0:T(8,128)(2,1)} %get-tuple-element.280), channel_id=1, source_target_pairs={{0,2},{1,3},{2,0},{3,1},{4,6},{5,7},{6,4},{7,5},{8,10},{9,11},{10,... | collective-permute-start | bytes 1474568 | tf_op jit(solution)/shard_map/ppermute | solution.py:110
  494.0 484.9 %reduce-scatter.5.cloned.1.call-start = ((), (), s32[]{:S(2)}) async-start(), calls=%async_computation.7 | async-start | bytes 3440640 | tf_op jit(solution)/shard_map/reduce_scatter | solution.py:496
  537.6 593.4 %reduce-scatter.3.cloned.1.call-start = ((), (), s32[]{:S(2)}) async-start(), calls=%async_computation.6 | async-start | bytes 6881280 | tf_op jit(solution)/shard_map/reduce_scatter | solution.py:493
  554.0 50.7 %collective-permute-start.48 = (bf16[192,1280]{1,0:T(8,128)(2,1)S(1)}, bf16[192,1280]{1,0:T(8,128)(2,1)S(1)}, u32[]{:S(2)}, u32[]{:S(2)}) collective-permute-start(bf16[192,1280]{1,0:T(8,128)(2,1)S(1)} %get-tuple-element.249), channel_id=1, source_target_pairs={{0,1},{1,0},{2,3},{3,2},{4,5},{5,4},{6,7},{7,6},{8,9},{9,8},{10,11... | collective-permute-start | bytes 1474568 | tf_op jit(solution)/shard_map/ppermute | solution.py:110
  630.1 46.8 %collective-permute-start.12 = (bf16[192,1280]{1,0:T(8,128)(2,1)S(1)}, bf16[192,1280]{1,0:T(8,128)(2,1)S(1)}, u32[]{:S(2)}, u32[]{:S(2)}) collective-permute-start(bf16[192,1280]{1,0:T(8,128)(2,1)S(1)} %get-tuple-element.252), channel_id=1, source_target_pairs={{0,2},{1,3},{2,0},{3,1},{4,6},{5,7},{6,4},{7,5},{8,10},{9,11},{10,... | collective-permute-start | bytes 1474568 | tf_op jit(solution)/shard_map/ppermute | solution.py:110
  631.0 51.7 %collective-permute-start.13 = (bf16[192,1280]{1,0:T(8,128)(2,1)S(1)}, bf16[192,1280]{1,0:T(8,128)(2,1)S(1)}, u32[]{:S(2)}, u32[]{:S(2)}) collective-permute-start(bf16[192,1280]{1,0:T(8,128)(2,1)S(1)} %get-tuple-element.251), channel_id=1, source_target_pairs={{0,3},{1,2},{2,1},{3,0},{4,7},{5,6},{6,5},{7,4},{8,11},{9,10},{10,... | collective-permute-start | bytes 1474568 | tf_op jit(solution)/shard_map/ppermute | solution.py:110
  685.8 75.5 %collective-permute-start.58 = (bf16[384,1280]{1,0:T(8,128)(2,1)S(1)}, bf16[384,1280]{1,0:T(8,128)(2,1)S(1)}, u32[]{:S(2)}, u32[]{:S(2)}) collective-permute-start(bf16[384,1280]{1,0:T(8,128)(2,1)S(1)} %convolution_convert_fusion.16), channel_id=1, source_target_pairs={{0,8},{1,9},{2,10},{3,11},{4,12},{5,13},{6,14},{7,15},{8,0},{9,1},... | collective-permute-start | bytes 2949128 | tf_op jit(solution)/shard_map/ppermute | solution.py:106
  687.5 73.8 %collective-permute-start.62 = (bf16[384,1280]{1,0:T(8,128)(2,1)S(1)}, bf16[384,1280]{1,0:T(8,128)(2,1)S(1)}, u32[]{:S(2)}, u32[]{:S(2)}) collective-permute-start(bf16[384,1280]{1,0:T(8,128)(2,1)S(1)} %convolution_convert_fusion.15), channel_id=1, source_target_pairs={{0,4},{1,5},{2,6},{3,7},{4,8},{5,9},{6,10},{7,11},{8,12},{9,13},{1... | collective-permute-start | bytes 2949128 | tf_op jit(solution)/shard_map/ppermute | solution.py:106
  729.0 176.0 %collective-permute-start.3 = (bf16[192,1280]{1,0:T(8,128)(2,1)}, bf16[192,1280]{1,0:T(8,128)(2,1)}, u32[]{:S(2)}, u32[]{:S(2)}) collective-permute-start(bf16[192,1280]{1,0:T(8,128)(2,1)} %get-tuple-element.265), channel_id=1, source_target_pairs={{0,1},{1,0},{2,3},{3,2},{4,5},{5,4},{6,7},{7,6},{8,9},{9,8},{10,11... | collective-permute-start | bytes 1474568 | tf_op jit(solution)/shard_map/ppermute | solution.py:110
  730.8 176.7 %collective-permute-start.4 = (bf16[192,1280]{1,0:T(8,128)(2,1)}, bf16[192,1280]{1,0:T(8,128)(2,1)}, u32[]{:S(2)}, u32[]{:S(2)}) collective-permute-start(bf16[192,1280]{1,0:T(8,128)(2,1)} %get-tuple-element.264), channel_id=1, source_target_pairs={{0,2},{1,3},{2,0},{3,1},{4,6},{5,7},{6,4},{7,5},{8,10},{9,11},{10,... | collective-permute-start | bytes 1474568 | tf_op jit(solution)/shard_map/ppermute | solution.py:110
  732.1 175.5 %collective-permute-start.5 = (bf16[192,1280]{1,0:T(8,128)(2,1)}, bf16[192,1280]{1,0:T(8,128)(2,1)}, u32[]{:S(2)}, u32[]{:S(2)}) collective-permute-start(bf16[192,1280]{1,0:T(8,128)(2,1)} %get-tuple-element.263), channel_id=1, source_target_pairs={{0,3},{1,2},{2,1},{3,0},{4,7},{5,6},{6,5},{7,4},{8,11},{9,10},{10,... | collective-permute-start | bytes 1474568 | tf_op jit(solution)/shard_map/ppermute | solution.py:110
  761.3 160.9 %collective-permute-start.14 = (bf16[384,1280]{1,0:T(8,128)(2,1)}, bf16[384,1280]{1,0:T(8,128)(2,1)}, u32[]{:S(2)}, u32[]{:S(2)}) collective-permute-start(bf16[384,1280]{1,0:T(8,128)(2,1)} %convolution_convert_fusion.20), channel_id=1, source_target_pairs={{0,12},{1,13},{2,14},{3,15},{4,0},{5,1},{6,2},{7,3},{8,4},{9,5},{1... | collective-permute-start | bytes 2949128 | tf_op jit(solution)/shard_map/ppermute | solution.py:106
  808.2 177.1 %collective-permute-start.79 = (bf16[4,2,2,40,3968]{4,3,2,1,0:T(8,128)(2,1)}, bf16[4,2,2,40,3968]{4,3,2,1,0:T(8,128)(2,1)}, u32[]{:S(2)}, u32[]{:S(2)}) collective-permute-start(bf16[4,2,2,40,3968]{4,3,2,1,0:T(8,128)(2,1)} %dynamic-slice_bitcast_fusion), channel_id=1, source_target_pairs={{0,16},{16,0},{1,17},{17,1},{2,18},{18,2},{3,19},{19,3},{4,20},{20... | collective-permute-start | bytes 15237128 | tf_op jit(solution)/shard_map/ppermute | solution.py:138
  905.0 67.5 %collective-permute-start.23 = (bf16[384,1280]{1,0:T(8,128)(2,1)}, bf16[384,1280]{1,0:T(8,128)(2,1)}, u32[]{:S(2)}, u32[]{:S(2)}) collective-permute-start(bf16[384,1280]{1,0:T(8,128)(2,1)} %convolution_convert_fusion.19), channel_id=1, source_target_pairs={{0,8},{1,9},{2,10},{3,11},{4,12},{5,13},{6,14},{7,15},{8,0},{9,1},... | collective-permute-start | bytes 2949128 | tf_op jit(solution)/shard_map/ppermute | solution.py:106
  907.4 65.1 %collective-permute-start.32 = (bf16[384,1280]{1,0:T(8,128)(2,1)}, bf16[384,1280]{1,0:T(8,128)(2,1)}, u32[]{:S(2)}, u32[]{:S(2)}) collective-permute-start(bf16[384,1280]{1,0:T(8,128)(2,1)} %convolution_convert_fusion.18), channel_id=1, source_target_pairs={{0,4},{1,5},{2,6},{3,7},{4,8},{5,9},{6,10},{7,11},{8,12},{9,13},{1... | collective-permute-start | bytes 2949128 | tf_op jit(solution)/shard_map/ppermute | solution.py:106
  907.6 86.6 %collective-permute-start.63 = (bf16[4,2,2,40,3968]{4,3,2,1,0:T(8,128)(2,1)}, bf16[4,2,2,40,3968]{4,3,2,1,0:T(8,128)(2,1)}, u32[]{:S(2)}, u32[]{:S(2)}) collective-permute-start(bf16[4,2,2,40,3968]{4,3,2,1,0:T(8,128)(2,1)} %dynamic-slice_bitcast_fusion.1), channel_id=1, source_target_pairs={{0,16},{16,0},{1,17},{17,1},{2,18},{18,2},{3,19},{19,3},{4,20},{20... | collective-permute-start | bytes 15237128 | tf_op jit(solution)/shard_map/ppermute | solution.py:138
  1001.7 51.5 %collective-permute-start.85 = (bf16[4,2,40,1408]{3,2,1,0:T(8,128)(2,1)S(1)}, bf16[4,2,40,1408]{3,2,1,0:T(8,128)(2,1)S(1)}, u32[]{:S(2)}, u32[]{:S(2)}) collective-permute-start(bf16[4,2,40,1408]{3,2,1,0:T(8,128)(2,1)S(1)} %dynamic-slice_bitcast_fusion.3), channel_id=1, source_target_pairs={{0,1},{1,0},{2,3},{3,2},{4,5},{5,4},{6,7},{7,6},{8,9},{9,8},{10,11... | collective-permute-start | bytes 2703368 | tf_op jit(solution)/shard_map/ppermute | solution.py:110
  1003.7 51.2 %collective-permute-start.90 = (bf16[4,2,40,1408]{3,2,1,0:T(8,128)(2,1)S(1)}, bf16[4,2,40,1408]{3,2,1,0:T(8,128)(2,1)S(1)}, u32[]{:S(2)}, u32[]{:S(2)}) collective-permute-start(bf16[4,2,40,1408]{3,2,1,0:T(8,128)(2,1)S(1)} %dynamic-slice_bitcast_fusion.2), channel_id=1, source_target_pairs={{0,2},{1,3},{2,0},{3,1},{4,6},{5,7},{6,4},{7,5},{8,10},{9,11},{10,... | collective-permute-start | bytes 2703368 | tf_op jit(solution)/shard_map/ppermute | solution.py:110
  (242 other events, 3713.5 us)
Sparse Core Ops, SparseCore 0:
  11.6 132.5 all-gather.6
  147.7 83.8 all-gather.8
  233.7 12.7 all-gather.10
  248.4 12.0 all-gather.12
  537.7 7.5 reduce-scatter.4
  922.3 15.5 reduce-scatter.2

commit v2 on v1

v2 whole, which is shorter than its diff:
```python
import functools

import jax
import jax.numpy as jnp
from jax import lax
from jax.experimental import pallas as pl
from jax.experimental.pallas import tpu as pltpu
from jax.sharding import PartitionSpec as P

HD = 128
STEP = 4


eps_norm = 1e-06
theta_base = 10000.0
momentum_decay = 0.9
mask_fill = -1e30
rate_attention_in = 2e-05
rate_attention_out = 0.002
rate_shared_in = 3e-05
rate_shared_down = 0.0002
rate_router = 1.5e-05
rate_gains = 0.0002
rate_expert_in = 0.0004
rate_expert_down = 0.008


def rope_tables(length, head_width):
    half_width = head_width // 2
    frequency = theta_base ** (-(jnp.arange(half_width, dtype=jnp.float32) * 2.0 / head_width))
    angles = jnp.arange(length, dtype=jnp.float32)[:, None] * frequency[None, :]
    cosine, sine_table = jnp.cos(angles), jnp.sin(angles)
    return (
        jnp.concatenate([cosine, cosine], axis=1),
        jnp.concatenate([-sine_table, sine_table], axis=1),
    )


def allowed_keys(length, keep_flags):
    amount = keep_flags.shape[0]
    position = jnp.arange(amount)
    causal = position[None, :] <= position[:, None]
    usable = (position < length) & (keep_flags == 1)
    return causal & (usable[None, :] | (position[None, :] == position[:, None]))


def silu_parts(values):
    logistic = jax.nn.sigmoid(values)
    return (values * logistic, logistic * (1.0 + values * (1.0 - logistic)))


def advance(weight, moment, average, gradient, step_rate):
    moment_new = momentum_decay * moment + gradient
    weight_new = weight - step_rate * (gradient + momentum_decay * moment_new)
    average_new = average + (weight_new - average) / (STEP + 1)
    return (weight_new, moment_new, average_new)


def dot_nn(a, b):
    return lax.dot_general(a, b, (((1,), (0,)), ((), ())), preferred_element_type=jnp.float32)


def dot_nt(a, b):
    return lax.dot_general(a, b, (((1,), (1,)), ((), ())), preferred_element_type=jnp.float32)


def dot_tn(a, b):
    return lax.dot_general(a, b, (((0,), (0,)), ((), ())), preferred_element_type=jnp.float32)


PLANE = 4
MESH = pl.DeviceIdType.MESH


class Spot:
    def __init__(self, line):
        here = lax.axis_index("expert")
        self.line = line
        self.core = lax.axis_index("dp")
        self.at = lax.div(here, PLANE)
        rest = lax.rem(here, PLANE)
        self.y, self.x = lax.div(rest, 2), lax.rem(rest, 2)

    def chip(self, at, y, x):
        return (self.core, at * PLANE + y * 2 + x)

    def around(self, amount):
        return lax.rem(self.at + amount + self.line, self.line)

    def partner(self, way):
        if way == "core":
            return (1 - self.core, self.at * PLANE + self.y * 2 + self.x)
        if way == "x":
            return self.chip(self.at, self.y, 1 - self.x)
        if way == "y":
            return self.chip(self.at, 1 - self.y, self.x)
        return self.chip(self.around(1 if way == "up" else -1), self.y, self.x)


def meet(spot):
    barrier = pltpu.get_barrier_semaphore()
    for way in ("core", "x", "y", "up", "down"):
        pl.semaphore_signal(barrier, inc=1, device_id=spot.partner(way), device_id_type=MESH)
    pl.semaphore_wait(barrier, 5)


class Moves:
    def __init__(self, spot, send_sems, recv_sems, local_sems):
        self.spot, self.send_sems, self.recv_sems = spot, send_sems, recv_sems
        self.local_sems = local_sems
        self.made, self.kept, self.loose = 0, 0, []

    def start(self, source, target, way, later=False):
        copy = pltpu.make_async_remote_copy(
            src_ref=source,
            dst_ref=target,
            send_sem=self.send_sems.at[self.made],
            recv_sem=self.recv_sems.at[self.made],
            device_id=self.spot.partner(way),
            device_id_type=MESH,
        )
        self.made += 1
        copy.start()
        if later:
            self.loose.append(copy)
        return copy

    def keep(self, source, target, later=False):
        copy = pltpu.make_async_copy(source, target, self.local_sems.at[self.kept])
        self.kept += 1
        copy.start()
        if later:
            self.loose.append(copy)
        return copy

    def finish(self):
        for copy in self.loose:
            copy.wait()


def in_turn(chains):
    while chains:
        left = []
        for chain in chains:
            try:
                next(chain)
                left.append(chain)
            except StopIteration:
                pass
        chains = left


def line_chain(moves, own, whole):
    line = moves.spot.line
    half, rest = line // 2, (line - 1) // 2
    moves.keep(own, whole.at[0], later=True)
    up, down = own, own
    for i in range(1, half + 1):
        rising = moves.start(up, whole.at[i], "up")
        if i <= rest:
            falling = moves.start(down, whole.at[line - i], "down")
        yield
        rising.wait()
        up = whole.at[i]
        if i <= rest:
            falling.wait()
            down = whole.at[line - i]


def swap_chain(moves, own, whole, way):
    core = moves.spot.core
    copy = moves.start(own, whole.at[core], way)
    yield
    copy.wait()
    moves.start(whole.at[core], whole.at[core], "core", later=True)


def core_chain(moves, own, whole):
    core = moves.spot.core
    moves.keep(own, whole.at[core], later=True)
    moves.start(own, whole.at[core], "core", later=True)
    yield


def dense_chain(moves, whole, columns, order):
    spot = moves.spot
    half, rest = spot.line // 2, (spot.line - 1) // 2
    everything = slice(None)
    held = {"z": spot.at, "y": spot.y, "x": spot.x}

    def region(**other):
        at = dict(held, **other)
        return whole.at[spot.core, at["z"], at["y"], at["x"], everything, columns]

    def forward(part):
        moves.start(part, part, "core", later=True)

    for stage, dim in enumerate(order):
        if dim == "z":
            up = down = None
            for i in range(1, half + 1):
                part = region(z=spot.around(1 - i))
                up = moves.start(part, part, "up")
                if i <= rest:
                    part = region(z=spot.around(i - 1))
                    down = moves.start(part, part, "down")
                if stage == 0 and i == 1:
                    forward(region())
                yield
                up.wait()
                forward(region(z=spot.around(-i)))
                if i <= rest:
                    down.wait()
                    forward(region(z=spot.around(i)))
        else:
            part = region()
            copy = moves.start(part, part, dim)
            if stage == 0:
                forward(region())
            yield
            copy.wait()
            forward(region(**{dim: 1 - held[dim]}))
        held[dim] = everything


ORDERS = ("xyz", "yzx", "zxy", "zyx")


def first_kernel(line, plans, *refs):
    count = len(plans)
    shards, refs = refs[:count], refs[count:]
    grads, gate, up, down = refs[:4]
    results, refs = refs[4 : 4 + count], refs[4 + count :]
    line_grads, gates, ups, downs = refs[0], refs[1:4], refs[4:5], refs[5:8]
    refs = refs[8:]
    wholes, refs = refs[:count], refs[count:]
    spot = Spot(line)
    meet(spot)
    moves = Moves(spot, *refs)
    loads = [
        moves.keep(shards[n], wholes[n].at[spot.core, spot.at, spot.y, spot.x])
        for n in range(count)
    ]
    for copy in loads:
        copy.wait()
    chains = []
    for n, plan in enumerate(plans):
        start = 0
        for order, width in plan:
            columns = slice(start, start + width)
            chains.append(dense_chain(moves, wholes[n], columns, ORDERS[order]))
            start += width
    chains.append(line_chain(moves, grads, line_grads))
    for own, whole in ((gate, gates), (down, downs)):
        chains.append(swap_chain(moves, own, whole[1], "x"))
        chains.append(swap_chain(moves, own, whole[2], "y"))
    for own, whole in ((gate, gates), (up, ups), (down, downs)):
        chains.append(core_chain(moves, own, whole[0]))
    in_turn(chains)
    moves.finish()
    stores = [moves.keep(wholes[n], results[n]) for n in range(count)]
    for copy in stores:
        copy.wait()


def hbm(count):
    return [pl.BlockSpec(memory_space=pl.ANY)] * count


def semaphores(remote, local):
    return [
        pltpu.SemaphoreType.DMA((remote,)),
        pltpu.SemaphoreType.DMA((remote,)),
        pltpu.SemaphoreType.DMA((local,)),
    ]


def both_halves(array):
    return jax.ShapeDtypeStruct((2,) + array.shape, array.dtype)


def first_exchange(experts, shards, plans, grads, gate, up, down):
    line = experts // PLANE
    count = len(shards)
    chains = sum(len(plan) for plan in plans)
    remote = chains * (2 * line + 3) + line + 4 * 2 + 3
    out_shape = [
        jax.ShapeDtypeStruct((2, line, 2, 2) + shard.shape, shard.dtype) for shard in shards
    ]
    out_shape += [jax.ShapeDtypeStruct((line,) + grads.shape, grads.dtype)]
    out_shape += [both_halves(gate)] * 3 + [both_halves(up)] + [both_halves(down)] * 3
    out = pl.pallas_call(
        functools.partial(first_kernel, line, plans),
        out_shape=out_shape,
        in_specs=hbm(count + 4),
        out_specs=hbm(count + 8),
        scratch_shapes=[
            pltpu.VMEM((2, line, 2, 2) + shard.shape, shard.dtype) for shard in shards
        ]
        + semaphores(remote, 2 * count + 4),
        compiler_params=pltpu.CompilerParams(
            collective_id=1, has_side_effects=True, vmem_limit_bytes=48 * 1024 * 1024
        ),
    )(*shards, grads, gate, up, down)
    return out[:count], out[count], out[count + 1 : count + 4], out[count + 4], out[count + 5 :]


def second_kernel(line, *refs):
    rows, up, gate_x, down_x, down_y = refs[:5]
    line_rows, up_x, up_y, far_gate, far_up, far_down = refs[5:11]
    spot = Spot(line)
    meet(spot)
    moves = Moves(spot, *refs[11:])
    core = spot.core
    half = down_x.shape[1] // 2

    def far_up_chain():
        yield
        copy = moves.start(up_y.at[core], far_up.at[core], "x")
        yield
        copy.wait()
        moves.start(far_up.at[core], far_up.at[core], "core", later=True)

    def part_chain(source, whole, part, way):
        copy = moves.start(source.at[core, part], whole.at[core, part], way)
        yield
        copy.wait()
        moves.start(whole.at[core, part], whole.at[core, part], "core", later=True)

    everything = slice(None)
    in_turn(
        [
            swap_chain(moves, up, up_x, "x"),
            swap_chain(moves, up, up_y, "y"),
            line_chain(moves, rows, line_rows),
            far_up_chain(),
            part_chain(down_y, far_down, slice(half, 2 * half), "x"),
            part_chain(down_x, far_down, slice(0, half), "y"),
            part_chain(gate_x, far_gate, everything, "y"),
        ]
    )
    moves.finish()


def second_exchange(experts, rows, up, gate_x, down_x, down_y):
    line = experts // PLANE
    out_shape = [jax.ShapeDtypeStruct((line,) + rows.shape, rows.dtype)]
    out_shape += [both_halves(up)] * 2
    out_shape += [jax.ShapeDtypeStruct(array.shape, array.dtype) for array in (gate_x, gate_x, down_x)]
    return pl.pallas_call(
        functools.partial(second_kernel, line),
        out_shape=out_shape,
        in_specs=hbm(5),
        out_specs=hbm(6),
        scratch_shapes=semaphores(line + 12, 1),
        compiler_params=pltpu.CompilerParams(collective_id=3, has_side_effects=True),
    )(rows, up, gate_x, down_x, down_y)


def third_kernel(line, *refs):
    low, full = jnp.bfloat16, jnp.float32
    grads = refs[0]
    kept = [refs[1 + 5 * q : 6 + 5 * q] for q in range(PLANE)]
    refs = refs[1 + 5 * PLANE :]
    total = refs[0]
    owns = [refs[1 + 3 * q : 4 + 3 * q] for q in range(PLANE - 1)]
    refs = refs[1 + 3 * (PLANE - 1) :]
    crossed = [refs[3 * q : 3 + 3 * q] for q in range(PLANE - 1)]
    refs = refs[3 * (PLANE - 1) :]
    far_in, refs = refs[:4], refs[4:]
    boxes, extra, refs = refs[0], refs[1:3], refs[3:]
    loaded, refs = [refs[:5], refs[5:10]], refs[10:]
    results, refs = [refs[:6], refs[6:12]], refs[12:]
    far_box, down_grad, total_box, refs = refs[:3], refs[3], refs[4], refs[5:]
    spot = Spot(line)
    meet(spot)
    moves = Moves(spot, *refs)
    half, rest = line // 2, (line - 1) // 2
    order = (3, 1, 2, 0)
    loads = {}

    def load(n):
        loads[n] = [moves.keep(kept[order[n]][i], loaded[n % 2][i]) for i in range(5)]

    def add(target, source):
        target[...] = (target[...].astype(full) + source[...].astype(full)).astype(low)

    def sums(way, sign, steps):
        at = lambda i: i if sign > 0 else (line - i) % line
        source = grads.at[at(steps)]
        box = extra[0 if sign > 0 else 1]
        for i in range(steps, 0, -1):
            copy = moves.start(source, boxes.at[at(i) - 1], way)
            if i > 1:
                part = moves.keep(grads.at[at(i - 1)], box)
            yield
            copy.wait()
            source = boxes.at[at(i) - 1]
            if i > 1:
                part.wait()
                add(source, box)
            else:
                total_box[...] += source[...].astype(full)

    own_part = moves.keep(grads.at[0], extra[0])
    load(0)
    own_part.wait()
    total_box[...] = extra[0][...].astype(full)

    rows_half = results[0][0].shape[0]
    down_half = results[0][2].shape[0]
    sent = {}

    def weights(n):
        if n + 1 < PLANE:
            load(n + 1)
        for copy in loads[n]:
            copy.wait()
        rows, inner, gated, grad_gate, grad_up = loaded[n % 2]
        buffers = results[n % 2]
        if n == 3:
            for copy in sent[1]:
                copy.wait()
        down_grad[...] = dot_tn(inner[...], gated[...]).astype(low)
        for which in (1, 0):
            place = jnp.bitwise_xor(spot.core, which)
            gate_out, up_out, down_out = buffers[3 * which : 3 * which + 3]
            part = rows[:, pl.ds(pl.multiple_of(place * rows_half, 128), rows_half)]
            gate_out[...] = dot_tn(part, grad_gate[...]).astype(low)
            up_out[...] = dot_tn(part, grad_up[...]).astype(low)
            down_out[...] = down_grad[pl.ds(pl.multiple_of(place * down_half, 16), down_half), :]
            q = order[n]
            targets = far_box if q == PLANE - 1 else crossed[q]
            if which:
                sent[n] = [
                    moves.start(buffers[3 + i], targets[i], "core") for i in range(3)
                ]
            elif q < PLANE - 1:
                sent[n] += [moves.keep(buffers[i], owns[q][i]) for i in range(3)]

    def far():
        for copy in sent[0]:
            copy.wait()
        mine = results[0][:3]
        for i in range(3):
            add(far_box[i], mine[i])
        edge = down_half // 2
        moves.start(far_box[0], far_in[0], "y", later=True)
        moves.start(far_box[1], far_in[1], "x", later=True)
        moves.start(far_box[2].at[pl.ds(0, edge)], far_in[2], "y", later=True)
        moves.start(far_box[2].at[pl.ds(edge, edge)], far_in[3], "x", later=True)

    chains = [sums("down", 1, half), sums("up", -1, rest)]
    for chain in chains:
        next(chain, None)
    weights(0)
    weights(1)
    far()
    weights(2)
    for chain in chains:
        next(chain, None)
    weights(3)
    in_turn(chains)
    store = moves.keep(total_box, total)
    for n in (2, 3):
        for copy in sent[n]:
            copy.wait()
    store.wait()
    moves.finish()


def third_exchange(experts, grads, kept):
    line = experts // PLANE
    low = jnp.bfloat16
    rows, inner = kept[0][0], kept[0][1]
    width, hidden_width = rows.shape[1], inner.shape[1]
    half, down_half = width // 2, hidden_width // 2
    pieces = [(half, hidden_width), (half, hidden_width), (down_half, width)]
    far = pieces[:2] + [(down_half // 2, width)] * 2
    shape = lambda size, dtype=low: jax.ShapeDtypeStruct(size, dtype)
    out = pl.pallas_call(
        functools.partial(third_kernel, line),
        out_shape=[shape(grads.shape[1:], jnp.float32)]
        + [shape(size) for size in pieces * (2 * (PLANE - 1))]
        + [shape(size) for size in far],
        in_specs=hbm(1 + 5 * PLANE),
        out_specs=hbm(1 + 6 * (PLANE - 1) + 4),
        scratch_shapes=[pltpu.VMEM((line - 1,) + grads.shape[1:], low)]
        + [pltpu.VMEM(grads.shape[1:], low)] * 2
        + [pltpu.VMEM(array.shape, low) for array in kept[0]] * 2
        + [pltpu.VMEM(size, low) for size in pieces * 4]
        + [pltpu.VMEM(size, low) for size in pieces]
        + [pltpu.VMEM((hidden_width, width), low), pltpu.VMEM(grads.shape[1:], jnp.float32)]
        + semaphores(line + 3 * PLANE + 4, line + 8 * PLANE + 2),
        compiler_params=pltpu.CompilerParams(
            collective_id=4, has_side_effects=True, vmem_limit_bytes=62 * 1024 * 1024
        ),
    )(grads, *[array for parts in kept for array in parts])
    total, out = out[0], out[1:]
    count = 3 * (PLANE - 1)
    triples = lambda arrays: [arrays[3 * q : 3 * q + 3] for q in range(PLANE - 1)]
    return total, triples(out[:count]), triples(out[count : 2 * count]), out[2 * count :]


def sum_kernel(line, plans, ways, *refs):
    count = len(plans)
    given = sum(len(order) for plan in plans for order in plan)
    grads, refs = refs[:given], refs[given:]
    moved, refs = refs[: len(ways)], refs[len(ways) :]
    sums, refs = refs[:count], refs[count:]
    arrived, refs = refs[: len(ways)], refs[len(ways) :]
    kept, refs = refs[: 3 * count], refs[3 * count :]
    core_in, refs = refs[: 3 * count], refs[3 * count :]
    first_in, refs = refs[: 3 * count], refs[3 * count :]
    second_in, refs = refs[: 3 * count], refs[3 * count :]
    third_in, refs = refs[: 3 * count], refs[3 * count :]
    spot = Spot(line)
    meet(spot)
    moves = Moves(spot, *refs)
    half, rest = line // 2, (line - 1) // 2
    everything = slice(None)
    orders = ("xyz", "yzx", "zxy")

    loads, swaps = [], []
    at = 0
    for n, plan in enumerate(plans):
        for o, pieces in enumerate(plan):
            mine, theirs = [], []
            start = 0
            for first, width in pieces:
                ref = grads[at]
                source = slice(first, first + width)
                target = slice(start, start + width)
                mine.append(
                    moves.keep(
                        ref.at[spot.core, :, :, :, :, source],
                        kept[3 * n + o].at[:, :, :, :, target],
                    )
                )
                theirs.append(
                    moves.start(
                        ref.at[1 - spot.core, :, :, :, :, source],
                        core_in[3 * n + o].at[:, :, :, :, target],
                        "core",
                    )
                )
                at += 1
                start += width
            loads.append(mine)
            swaps.append(theirs)

    for way, source, target in zip(ways, moved, arrived):
        moves.start(source, target, way, later=True)

    def add(target, source):
        lead = target.shape[:-2]
        total = 1
        for extent in lead:
            total *= extent

        def one(i, carry):
            index = []
            for extent in reversed(lead):
                index.insert(0, lax.rem(i, extent))
                i = lax.div(i, extent)
            index = tuple(index)
            target[index] = (
                target[index].astype(jnp.float32) + source[index].astype(jnp.float32)
            ).astype(target.dtype)
            return carry

        lax.fori_loop(0, total, one, 0)

    def chain(n, o):
        buffer = kept[3 * n + o]
        mine, theirs = loads[3 * n + o], swaps[3 * n + o]
        for copy in mine:
            copy.wait()
        for copy in theirs:
            copy.wait()
        add(buffer, core_in[3 * n + o])
        inbox = [first_in[3 * n + o], second_in[3 * n + o], third_in[3 * n + o]]
        held = {"z": everything, "y": everything, "x": everything}

        def region(**other):
            at = dict(held, **other)
            return buffer.at[at["z"], at["y"], at["x"]]

        for stage, dim in enumerate(orders[o]):
            box = inbox[stage]
            if dim == "z":
                up = down = None
                for i in range(half, 0, -1):
                    down = moves.start(region(z=spot.around(-i)), box.at[i - 1], "down")
                    if i <= rest:
                        up = moves.start(region(z=spot.around(i)), box.at[half + i - 1], "up")
                    yield
                    down.wait()
                    add(region(z=spot.around(1 - i)), box.at[i - 1])
                    if i <= rest:
                        up.wait()
                        add(region(z=spot.around(i - 1)), box.at[half + i - 1])
                held[dim] = spot.at
            else:
                own = spot.y if dim == "y" else spot.x
                copy = moves.start(region(**{dim: 1 - own}), box, dim)
                yield
                copy.wait()
                held[dim] = own
                add(region(), box)
        start = sum(sum(width for _, width in pieces) for pieces in plans[n][:o])
        width = sum(width for _, width in plans[n][o])
        result = moves.keep(region(), sums[n].at[:, slice(start, start + width)])
        yield
        result.wait()

    in_turn([chain(n, o) for n in range(count) for o in range(3)])
    moves.finish()


def sum_all(experts, grads, plans, moved, ways):
    line = experts // PLANE
    half, rest = line // 2, (line - 1) // 2
    rows = grads[0].shape[0] // (2 * experts)
    dtype = grads[0].dtype
    operands, kernel_plans, shapes = [], [], []
    boxes = [[], [], [], [], []]
    for plan in plans:
        kernel_plan = []
        for o, pieces in enumerate(plan):
            for which, _, _ in pieces:
                array = grads[which]
                operands.append(array.reshape(2, line, 2, 2, rows, array.shape[1]))
            kernel_plan.append(tuple((first, width) for _, first, width in pieces))
            width = sum(width for _, _, width in pieces)
            steps = half + rest
            block = (rows, width)
            boxes[0].append((line, 2, 2) + block)
            boxes[1].append((line, 2, 2) + block)
            if o == 0:
                inboxes = [(line, 2), (line,), (steps,)]
            elif o == 1:
                inboxes = [(line, 2), (steps, 2), ()]
            else:
                inboxes = [(steps, 2, 2), (2,), ()]
            for i, lead in enumerate(inboxes):
                boxes[2 + i].append(lead + block)
        kernel_plans.append(tuple(kernel_plan))
        total = sum(width for pieces in kernel_plan for _, width in pieces)
        shapes.append(jax.ShapeDtypeStruct((rows, total), dtype))
    count = len(plans)
    number = len(operands) + 3 * count * (line + 1) + len(moved)
    shapes += [jax.ShapeDtypeStruct(array.shape, array.dtype) for array in moved]
    return pl.pallas_call(
        functools.partial(sum_kernel, line, tuple(kernel_plans), ways),
        out_shape=shapes,
        in_specs=hbm(len(operands) + len(moved)),
        out_specs=hbm(count + len(moved)),
        scratch_shapes=[pltpu.VMEM(shape, dtype) for kind in boxes for shape in kind]
        + semaphores(number, len(operands) + 3 * count),
        compiler_params=pltpu.CompilerParams(
            collective_id=2, has_side_effects=True, vmem_limit_bytes=60 * 1024 * 1024
        ),
    )(*operands, *moved)


def turn(values, cosine, sine_table):
    return values * cosine + pltpu.roll(values, HD // 2, 1) * sine_table


def turn_back(values, cosine, sine_table):
    return values * cosine - pltpu.roll(values, HD // 2, 1) * sine_table


def probabilities(query, key, bias):
    scores = dot_nt(query, key) * HD ** (-0.5) + bias
    exps = jnp.exp(scores - jnp.max(scores, axis=1, keepdims=True))
    return exps / jnp.sum(exps, axis=1, keepdims=True)


def attend_kernel(
    steps,
    normed,
    query_weight,
    key_weight,
    value_weight,
    out_weight,
    bias,
    cosine,
    sine_table,
    inputs,
    gain,
    query_out,
    key_out,
    value_out,
    attended_out,
    hidden_out,
    normed_out,
):
    step = pl.program_id(0)
    low = jnp.bfloat16
    n1 = normed[...]
    cos, sin = cosine[...], sine_table[...]
    query = dot_nt(n1, query_weight[...])
    key = dot_nt(n1, key_weight[...])
    value_out[...] = dot_nt(n1, value_weight[...]).astype(low)
    for part in range(query.shape[1] // HD):
        columns = slice(part * HD, (part + 1) * HD)
        q = turn(query[:, columns], cos, sin).astype(low)
        k = turn(key[:, columns], cos, sin).astype(low)
        query_out[:, columns] = q
        key_out[:, columns] = k
        probs = probabilities(q, k, bias[...])
        attended_out[:, columns] = dot_nn(probs.astype(low), value_out[:, columns]).astype(low)
    branch = dot_nt(attended_out[...], out_weight[...])

    @pl.when(step == 0)
    def _():
        hidden_out[...] = inputs[...].astype(jnp.float32) + branch

    @pl.when(step > 0)
    def _():
        hidden_out[...] += branch

    @pl.when(step == steps - 1)
    def _():
        hidden = hidden_out[...]
        rstd = lax.rsqrt(jnp.mean(hidden * hidden, axis=1, keepdims=True) + eps_norm)
        normed_out[...] = (hidden * rstd * gain[...]).astype(low)


def attend(normed, weights, out_weight, bias, cosine, sine_table, inputs, gain):
    tokens, width = normed.shape
    group = 2 * HD
    steps = width // group
    low = jnp.bfloat16
    whole = lambda *shape: pl.BlockSpec(shape, lambda i: (0,) * len(shape))
    columns = pl.BlockSpec((tokens, group), lambda i: (0, i))
    return pl.pallas_call(
        functools.partial(attend_kernel, steps),
        grid=(steps,),
        in_specs=[whole(tokens, width)]
        + [pl.BlockSpec((group, width), lambda i, m=m: (i, m)) for m in range(3)]
        + [
            pl.BlockSpec((width, group), lambda i: (0, i)),
            whole(tokens, tokens),
            whole(tokens, HD),
            whole(tokens, HD),
            whole(tokens, width),
            whole(1, width),
        ],
        out_specs=[columns] * 4 + [whole(tokens, width)] * 2,
        out_shape=[jax.ShapeDtypeStruct((tokens, width), low)] * 4
        + [
            jax.ShapeDtypeStruct((tokens, width), jnp.float32),
            jax.ShapeDtypeStruct((tokens, width), low),
        ],
        compiler_params=pltpu.CompilerParams(vmem_limit_bytes=48 * 1024 * 1024),
        cost_estimate=pl.CostEstimate(
            flops=8 * tokens * width * width, bytes_accessed=20 * width * width, transcendentals=0
        ),
    )(normed, weights, weights, weights, out_weight, bias, cosine, sine_table, inputs, gain)


def attend_back_kernel(
    grad_branch,
    normed,
    query_in,
    key_in,
    value_in,
    attended_in,
    query_weight,
    key_weight,
    value_weight,
    out_weight,
    bias,
    cosine,
    sine_table,
    grad_query_weight,
    grad_key_weight,
    grad_value_weight,
    grad_out_weight,
    grad_normed,
    grads,
):
    step = pl.program_id(0)
    low = jnp.bfloat16
    da = grad_branch[...]
    n1 = normed[...]
    cos, sin = cosine[...], sine_table[...]
    scaling = HD ** (-0.5)
    group = query_in.shape[1]
    grad_out_weight[...] = dot_tn(da, attended_in[...]).astype(low)
    grad_attended = dot_nn(da, out_weight[...]).astype(low)
    for part in range(group // HD):
        columns = slice(part * HD, (part + 1) * HD)
        q, k, v = query_in[:, columns], key_in[:, columns], value_in[:, columns]
        do = grad_attended[:, columns]
        probs = probabilities(q, k, bias[...])
        grad_probs = dot_nt(do, v)
        grad_scores = probs * (grad_probs - jnp.sum(probs * grad_probs, axis=1, keepdims=True))
        grad_scores = grad_scores.astype(low)
        grads[0, :, columns] = turn_back(dot_nn(grad_scores, k) * scaling, cos, sin).astype(low)
        grads[1, :, columns] = turn_back(dot_tn(grad_scores, q) * scaling, cos, sin).astype(low)
        grads[2, :, columns] = dot_tn(probs.astype(low), do).astype(low)
    grad_query_weight[...] = dot_tn(grads[0], n1).astype(low)
    grad_key_weight[...] = dot_tn(grads[1], n1).astype(low)
    grad_value_weight[...] = dot_tn(grads[2], n1).astype(low)
    total = (
        dot_nn(grads[0], query_weight[...])
        + dot_nn(grads[1], key_weight[...])
        + dot_nn(grads[2], value_weight[...])
    )

    @pl.when(step == 0)
    def _():
        grad_normed[...] = total

    @pl.when(step > 0)
    def _():
        grad_normed[...] += total


def attend_back(
    grad_branch, normed, query, key, value, attended, weights, out_weight, bias, cosine, sine_table
):
    tokens, width = normed.shape
    group = 2 * HD
    steps = width // group
    low = jnp.bfloat16
    whole = lambda *shape: pl.BlockSpec(shape, lambda i: (0,) * len(shape))
    columns = pl.BlockSpec((tokens, group), lambda i: (0, i))
    return pl.pallas_call(
        attend_back_kernel,
        grid=(steps,),
        in_specs=[whole(tokens, width)] * 2
        + [columns] * 4
        + [pl.BlockSpec((group, width), lambda i, m=m: (i, m)) for m in range(3)]
        + [
            pl.BlockSpec((width, group), lambda i: (0, i)),
            whole(tokens, tokens),
            whole(tokens, HD),
            whole(tokens, HD),
        ],
        out_specs=[pl.BlockSpec((group, width), lambda i: (i, 0))] * 3
        + [pl.BlockSpec((width, group), lambda i: (0, i)), whole(tokens, width)],
        out_shape=[jax.ShapeDtypeStruct((width, width), low)] * 4
        + [jax.ShapeDtypeStruct((tokens, width), jnp.float32)],
        scratch_shapes=[pltpu.VMEM((3, tokens, group), low)],
        compiler_params=pltpu.CompilerParams(vmem_limit_bytes=48 * 1024 * 1024),
        cost_estimate=pl.CostEstimate(
            flops=16 * tokens * width * width, bytes_accessed=40 * width * width, transcendentals=0
        ),
    )(
        grad_branch,
        normed,
        query,
        key,
        value,
        attended,
        weights,
        weights,
        weights,
        out_weight,
        bias,
        cosine,
        sine_table,
    )


def expert_kernel(
    place,
    rows_in,
    grads_in,
    slots_in,
    gates_in,
    gate_weight,
    up_weight,
    down_weight,
    *refs,
    slots,
    add,
):
    if add:
        grad_before, result_before, *refs = refs
    (
        grad_total,
        result_total,
        rows_out,
        inner_out,
        gated_out,
        grad_gate_out,
        grad_up_out,
    ) = refs
    low, full = jnp.bfloat16, jnp.float32
    group, tokens = slots_in.shape[0], slots_in.shape[2]
    width = rows_in.shape[2]

    slot_ids = lax.broadcasted_iota(jnp.int32, (slots, tokens), 0).astype(full)
    places = [slots_in[r] == slot_ids for r in range(group)]
    hot = [here.astype(low) for here in places]
    gate_col = jnp.concatenate(
        [
            jnp.sum(jnp.where(places[r], gates_in[r], 0.0), axis=1, keepdims=True)
            for r in range(group)
        ],
        axis=0,
    )
    for r in range(group):
        rows_out[r * slots : (r + 1) * slots, :] = dot_nn(hot[r], rows_in[r, :tokens]).astype(low)
    grad_rows = jnp.concatenate(
        [dot_nn(hot[r], grads_in[r, :tokens]) for r in range(group)], axis=0
    )
    gated = (grad_rows * gate_col).astype(low)
    gated_out[...] = gated
    rows = rows_out[...]
    gate_rows = dot_nn(rows, gate_weight[...])
    up_rows = dot_nn(rows, up_weight[...])
    logistic = jax.nn.sigmoid(gate_rows)
    silu_rows = gate_rows * logistic
    slope_rows = logistic * (1.0 + gate_rows * (1.0 - logistic))
    inner = (silu_rows * up_rows).astype(low)
    inner_out[...] = inner
    grad_inner = dot_nt(gated, down_weight[...])
    grad_gate_rows = (grad_inner * up_rows * slope_rows).astype(low)
    grad_up_rows = (grad_inner * silu_rows).astype(low)
    grad_gate_out[...] = grad_gate_rows
    grad_up_out[...] = grad_up_rows
    sent_grads = (
        dot_nt(grad_gate_rows, gate_weight[...]) + dot_nt(grad_up_rows, up_weight[...])
    ).astype(low)
    result_rows = dot_nn(inner, down_weight[...])
    gate_grad = jnp.sum(result_rows * grad_rows, axis=1, keepdims=True)
    sent_results = (result_rows * gate_col).astype(low)
    experts = grad_total.shape[1] - tokens
    for r in range(group):
        part = slice(r * slots, (r + 1) * slots)
        grad_sum = dot_tn(hot[r], sent_grads[part])
        result_sum = dot_tn(hot[r], sent_results[part])
        token_grad = jnp.sum(jnp.where(places[r], gate_grad[part], 0.0), axis=0, keepdims=True)
        words = jnp.concatenate(
            split_words(token_grad) + [jnp.zeros((1, width - 3 * tokens), low)], axis=1
        )
        expert_ids = lax.broadcasted_iota(jnp.int32, (experts, width), 0)
        words = jnp.where(expert_ids == place[0], words.astype(full), 0.0)
        if add:
            grad_sum = grad_sum + grad_before[r, :tokens].astype(full)
            result_sum = result_sum + result_before[r].astype(full)
            words = words + grad_before[r, tokens:].astype(full)
        grad_total[r, :tokens] = grad_sum.astype(low)
        grad_total[r, tokens:] = words.astype(low)
        result_total[r] = result_sum.astype(low)


def run_expert(place, rows, grads, slot_rows, gate_rows, weights, before, slots):
    line, _, width = rows.shape
    tokens = slot_rows.shape[2]
    low = jnp.bfloat16
    hidden_width = weights[0].shape[1]
    group = 2
    steps = line // group
    whole = lambda array: pl.BlockSpec(
        array.shape, lambda i, place: (0,) * array.ndim, pipeline_mode=pl.Buffered(1)
    )
    per_line = lambda size: pl.BlockSpec((group, size, width), lambda i, place: (i, 0, 0))
    per_token = pl.BlockSpec((group, 1, tokens), lambda i, place: (i, 0, 0))
    per_row = lambda size: pl.BlockSpec((group * slots, size), lambda i, place: (i, 0))
    count = line * slots
    extended = rows.shape[1]
    return pl.pallas_call(
        functools.partial(expert_kernel, slots=slots, add=bool(before)),
        grid_spec=pltpu.PrefetchScalarGridSpec(
            num_scalar_prefetch=1,
            grid=(steps,),
            in_specs=[per_line(extended), per_line(extended), per_token, per_token]
            + [whole(array) for array in weights]
            + [per_line(extended), per_line(tokens)][: len(before)],
            out_specs=[per_line(extended), per_line(tokens)]
            + [
                per_row(width),
                per_row(hidden_width),
                per_row(width),
                per_row(hidden_width),
                per_row(hidden_width),
            ],
        ),
        out_shape=[jax.ShapeDtypeStruct((line, size, width), low) for size in (extended, tokens)]
        + [
            jax.ShapeDtypeStruct((count, size), low)
            for size in (width, hidden_width, width, hidden_width, hidden_width)
        ],
        compiler_params=pltpu.CompilerParams(vmem_limit_bytes=62 * 1024 * 1024),
        cost_estimate=pl.CostEstimate(
            flops=10 * count * width * hidden_width + 8 * line * slots * tokens * width,
            bytes_accessed=16 * line * tokens * width,
            transcendentals=0,
        ),
    )(place, rows, grads, slot_rows, gate_rows, *weights, *before)


FIRST_ORDERS = (2, 3, 2, 3)


def gather_plan(units, orders):
    least, more = divmod(units, len(orders))
    count = len(orders)
    return tuple((order, 128 * (least + (i >= count - more))) for i, order in enumerate(orders))


def split_words(values):
    words = []
    for _ in range(3):
        words.append(values.astype(jnp.bfloat16))
        values = values - words[-1].astype(jnp.float32)
    return words


def after(value, other):
    return lax.optimization_barrier((value, other))[0]


def add_low(a, b):
    return (a.astype(jnp.float32) + b.astype(jnp.float32)).astype(jnp.bfloat16)


class Grid:
    def __init__(self, experts):
        self.experts = experts
        self.line = experts // PLANE
        here = lax.axis_index("expert")
        self.core = lax.axis_index("dp")
        self.at_line = here // PLANE
        self.at_plane = here % PLANE

    def shift(self, block, amount):
        pairs = [
            (i, ((i // PLANE + amount) % self.line) * PLANE + i % PLANE)
            for i in range(self.experts)
        ]
        return lax.ppermute(block, "expert", pairs)

    def line_sum(self, parts):
        half, rest = self.line // 2, (self.line - 1) // 2
        low = parts[half]
        for i in range(half, 0, -1):
            low = self.shift(low, -1)
            if i > 1:
                low = add_low(parts[i - 1], low)
        total = parts[0].astype(jnp.float32) + low.astype(jnp.float32)
        if rest:
            high = parts[self.line - rest]
            for i in range(rest, 0, -1):
                high = self.shift(high, 1)
                if i > 1:
                    high = add_low(parts[self.line - i + 1], high)
            total = total + high.astype(jnp.float32)
        return total


def local(
    tokens_in,
    lengths,
    key_keep,
    routes,
    cotangent,
    attention_in,
    attention_in_momentum,
    attention_in_average,
    attention_out,
    attention_out_momentum,
    attention_out_average,
    shared_in,
    shared_in_momentum,
    shared_in_average,
    shared_down,
    shared_down_momentum,
    shared_down_average,
    router,
    router_momentum,
    router_average,
    norm_gains,
    norm_gains_momentum,
    norm_gains_average,
    expert_in,
    expert_in_momentum,
    expert_in_average,
    expert_down,
    expert_down_momentum,
    expert_down_average,
):
    low = jnp.bfloat16
    full = jnp.float32
    tokens = tokens_in.shape[0]
    model_width = tokens_in.shape[1]
    top_count = routes.shape[1]
    block_rows = router.shape[0]
    experts = router.shape[1]
    hidden_width = shared_in.shape[2]
    grid = Grid(experts)
    capacity = 9 * tokens * top_count // (8 * experts)
    slots = -(-capacity // 16) * 16
    extra_width = -(-(experts + 2) // 128) * 128

    pack_one = jnp.concatenate(
        [attention_in[m].astype(low).T for m in range(3)]
        + [
            router.astype(low),
            norm_gains.astype(low).T,
            jnp.zeros((block_rows, extra_width - experts - 2), low),
        ],
        axis=1,
    )
    pack_out = attention_out.astype(low).T
    pack_shared = jnp.concatenate(
        [shared_in[0].astype(low), shared_in[1].astype(low), shared_down.astype(low).T], axis=1
    )
    position = jnp.arange(tokens, dtype=jnp.int32)
    usable = position < lengths[0]
    named = jnp.any(
        routes.T[None, :, :] == jnp.arange(experts, dtype=jnp.int32)[:, None, None], axis=1
    )
    member = named & usable[None, :]
    earlier = (position[:, None] < position[None, :]).astype(low)
    counted = dot_nn(member.astype(low), earlier)
    slot_of = jnp.where(member, counted, -1.0)
    wanted = grid.at_line * PLANE + (grid.at_plane ^ jnp.arange(PLANE, dtype=jnp.int32))
    choose = (wanted[:, None] == jnp.arange(experts, dtype=jnp.int32)[None, :]).astype(low)

    def widen(rows):
        return jnp.pad(rows, ((0, 0), (0, model_width - rows.shape[1])))

    gate, up, down = (
        expert_in[0, 0].astype(low),
        expert_in[0, 1].astype(low),
        expert_down[0].astype(low),
    )
    plans = (
        gather_plan(pack_one.shape[1] // 128, FIRST_ORDERS),
        gather_plan(model_width // 128, FIRST_ORDERS),
    )
    (all_one, turned_out), line_grads, gates, up_own, downs = first_exchange(
        experts,
        [pack_one, pack_out],
        plans,
        jnp.concatenate([cotangent, widen(slot_of.astype(low))], axis=0),
        gate,
        up,
        down,
    )
    slot_rows = jnp.stack(
        [dot_nn(choose, line_grads[r, tokens:, :tokens]) for r in range(grid.line)]
    )
    all_one = all_one.reshape(model_width, -1)
    turned_out = turned_out.reshape(model_width, model_width)
    extra = all_one[:, 3 * model_width :]
    router_low = extra[:, :experts]
    gains = extra[:, experts : experts + 2].astype(full).T
    gain_one, gain_two = gains[0], gains[1]
    pack_shared, _ = lax.optimization_barrier((pack_shared, turned_out))
    all_shared = lax.all_gather(pack_shared, ("dp", "expert"), axis=0, tiled=True)
    shared_pair = [all_shared[:, m * hidden_width : (m + 1) * hidden_width] for m in range(2)]
    turned_down = all_shared[:, 2 * hidden_width :]
    inputs = tokens_in.astype(full)
    rstd_one = lax.rsqrt(jnp.mean(inputs * inputs, axis=-1, keepdims=True) + eps_norm)
    normed_one = (inputs * rstd_one * gain_one).astype(low)
    cosine, sine_table = rope_tables(tokens, HD)
    bias = jnp.where(allowed_keys(lengths[0], key_keep), 0.0, mask_fill)
    query, key_rot, value, attended, hidden, normed_two = attend(
        normed_one, all_one, turned_out, bias, cosine, sine_table, tokens_in, gain_two[None]
    )
    rstd_two = lax.rsqrt(jnp.mean(hidden * hidden, axis=-1, keepdims=True) + eps_norm)

    logits = lax.dot_general(
        router_low, normed_two, (((0,), (1,)), ((), ())), preferred_element_type=full
    )
    logits = jnp.where(named, logits, mask_fill)
    logit_exps = jnp.exp(logits - jnp.max(logits, axis=0, keepdims=True))
    gating = logit_exps / jnp.sum(logit_exps, axis=0, keepdims=True)
    gating_live = jnp.where(member, gating, 0.0)
    gate_words = jnp.concatenate(split_words(gating_live), axis=1)
    line_rows, up_x, up_y, *far = second_exchange(
        experts,
        jnp.concatenate([normed_two, widen(gate_words)], axis=0),
        up,
        gates[1],
        downs[1],
        downs[2],
    )
    weights = list(zip(gates, (up_own, up_x, up_y), downs)) + [(far[0], far[1], far[2])]
    weights = [[part.reshape(-1, part.shape[-1]) for part in parts] for parts in weights]
    gate_rows = []
    for r in range(grid.line):
        words = dot_nn(choose, line_rows[r, tokens:, : 3 * tokens])
        gate_rows.append(
            words[:, :tokens] + words[:, tokens : 2 * tokens] + words[:, 2 * tokens :]
        )
    gate_rows = jnp.stack(gate_rows)

    before, kept = [], []
    for q in range(PLANE):
        *before, rows, inner, gated, grad_gate, grad_up = run_expert(
            wanted[q : q + 1],
            line_rows,
            line_grads,
            slot_rows[:, q : q + 1],
            gate_rows[:, q : q + 1],
            weights[q],
            before,
            slots,
        )
        kept.append((rows, inner, gated, grad_gate, grad_up))
    routed_grad, routed_result = before
    routed_grad, owns, crossed, far = third_exchange(experts, routed_grad, kept)
    routed_result = grid.line_sum(after(routed_result, routed_grad))
    gate_grads = routed_grad[tokens:]
    routed_grad = routed_grad[:tokens]
    grad_gating = (
        gate_grads[:, :tokens]
        + gate_grads[:, tokens : 2 * tokens]
        + gate_grads[:, 2 * tokens : 3 * tokens]
    )
    grad_chosen = gating * (grad_gating - jnp.sum(gating * grad_gating, axis=0, keepdims=True))
    grad_logits = grad_chosen.astype(low)
    grad_router = lax.dot_general(
        normed_two, grad_logits, (((0,), (1,)), ((), ())), preferred_element_type=full
    )

    grad_out = cotangent.astype(full)
    shared_gate = dot_nn(normed_two, shared_pair[0])
    shared_up = dot_nn(normed_two, shared_pair[1])
    shared_silu, shared_slope = silu_parts(shared_gate)
    shared_hidden = (shared_silu * shared_up).astype(low)
    shared_result = dot_nt(shared_hidden, turned_down)
    grad_shared_hidden = dot_nn(cotangent, turned_down)
    grad_shared_gate = (grad_shared_hidden * shared_up * shared_slope).astype(low)
    grad_shared_up = (grad_shared_hidden * shared_silu).astype(low)
    grad_normed_two = dot_nt(grad_shared_gate, shared_pair[0]) + dot_nt(
        grad_shared_up, shared_pair[1]
    )
    grad_normed_two = grad_normed_two + lax.dot_general(
        grad_logits, router_low, (((0,), (1,)), ((), ())), preferred_element_type=full
    )

    grad_normed_two = grad_normed_two + routed_grad
    scaled_two = grad_normed_two * gain_two
    grad_gain_two = jnp.sum(grad_normed_two * hidden * rstd_two, axis=0)
    grad_hidden = (
        grad_out
        + rstd_two * scaled_two
        - hidden * rstd_two**3 * jnp.mean(scaled_two * hidden, axis=-1, keepdims=True)
    )
    grad_branch = grad_hidden.astype(low)
    grads_shared = [
        dot_tn(normed_two, grad_shared_gate).astype(low),
        dot_tn(normed_two, grad_shared_up).astype(low),
        dot_tn(cotangent, shared_hidden).astype(low),
    ]
    *grads_attention, grad_normed_one = attend_back(
        grad_branch,
        normed_one,
        query,
        key_rot,
        value,
        attended,
        all_one,
        turned_out,
        bias,
        cosine,
        sine_table,
    )
    near_x = [add_low(*pair) for pair in zip(owns[1], crossed[1])]
    near_y = [add_low(*pair) for pair in zip(owns[2], crossed[2])]
    edge = far[2].shape[0]
    near_x[0] = add_low(near_x[0], far[0])
    near_y[1] = add_low(near_y[1], far[1])
    near_x[2] = jnp.concatenate([add_low(near_x[2][:edge], far[2]), near_x[2][edge:]], axis=0)
    near_y[2] = jnp.concatenate([near_y[2][:edge], add_low(near_y[2][edge:], far[3])], axis=0)
    scaled_one = grad_normed_one * gain_one
    grad_gain_one = jnp.sum(grad_normed_one * inputs * rstd_one, axis=0)
    input_grad = (
        grad_hidden
        + rstd_one * scaled_one
        - inputs * rstd_one**3 * jnp.mean(scaled_one * inputs, axis=-1, keepdims=True)
    )
    grad_extra = jnp.concatenate(
        [
            grad_router.astype(low),
            jnp.stack([grad_gain_one, grad_gain_two], axis=1).astype(low),
            jnp.zeros((model_width, extra_width - experts - 2), low),
        ],
        axis=1,
    )
    cut = 512
    summed_one, summed_two, *arrived = sum_all(
        experts,
        grads_attention + grads_shared + [grad_extra],
        [
            [
                [(0, 0, model_width), (2, 0, cut)],
                [(1, 0, model_width), (7, 0, extra_width)],
                [(2, cut, model_width - cut)],
            ],
            [
                [(4, 0, hidden_width), (5, 0, hidden_width)],
                [(3, 0, model_width)],
                [(6, 0, hidden_width)],
            ],
        ],
        near_x + near_y,
        ("x",) * 3 + ("y",) * 3,
    )
    summed_one, summed_two = summed_one.astype(full), summed_two.astype(full)

    output = (hidden + shared_result + routed_result).astype(low)

    summed_gate, summed_up, summed_expert_down = [
        sum(part.astype(full) for part in four)
        for four in zip(owns[0], crossed[0], arrived[:3], arrived[3:])
    ]
    summed_expert_in = jnp.stack([summed_gate, summed_up], axis=0)[None]
    summed_expert_down = summed_expert_down[None]

    def take(array, start, width):
        return array[:, start : start + width]

    at = model_width + cut
    summed_value = jnp.concatenate(
        [
            take(summed_one, model_width, cut),
            take(summed_one, at + model_width + extra_width, model_width - cut),
        ],
        axis=1,
    )
    summed_in = jnp.stack(
        [take(summed_one, 0, model_width).T, take(summed_one, at, model_width).T, summed_value.T],
        axis=0,
    )
    at = at + model_width
    summed_router = take(summed_one, at, experts)
    summed_gains = take(summed_one, at + experts, 2).T
    summed_shared_in = jnp.stack(
        [take(summed_two, 0, hidden_width), take(summed_two, hidden_width, hidden_width)], axis=0
    )
    at = 2 * hidden_width
    summed_out = take(summed_two, at, model_width).T
    summed_shared_down = take(summed_two, at + model_width, hidden_width).T
    upd_attn_in = advance(
        attention_in, attention_in_momentum, attention_in_average, summed_in, rate_attention_in
    )
    upd_attn_out = advance(
        attention_out, attention_out_momentum, attention_out_average, summed_out, rate_attention_out
    )
    upd_shared_in = advance(
        shared_in, shared_in_momentum, shared_in_average, summed_shared_in, rate_shared_in
    )
    upd_shared_down = advance(
        shared_down, shared_down_momentum, shared_down_average, summed_shared_down, rate_shared_down
    )
    upd_router = advance(router, router_momentum, router_average, summed_router, rate_router)
    upd_gains = advance(
        norm_gains, norm_gains_momentum, norm_gains_average, summed_gains, rate_gains
    )
    upd_expert_in = advance(
        expert_in, expert_in_momentum, expert_in_average, summed_expert_in, rate_expert_in
    )
    upd_expert_down = advance(
        expert_down, expert_down_momentum, expert_down_average, summed_expert_down, rate_expert_down
    )
    return (
        output,
        input_grad,
        upd_attn_in[0],
        upd_attn_in[1],
        upd_attn_in[2],
        upd_attn_out[0],
        upd_attn_out[1],
        upd_attn_out[2],
        upd_shared_in[0],
        upd_shared_in[1],
        upd_shared_in[2],
        upd_shared_down[0],
        upd_shared_down[1],
        upd_shared_down[2],
        upd_router[0],
        upd_router[1],
        upd_router[2],
        upd_gains[0],
        upd_gains[1],
        upd_gains[2],
        upd_expert_in[0],
        upd_expert_in[1],
        upd_expert_in[2],
        upd_expert_down[0],
        upd_expert_down[1],
        upd_expert_down[2],
    )


def solution(mesh):
    in_specs = (
        P(("dp", "expert"), None),
        P(("dp", "expert")),
        P(("dp", "expert")),
        P(("dp", "expert"), None),
        P(("dp", "expert"), None),
        P(None, None, ("dp", "expert")),
        P(None, None, ("dp", "expert")),
        P(None, None, ("dp", "expert")),
        P(None, ("dp", "expert")),
        P(None, ("dp", "expert")),
        P(None, ("dp", "expert")),
        P(None, ("dp", "expert"), None),
        P(None, ("dp", "expert"), None),
        P(None, ("dp", "expert"), None),
        P(None, ("dp", "expert")),
        P(None, ("dp", "expert")),
        P(None, ("dp", "expert")),
        P(("dp", "expert"), None),
        P(("dp", "expert"), None),
        P(("dp", "expert"), None),
        P(None, ("dp", "expert")),
        P(None, ("dp", "expert")),
        P(None, ("dp", "expert")),
        P("expert", None, "dp", None),
        P("expert", None, "dp", None),
        P("expert", None, "dp", None),
        P("expert", "dp", None),
        P("expert", "dp", None),
        P("expert", "dp", None),
    )
    out_specs = (
        P(("dp", "expert"), None),
        P(("dp", "expert"), None),
        P(None, None, ("dp", "expert")),
        P(None, None, ("dp", "expert")),
        P(None, None, ("dp", "expert")),
        P(None, ("dp", "expert")),
        P(None, ("dp", "expert")),
        P(None, ("dp", "expert")),
        P(None, ("dp", "expert"), None),
        P(None, ("dp", "expert"), None),
        P(None, ("dp", "expert"), None),
        P(None, ("dp", "expert")),
        P(None, ("dp", "expert")),
        P(None, ("dp", "expert")),
        P(("dp", "expert"), None),
        P(("dp", "expert"), None),
        P(("dp", "expert"), None),
        P(None, ("dp", "expert")),
        P(None, ("dp", "expert")),
        P(None, ("dp", "expert")),
        P("expert", None, "dp", None),
        P("expert", None, "dp", None),
        P("expert", None, "dp", None),
        P("expert", "dp", None),
        P("expert", "dp", None),
        P("expert", "dp", None),
    )
    return jax.shard_map(local, mesh=mesh, in_specs=in_specs, out_specs=out_specs, check_vma=False)
```

time: 1160 us -> 841 us (0.72)
  Pallas kernels: 0 us -> 667 us
  waiting for transfers between devices: 475 us -> 0.03 us
  matrix products: 266 us -> 32.2 us
  starting transfers between devices: 131 us -> 5.39 us
  local copies, waits for them, and re-layouts: 161 us -> 47.4 us
  other arithmetic: 99 us -> 63.9 us
    pallas_call x0 -> x10, Pallas kernels: none -> 667 us  [the longest x1 196 us: sum_all(): pl.pallas_call(functools.partial(sum_kernel, line, tuple(kernel_plans), w...]
    ppermute x33 -> x3, waiting for transfers between devices: 247 us -> 0.01 us  [shift(): return lax.ppermute(block, 'expert', pairs)]
    ppermute x62 -> x0, waiting for transfers between devices: 174 us -> none  [the longest x60 174 us: swap(): return lax.ppermute(block, 'expert', pairs)]
    dot_general x32 -> x12, matrix products: 104 us -> 13.2 us  [dot_nn(): lax.dot_general(a, b, (((1,), (0,)), ((), ())), preferred_element_type=jn...]
    ppermute x62 -> x0, starting transfers between devices: 79.2 us -> none  [the longest x60 78.9 us: swap(): return lax.ppermute(block, 'expert', pairs)]
    concatenate x7 -> x1, local copies, waits for them, and re-layouts: 77.1 us -> 0.59 us  [local(): jnp.concatenate([grad_router.astype(low), jnp.stack([grad_gain_one, grad_...]
    dot_general x18 -> x3, matrix products: 77.6 us -> 7.18 us  [dot_tn(): lax.dot_general(a, b, (((0,), (0,)), ((), ())), preferred_element_type=jn...]
    dot_general x19 -> x3, matrix products: 66.9 us -> 6.73 us  [dot_nt(): lax.dot_general(a, b, (((1,), (1,)), ((), ())), preferred_element_type=jn...]
  transfers between devices with their start and end apart: 103 -> 4, of which waited for: 40 -> 0; matrix products, arithmetic and copies ran while one was open for 40% -> 13% of each run, Pallas kernels for 0% -> 63%
where the time goes in v2:
time: 841 us; the launch traced here: 832 us
  Pallas kernels  667 us (79%)
  other arithmetic  63.9 us (8%)
  local copies, waits for them, and re-layouts  47.4 us (6%)
  matrix products  32.2 us (4%)
  between operations  16.1 us (2%)
    pallas_call x1, Pallas kernels, sum_all(): pl.pallas_call(functools.partial(sum_kernel, line, tuple(kernel_plans), w...  196 us
    pallas_call x1, Pallas kernels, first_exchange(): pl.pallas_call(functools.partial(first_kernel, line, plans), out_shape=ou...  146 us
    pallas_call x4, Pallas kernels, run_expert(): pl.pallas_call(functools.partial(expert_kernel, slots=slots, add=bool(bef...  108 us
    pallas_call x1, Pallas kernels, second_exchange(): pl.pallas_call(functools.partial(second_kernel, line), out_shape=out_shap...  97 us
    pallas_call x1, Pallas kernels, third_exchange(): pl.pallas_call(functools.partial(third_kernel, line), out_shape=[shape(gr...  74.1 us
    unnamed x199, local copies, waits for them, and re-layouts  27.8 us
    pallas_call x1, Pallas kernels, attend_back(): pl.pallas_call(attend_back_kernel, grid=(steps,), in_specs=[whole(tokens,...  27.1 us
    pallas_call x1, Pallas kernels, attend(): pl.pallas_call(functools.partial(attend_kernel, steps), grid=(steps,), in...  19 us
  transfers between devices with their start and end apart: 4, of which 0 were waited for; matrix products, arithmetic and copies ran while one was open for 13% of the time, Pallas kernels for 63%

profile of v2, /device:TPU:0, one launch (start us, length us, event | category | flops | bytes accessed | tf_op | source)
XLA Modules:
  0.0 832.3 jit_solution(11777015357593221370)
XLA Ops:
  12.6 2.5 convert.25
  21.4 1.8 concatenate.34.refs_0_
  25.4 146.3 %shard_map.476 = (bf16[2,4,2,2,40,3968]{5,4,3,2,1,0:T(8,128)(2,1)}, bf16[2,4,2,2,40,1280]{5,4,3,2,1,0:T(8,128)(2,1)}, bf16[4,400,1280]{2,1,0:T(8,128)(2,1)}, bf1...) custom-call(bf16[40,3968]{1,0:T(8,128)(2,1)S(1)} %copy-done.3, ...), custom_call_target="tpu_custom_call" | custom-call | tf_op jit(solution)/shard_map/pallas_call | solution.py:292
  176.9 19.0 %shard_map.477 = (bf16[384,1280]{1,0:T(8,128)(2,1)S(1)}, bf16[384,1280]{1,0:T(8,128)(2,1)S(1)}, bf16[384,1280]{1,0:T(8,128)(2,1)S(1)}, bf16[384,1280]{1,0:T(8,12...) custom-call(bf16[384,1280]{1,0:T(8,128)(2,1)} %fusion.17.normed, bf16[1280,3968]{1,0:T(8,128)(2,1)} %bitcast.184, ...), custom_call_target="tpu_custom_call" | custom-call | flops 5033164800 | bytes 32768000 | tf_op jit(solution)/shard_map/pallas_call | solution.py:739
  202.8 97.0 %shard_map.478 = (bf16[4,400,1280]{2,1,0:T(8,128)(2,1)}, bf16[2,640,896]{2,1,0:T(8,128)(2,1)}, bf16[2,640,896]{2,1,0:T(8,128)(2,1)}, bf16[2,640,896]{2,1,0:T(8,1...) custom-call(bf16[400,1280]{1,0:T(8,128)(2,1)} %pad_maximum_fusion.2.refs_0_, ...), custom_call_target="tpu_custom_call" | custom-call | tf_op jit(solution)/shard_map/pallas_call | solution.py:350
  308.5 25.6 %shard_map.479 = (bf16[4,400,1280]{2,1,0:T(8,128)(2,1)}, bf16[4,384,1280]{2,1,0:T(8,128)(2,1)}, bf16[768,1280]{1,0:T(8,128)(2,1)}, bf16[768,896]{1,0:T(8,128)(2,...) custom-call(s32[1]{0:T(128)} %get-tuple-element.370.place, ...), custom_call_target="tpu_custom_call" | custom-call | flops 11827937280 | bytes 31457280 | tf_op jit(solution)/shard_map/pallas_call | solution.py:970
  334.2 27.3 %shard_map.480 = (bf16[4,400,1280]{2,1,0:T(8,128)(2,1)}, bf16[4,384,1280]{2,1,0:T(8,128)(2,1)}, bf16[768,1280]{1,0:T(8,128)(2,1)}, bf16[768,896]{1,0:T(8,128)(2,...) custom-call(s32[1]{0:T(128)} %get-tuple-element.371.place, ...), custom_call_target="tpu_custom_call" | custom-call | flops 11827937280 | bytes 31457280 | tf_op jit(solution)/shard_map/pallas_call | solution.py:970
  361.5 27.6 %shard_map.481 = (bf16[4,400,1280]{2,1,0:T(8,128)(2,1)}, bf16[4,384,1280]{2,1,0:T(8,128)(2,1)}, bf16[768,1280]{1,0:T(8,128)(2,1)}, bf16[768,896]{1,0:T(8,128)(2,...) custom-call(s32[1]{0:T(128)} %get-tuple-element.372.place, ...), custom_call_target="tpu_custom_call" | custom-call | flops 11827937280 | bytes 31457280 | tf_op jit(solution)/shard_map/pallas_call | solution.py:970
  389.1 27.5 %shard_map.482 = (bf16[4,400,1280]{2,1,0:T(8,128)(2,1)}, bf16[4,384,1280]{2,1,0:T(8,128)(2,1)}, bf16[768,1280]{1,0:T(8,128)(2,1)}, bf16[768,896]{1,0:T(8,128)(2,...) custom-call(s32[1]{0:T(128)} %get-tuple-element.373.place, ...), custom_call_target="tpu_custom_call" | custom-call | flops 11827937280 | bytes 31457280 | tf_op jit(solution)/shard_map/pallas_call | solution.py:970
  416.6 74.1 %shard_map.483 = (f32[400,1280]{1,0:T(8,128)}, bf16[640,896]{1,0:T(8,128)(2,1)}, bf16[640,896]{1,0:T(8,128)(2,1)}, bf16[448,1280]{1,0:T(8,128)(2,1)}, bf16[640,8...) custom-call(bf16[4,400,1280]{2,1,0:T(8,128)(2,1)} %get-tuple-element, ...), custom_call_target="tpu_custom_call" | custom-call | tf_op jit(solution)/shard_map/pallas_call | solution.py:481
  490.7 2.9 slice_bitcast_fusion.3
  496.6 2.0 add_convert_fusion
  506.9 1.8 multiply_reduce_fusion.2
  520.0 2.7 fusion.23
  522.7 3.2 collective-permute-start.1
  525.9 3.0 fusion.9
  530.8 1.5 multiply_convert_fusion
  532.3 2.9 convolution_convert_fusion.2
  535.2 2.9 convolution_convert_fusion.1
  540.9 2.7 multiply_reduce_fusion
  543.6 1.9 fusion.87
  546.4 27.1 %shard_map.484 = (bf16[1280,1280]{1,0:T(8,128)(2,1)}, bf16[1280,1280]{1,0:T(8,128)(2,1)}, bf16[1280,1280]{1,0:T(8,128)(2,1)}, bf16[1280,1280]{1,0:T(8,128)(2,1)}, f32[384,1280]{1,0:T(8,128)}) custom-call(bf16[384,1280]{1,0:T(8,128)(2,1)S(1)} %get-tuple-element.336.grad_branch, bf16[384,1280]{1,0:T(8,128)(2,1)S(1)} %copy-done.1, ...), custom_call_target="tpu_custom_call" | custom-call | flops 10066329600 | bytes 65536000 | tf_op jit(solution)/shard_map/pallas_call | solution.py:833
  573.5 2.1 fusion.22
  578.9 3.2 copy.129
  582.2 2.2 maximum_maximum_fusion
  584.4 195.8 %shard_map.485 = (bf16[40,3968]{1,0:T(8,128)(2,1)}, bf16[40,3968]{1,0:T(8,128)(2,1)}, bf16[640,896]{1,0:T(8,128)(2,1)}, bf16[640,896]{1,0:T(8,128)(2,1)}, bf16[4...) custom-call(bf16[2,4,2,2,40,1280]{5,4,3,2,1,0:T(8,128)(2,1)} %bitcast.197,, ...), custom_call_target="tpu_custom_call" | custom-call | tf_op jit(solution)/shard_map/pallas_call | solution.py:654
  786.6 1.8 fusion.19
  791.9 1.9 add_bitcast_fusion
  798.7 4.0 multiply_add_fusion.2
  802.7 4.3 convolution_add_fusion.2
  811.0 10.7 %multiply_add_fusion = (f32[1,2,640,896]{3,2,1,0:T(8,128)}, f32[1,2,640,896]{3,2,1,0:T(8,128)}, f32[1,2,640,896]{3,2,1,0:T(8,128)}) fusion(f32[1,2,640,896]{3,2,1,0:T(8,128)} %param.54, f32[1,2,640,896]{3,2,1,0:T(8,128)} %param.52, f32[1,640,896]{2,1,0:T(8,128)} %add_bitcast_fusion, f32[1,640,896]{2,1,0:T(8,128)S(1)} %add_bitcast_fusion.1, ...), kind=kLoop, calls=%fused_computation.1 | loop fusion | flops 11468800 | bytes 32112640 | tf_op jit(solution)/shard_map/add | solution.py:55
  821.8 3.2 fusion.26
  (300 shorter events, 83.7 us)
Async XLA Ops:
  7.2 518.7 %all-gather.2.cloned.1.call-start = ((), (), s32[]{:S(2)}) async-start(), calls=%async_computation | async-start | bytes 7096320 | tf_op jit(solution)/shard_map/all_gather | solution.py:1160
  12.0 6.9 copy-start.76
  16.8 6.4 copy-start
  176.9 22.8 %copy-start.77 = (pred[16,384]{1,0:T(8,128)(4,1)S(1)}, pred[16,384]{1,0:T(8,128)(4,1)}, u32[]{:S(2)}) copy-start(pred[16,384]{1,0:T(8,128)(4,1)} %copy-done.76) | copy-start | bytes 18436
  176.9 24.2 %copy-start.87 = (pred[384]{0:T(512)(128)(4,1)S(1)}, pred[384]{0:T(512)(128)(4,1)}, u32[]{:S(2)}) copy-start(pred[384]{0:T(512)(128)(4,1)} %copy-done.86) | copy-start | bytes 1156
  201.1 98.7 %copy-start.78 = (f32[384]{0:T(512)}, f32[384]{0:T(512)S(1)}, u32[]{:S(2)}) copy-start(f32[384]{0:T(512)S(1)} %fusion.60) | copy-start | bytes 4612
  490.7 5.1 copy-start.80
  490.7 5.2 copy-start.91
  493.6 26.4 %collective-permute-start = (bf16[384,1280]{1,0:T(8,128)(2,1)}, bf16[384,1280]{1,0:T(8,128)(2,1)}, u32[]{:S(2)}, u32[]{:S(2)}) collective-permute-start(bf16[384,1280]{1,0:T(8,128)(2,1)} %get-tuple-element.338), channel_id=1, source_target_pairs={{0,12},{1,13},{2,14},{3,15},{4,0},{5,1},{6,2},{7,3},{8,4},{9,5},{1... | collective-permute-start | bytes 2949128 | tf_op jit(solution)/shard_map/ppermute | solution.py:1040
  495.0 326.7 %collective-permute-start.2 = (bf16[384,1280]{1,0:T(8,128)(2,1)}, bf16[384,1280]{1,0:T(8,128)(2,1)}, u32[]{:S(2)}, u32[]{:S(2)}) collective-permute-start(bf16[384,1280]{1,0:T(8,128)(2,1)} %get-tuple-element.339), channel_id=1, source_target_pairs={{0,4},{1,5},{2,6},{3,7},{4,8},{5,9},{6,10},{7,11},{8,12},{9,13},{1... | collective-permute-start | bytes 2949128 | tf_op jit(solution)/shard_map/ppermute | solution.py:1040
  500.7 4.2 copy-start.90
  500.7 4.9 copy-start.92
  522.7 299.0 %collective-permute-start.1 = (bf16[384,1280]{1,0:T(8,128)(2,1)}, bf16[384,1280]{1,0:T(8,128)(2,1)}, u32[]{:S(2)}, u32[]{:S(2)}) collective-permute-start(bf16[384,1280]{1,0:T(8,128)(2,1)} %fusion.23), channel_id=1, source_target_pairs={{0,12},{1,13},{2,14},{3,15},{4,0},{5,1},{6,2},{7,3},{8,4},{9,5},{1... | collective-permute-start | bytes 2949128 | tf_op jit(solution)/shard_map/ppermute | solution.py:1040
  532.3 45.2 %copy-start.57 = (bf16[384,896]{1,0:T(8,128)(2,1)}, bf16[384,896]{1,0:T(8,128)(2,1)S(1)}, u32[]{:S(2)}) copy-start(bf16[384,896]{1,0:T(8,128)(2,1)S(1)} %get-tuple-element.342) | copy-start | bytes 2064388
  546.4 27.1 %copy-start.14 = (bf16[384,1280]{1,0:T(8,128)(2,1)S(1)}, bf16[384,1280]{1,0:T(8,128)(2,1)}, u32[]{:S(2)}) copy-start(bf16[384,1280]{1,0:T(8,128)(2,1)} %inputs.1) | copy-start | bytes 2949124
  546.4 27.1 %copy-start.82 = (f32[384]{0:T(512)S(1)}, f32[384]{0:T(512)}, u32[]{:S(2)}) copy-start(f32[384]{0:T(512)} %copy-done.81) | copy-start | bytes 4612
  780.2 4.0 copy-start.56
  780.2 4.0 copy-start.67
  780.2 4.0 copy-start.68
  789.6 4.2 copy-start.54
  789.6 4.2 copy-start.65
  789.7 4.2 copy-start.66
  789.7 5.2 copy-start.60
  791.9 5.7 copy-start.27
  791.9 5.7 copy-start.29
  791.9 5.7 copy-start.30
  791.9 5.7 copy-start.31
  791.9 5.7 copy-start.32
  802.7 4.3 copy-start.73
  802.7 4.3 copy-start.74
  802.7 4.3 copy-start.75
  811.0 10.8 %copy-start.19 = (f32[384,1280]{1,0:T(8,128)S(1)}, f32[384,1280]{1,0:T(8,128)}, u32[]{:S(2)}) copy-start(f32[384,1280]{1,0:T(8,128)} %convolution_add_fusion.2) | copy-start | bytes 5898244
  (67 other events, 137.8 us)
Sparse Core Ops, SparseCore 0:
  171.9 107.4 all-gather.1

commit v3 on v2

--- a/solution.py
+++ b/solution.py
@@ -138,7 +138,7 @@
             copy.wait()
 
 
-def in_turn(chains):
+def in_steps(chains):
     while chains:
         left = []
         for chain in chains:
@@ -148,38 +148,25 @@
             except StopIteration:
                 pass
         chains = left
-
-
-def line_chain(moves, own, whole):
-    line = moves.spot.line
-    half, rest = line // 2, (line - 1) // 2
-    moves.keep(own, whole.at[0], later=True)
-    up, down = own, own
-    for i in range(1, half + 1):
-        rising = moves.start(up, whole.at[i], "up")
-        if i <= rest:
-            falling = moves.start(down, whole.at[line - i], "down")
         yield
-        rising.wait()
-        up = whole.at[i]
-        if i <= rest:
-            falling.wait()
-            down = whole.at[line - i]
-
-
-def swap_chain(moves, own, whole, way):
-    core = moves.spot.core
-    copy = moves.start(own, whole.at[core], way)
+
+
+def in_turn(chains):
+    for _ in in_steps(chains):
+        pass
+
+
+def place_chain(moves, source, buffer, target):
+    copy = moves.keep(source, buffer)
     yield
     copy.wait()
-    moves.start(whole.at[core], whole.at[core], "core", later=True)
-
-
-def core_chain(moves, own, whole):
+    moves.keep(buffer, target, later=True)
+
+
+def core_chain(moves, own, whole, buffer):
     core = moves.spot.core
-    moves.keep(own, whole.at[core], later=True)
     moves.start(own, whole.at[core], "core", later=True)
-    yield
+    return place_chain(moves, own, buffer, whole.at[core])
 
 
 def dense_chain(moves, whole, columns, order):
@@ -228,11 +215,8 @@
 
 def first_kernel(line, plans, *refs):
     count = len(plans)
-    shards, refs = refs[:count], refs[count:]
-    grads, gate, up, down = refs[:4]
-    results, refs = refs[4 : 4 + count], refs[4 + count :]
-    line_grads, gates, ups, downs = refs[0], refs[1:4], refs[4:5], refs[5:8]
-    refs = refs[8:]
+    shards, down, refs = refs[:count], refs[count], refs[count + 1 :]
+    results, over_x, over_y, refs = refs[:count], refs[count], refs[count + 1], refs[count + 2 :]
     wholes, refs = refs[:count], refs[count:]
     spot = Spot(line)
     meet(spot)
@@ -250,13 +234,12 @@
             columns = slice(start, start + width)
             chains.append(dense_chain(moves, wholes[n], columns, ORDERS[order]))
             start += width
-    chains.append(line_chain(moves, grads, line_grads))
-    for own, whole in ((gate, gates), (down, downs)):
-        chains.append(swap_chain(moves, own, whole[1], "x"))
-        chains.append(swap_chain(moves, own, whole[2], "y"))
-    for own, whole in ((gate, gates), (up, ups), (down, downs)):
-        chains.append(core_chain(moves, own, whole[0]))
-    in_turn(chains)
+    stages = 0
+    for _ in in_steps(chains):
+        stages += 1
+        if stages == 1:
+            moves.start(down, over_x, "x", later=True)
+            moves.start(down, over_y, "y", later=True)
     moves.finish()
     stores = [moves.keep(wholes[n], results[n]) for n in range(count)]
     for copy in stores:
@@ -279,134 +262,113 @@
     return jax.ShapeDtypeStruct((2,) + array.shape, array.dtype)
 
 
-def first_exchange(experts, shards, plans, grads, gate, up, down):
+def first_exchange(experts, shards, plans, down):
     line = experts // PLANE
     count = len(shards)
-    chains = sum(len(plan) for plan in plans)
-    remote = chains * (2 * line + 3) + line + 4 * 2 + 3
-    out_shape = [
-        jax.ShapeDtypeStruct((2, line, 2, 2) + shard.shape, shard.dtype) for shard in shards
-    ]
-    out_shape += [jax.ShapeDtypeStruct((line,) + grads.shape, grads.dtype)]
-    out_shape += [both_halves(gate)] * 3 + [both_halves(up)] + [both_halves(down)] * 3
+    remote = sum(len(plan) for plan in plans) * (2 * line + 3) + 2
     out = pl.pallas_call(
         functools.partial(first_kernel, line, plans),
-        out_shape=out_shape,
-        in_specs=hbm(count + 4),
-        out_specs=hbm(count + 8),
+        out_shape=[
+            jax.ShapeDtypeStruct((2, line, 2, 2) + shard.shape, shard.dtype) for shard in shards
+        ]
+        + [jax.ShapeDtypeStruct(down.shape, down.dtype)] * 2,
+        in_specs=hbm(count + 1),
+        out_specs=hbm(count + 2),
         scratch_shapes=[
             pltpu.VMEM((2, line, 2, 2) + shard.shape, shard.dtype) for shard in shards
         ]
-        + semaphores(remote, 2 * count + 4),
+        + semaphores(remote, 2 * count),
         compiler_params=pltpu.CompilerParams(
-            collective_id=1, has_side_effects=True, vmem_limit_bytes=48 * 1024 * 1024
+            collective_id=1, has_side_effects=True, vmem_limit_bytes=60 * 1024 * 1024
         ),
-    )(*shards, grads, gate, up, down)
-    return out[:count], out[count], out[count + 1 : count + 4], out[count + 4], out[count + 5 :]
+    )(*shards, down)
+    return out[:count], out[count], out[count + 1]
 
 
 def second_kernel(line, *refs):
-    rows, up, gate_x, down_x, down_y = refs[:5]
-    line_rows, up_x, up_y, far_gate, far_up, far_down = refs[5:11]
+    rows, pairs, downs, refs = refs[0], refs[1:4], refs[4:7], refs[7:]
+    rising, falling, wholes, refs = refs[0], refs[1], refs[2:5], refs[5:]
+    buffers, refs = refs[:9], refs[9:]
     spot = Spot(line)
     meet(spot)
-    moves = Moves(spot, *refs[11:])
+    moves = Moves(spot, *refs)
     core = spot.core
-    half = down_x.shape[1] // 2
-
-    def far_up_chain():
-        yield
-        copy = moves.start(up_y.at[core], far_up.at[core], "x")
+    gate, up, down = wholes
+    (_, pair_x, pair_y), (_, down_x, down_y) = pairs, downs
+    half = down_x.shape[0] // 2
+
+    def far_chain(source, target, way):
+        copy = moves.start(source, target, way)
         yield
         copy.wait()
-        moves.start(far_up.at[core], far_up.at[core], "core", later=True)
-
-    def part_chain(source, whole, part, way):
-        copy = moves.start(source.at[core, part], whole.at[core, part], way)
-        yield
-        copy.wait()
-        moves.start(whole.at[core, part], whole.at[core, part], "core", later=True)
-
-    everything = slice(None)
+        moves.start(target, target, "core", later=True)
+
+    moves.start(rows, rising, "up", later=True)
+    moves.start(rows, falling, "down", later=True)
+    upper, lower = pl.ds(0, half), pl.ds(half, half)
     in_turn(
         [
-            swap_chain(moves, up, up_x, "x"),
-            swap_chain(moves, up, up_y, "y"),
-            line_chain(moves, rows, line_rows),
-            far_up_chain(),
-            part_chain(down_y, far_down, slice(half, 2 * half), "x"),
-            part_chain(down_x, far_down, slice(0, half), "y"),
-            part_chain(gate_x, far_gate, everything, "y"),
+            far_chain(pair_y.at[1], up.at[3, core], "x"),
+            far_chain(pair_x.at[0], gate.at[3, core], "y"),
+            far_chain(down_y.at[lower], down.at[3, core, lower], "x"),
+            far_chain(down_x.at[upper], down.at[3, core, upper], "y"),
         ]
+        + [
+            core_chain(moves, half_of, wholes[i].at[q], buffers[3 * q + i])
+            for q in range(3)
+            for i, half_of in enumerate((pairs[q].at[0], pairs[q].at[1], downs[q]))
+        ]
     )
     moves.finish()
 
 
-def second_exchange(experts, rows, up, gate_x, down_x, down_y):
+def second_exchange(experts, rows, pairs, downs):
     line = experts // PLANE
-    out_shape = [jax.ShapeDtypeStruct((line,) + rows.shape, rows.dtype)]
-    out_shape += [both_halves(up)] * 2
-    out_shape += [jax.ShapeDtypeStruct(array.shape, array.dtype) for array in (gate_x, gate_x, down_x)]
+    low = rows.dtype
+    shapes = [pairs[0].shape[1:]] * 2 + [downs[0].shape]
     return pl.pallas_call(
         functools.partial(second_kernel, line),
-        out_shape=out_shape,
-        in_specs=hbm(5),
-        out_specs=hbm(6),
-        scratch_shapes=semaphores(line + 12, 1),
-        compiler_params=pltpu.CompilerParams(collective_id=3, has_side_effects=True),
-    )(rows, up, gate_x, down_x, down_y)
-
-
-def third_kernel(line, *refs):
+        out_shape=[jax.ShapeDtypeStruct(rows.shape, low)] * 2
+        + [jax.ShapeDtypeStruct((PLANE, 2) + shape, low) for shape in shapes],
+        in_specs=hbm(7),
+        out_specs=hbm(5),
+        scratch_shapes=[pltpu.VMEM(shape, low) for shape in shapes * 3] + semaphores(19, 18),
+        compiler_params=pltpu.CompilerParams(
+            collective_id=3, has_side_effects=True, vmem_limit_bytes=60 * 1024 * 1024
+        ),
+    )(rows, *pairs, *downs)
+
+
+def third_kernel(line, groups, *refs):
     low, full = jnp.bfloat16, jnp.float32
-    grads = refs[0]
-    kept = [refs[1 + 5 * q : 6 + 5 * q] for q in range(PLANE)]
-    refs = refs[1 + 5 * PLANE :]
-    total = refs[0]
-    owns = [refs[1 + 3 * q : 4 + 3 * q] for q in range(PLANE - 1)]
-    refs = refs[1 + 3 * (PLANE - 1) :]
+    kept = [refs[5 * r : 5 * r + 5] for r in range(groups)]
+    refs = refs[5 * groups :]
+    owns = [refs[3 * q : 3 + 3 * q] for q in range(PLANE - 1)]
+    refs = refs[3 * (PLANE - 1) :]
     crossed = [refs[3 * q : 3 + 3 * q] for q in range(PLANE - 1)]
     refs = refs[3 * (PLANE - 1) :]
     far_in, refs = refs[:4], refs[4:]
-    boxes, extra, refs = refs[0], refs[1:3], refs[3:]
     loaded, refs = [refs[:5], refs[5:10]], refs[10:]
     results, refs = [refs[:6], refs[6:12]], refs[12:]
-    far_box, down_grad, total_box, refs = refs[:3], refs[3], refs[4], refs[5:]
+    far_box, down_grad, refs = refs[:3], refs[3], refs[4:]
     spot = Spot(line)
     meet(spot)
     moves = Moves(spot, *refs)
-    half, rest = line // 2, (line - 1) // 2
     order = (3, 1, 2, 0)
+    slots = kept[0][0].shape[1]
     loads = {}
 
     def load(n):
-        loads[n] = [moves.keep(kept[order[n]][i], loaded[n % 2][i]) for i in range(5)]
+        loads[n] = [
+            moves.keep(kept[r][i].at[order[n]], loaded[n % 2][i].at[pl.ds(r * slots, slots)])
+            for r in range(groups)
+            for i in range(5)
+        ]
 
     def add(target, source):
         target[...] = (target[...].astype(full) + source[...].astype(full)).astype(low)
 
-    def sums(way, sign, steps):
-        at = lambda i: i if sign > 0 else (line - i) % line
-        source = grads.at[at(steps)]
-        box = extra[0 if sign > 0 else 1]
-        for i in range(steps, 0, -1):
-            copy = moves.start(source, boxes.at[at(i) - 1], way)
-            if i > 1:
-                part = moves.keep(grads.at[at(i - 1)], box)
-            yield
-            copy.wait()
-            source = boxes.at[at(i) - 1]
-            if i > 1:
-                part.wait()
-                add(source, box)
-            else:
-                total_box[...] += source[...].astype(full)
-
-    own_part = moves.keep(grads.at[0], extra[0])
     load(0)
-    own_part.wait()
-    total_box[...] = extra[0][...].astype(full)
-
     rows_half = results[0][0].shape[0]
     down_half = results[0][2].shape[0]
     sent = {}
@@ -432,9 +394,7 @@
             q = order[n]
             targets = far_box if q == PLANE - 1 else crossed[q]
             if which:
-                sent[n] = [
-                    moves.start(buffers[3 + i], targets[i], "core") for i in range(3)
-                ]
+                sent[n] = [moves.start(buffers[3 + i], targets[i], "core") for i in range(3)]
             elif q < PLANE - 1:
                 sent[n] += [moves.keep(buffers[i], owns[q][i]) for i in range(3)]
 
@@ -450,56 +410,46 @@
         moves.start(far_box[2].at[pl.ds(0, edge)], far_in[2], "y", later=True)
         moves.start(far_box[2].at[pl.ds(edge, edge)], far_in[3], "x", later=True)
 
-    chains = [sums("down", 1, half), sums("up", -1, rest)]
-    for chain in chains:
-        next(chain, None)
     weights(0)
     weights(1)
     far()
     weights(2)
-    for chain in chains:
-        next(chain, None)
     weights(3)
-    in_turn(chains)
-    store = moves.keep(total_box, total)
     for n in (2, 3):
         for copy in sent[n]:
             copy.wait()
-    store.wait()
     moves.finish()
 
 
-def third_exchange(experts, grads, kept):
+def third_exchange(experts, kept):
     line = experts // PLANE
     low = jnp.bfloat16
     rows, inner = kept[0][0], kept[0][1]
-    width, hidden_width = rows.shape[1], inner.shape[1]
+    slots, width, hidden_width = rows.shape[1], rows.shape[2], inner.shape[2]
     half, down_half = width // 2, hidden_width // 2
     pieces = [(half, hidden_width), (half, hidden_width), (down_half, width)]
     far = pieces[:2] + [(down_half // 2, width)] * 2
-    shape = lambda size, dtype=low: jax.ShapeDtypeStruct(size, dtype)
     out = pl.pallas_call(
-        functools.partial(third_kernel, line),
-        out_shape=[shape(grads.shape[1:], jnp.float32)]
-        + [shape(size) for size in pieces * (2 * (PLANE - 1))]
-        + [shape(size) for size in far],
-        in_specs=hbm(1 + 5 * PLANE),
-        out_specs=hbm(1 + 6 * (PLANE - 1) + 4),
-        scratch_shapes=[pltpu.VMEM((line - 1,) + grads.shape[1:], low)]
-        + [pltpu.VMEM(grads.shape[1:], low)] * 2
-        + [pltpu.VMEM(array.shape, low) for array in kept[0]] * 2
+        functools.partial(third_kernel, line, len(kept)),
+        out_shape=[
+            jax.ShapeDtypeStruct(size, low) for size in pieces * (2 * (PLANE - 1)) + far
+        ],
+        in_specs=hbm(5 * len(kept)),
+        out_specs=hbm(6 * (PLANE - 1) + 4),
+        scratch_shapes=[
+            pltpu.VMEM((len(kept) * slots, array.shape[2]), low) for array in list(kept[0]) * 2
+        ]
         + [pltpu.VMEM(size, low) for size in pieces * 4]
         + [pltpu.VMEM(size, low) for size in pieces]
-        + [pltpu.VMEM((hidden_width, width), low), pltpu.VMEM(grads.shape[1:], jnp.float32)]
-        + semaphores(line + 3 * PLANE + 4, line + 8 * PLANE + 2),
+        + [pltpu.VMEM((hidden_width, width), low)]
+        + semaphores(3 * PLANE + 4, 5 * PLANE * len(kept) + 3 * PLANE),
         compiler_params=pltpu.CompilerParams(
             collective_id=4, has_side_effects=True, vmem_limit_bytes=62 * 1024 * 1024
         ),
-    )(grads, *[array for parts in kept for array in parts])
-    total, out = out[0], out[1:]
+    )(*[array for parts in kept for array in parts])
     count = 3 * (PLANE - 1)
     triples = lambda arrays: [arrays[3 * q : 3 * q + 3] for q in range(PLANE - 1)]
-    return total, triples(out[:count]), triples(out[count : 2 * count]), out[2 * count :]
+    return triples(out[:count]), triples(out[count : 2 * count]), out[2 * count :]
 
 
 def sum_kernel(line, plans, ways, *refs):
@@ -868,137 +818,120 @@
     )
 
 
-def expert_kernel(
-    place,
-    rows_in,
-    grads_in,
-    slots_in,
-    gates_in,
-    gate_weight,
-    up_weight,
-    down_weight,
-    *refs,
-    slots,
-    add,
-):
-    if add:
-        grad_before, result_before, *refs = refs
-    (
-        grad_total,
-        result_total,
-        rows_out,
-        inner_out,
-        gated_out,
-        grad_gate_out,
-        grad_up_out,
-    ) = refs
+def expert_kernel(count, numbers, *refs):
     low, full = jnp.bfloat16, jnp.float32
-    group, tokens = slots_in.shape[0], slots_in.shape[2]
-    width = rows_in.shape[2]
-
+    rows_in, grads_in, slots_in, gates_in = [refs[i * count : (i + 1) * count] for i in range(4)]
+    gate_weight, up_weight, down_weight, *refs = refs[4 * count :]
+    grad_total, result_total = refs[:count], refs[count : 2 * count]
+    rows_out, inner_out, gated_out, grad_gate_out, grad_up_out = refs[2 * count : 2 * count + 5]
+    hot_all, grad_all, result_all, word_sums = refs[2 * count + 5 :]
+    tokens, width = slots_in[0].shape[2], rows_in[0].shape[1]
+    slots = rows_out.shape[1] // count
+    experts = word_sums.shape[1]
+    q = pl.program_id(0)
     slot_ids = lax.broadcasted_iota(jnp.int32, (slots, tokens), 0).astype(full)
-    places = [slots_in[r] == slot_ids for r in range(group)]
-    hot = [here.astype(low) for here in places]
-    gate_col = jnp.concatenate(
-        [
-            jnp.sum(jnp.where(places[r], gates_in[r], 0.0), axis=1, keepdims=True)
-            for r in range(group)
-        ],
-        axis=0,
-    )
-    for r in range(group):
-        rows_out[r * slots : (r + 1) * slots, :] = dot_nn(hot[r], rows_in[r, :tokens]).astype(low)
-    grad_rows = jnp.concatenate(
-        [dot_nn(hot[r], grads_in[r, :tokens]) for r in range(group)], axis=0
-    )
+    parts = [slice(r * slots, (r + 1) * slots) for r in range(count)]
+    here = pl.ds(pl.multiple_of(q * slots, slots), slots)
+    places, gate_cols, grad_parts = [], [], []
+    for r in range(count):
+        place = slots_in[r][0] == slot_ids
+        hot = place.astype(low)
+        hot_all[r, here] = hot
+        places.append(place)
+        gate_cols.append(jnp.sum(jnp.where(place, gates_in[r][0], 0.0), axis=1, keepdims=True))
+        rows_out[0, parts[r]] = dot_nn(hot, rows_in[r][:tokens]).astype(low)
+        grad_parts.append(dot_nn(hot, grads_in[r][:tokens]))
+    gate_col = jnp.concatenate(gate_cols, axis=0)
+    grad_rows = jnp.concatenate(grad_parts, axis=0)
+    rows = rows_out[0]
     gated = (grad_rows * gate_col).astype(low)
-    gated_out[...] = gated
-    rows = rows_out[...]
-    gate_rows = dot_nn(rows, gate_weight[...])
-    up_rows = dot_nn(rows, up_weight[...])
+    gated_out[0] = gated
+    gate_rows = dot_nn(rows, gate_weight[0])
+    up_rows = dot_nn(rows, up_weight[0])
     logistic = jax.nn.sigmoid(gate_rows)
     silu_rows = gate_rows * logistic
     slope_rows = logistic * (1.0 + gate_rows * (1.0 - logistic))
     inner = (silu_rows * up_rows).astype(low)
-    inner_out[...] = inner
-    grad_inner = dot_nt(gated, down_weight[...])
+    inner_out[0] = inner
+    grad_inner = dot_nt(gated, down_weight[0])
     grad_gate_rows = (grad_inner * up_rows * slope_rows).astype(low)
     grad_up_rows = (grad_inner * silu_rows).astype(low)
-    grad_gate_out[...] = grad_gate_rows
-    grad_up_out[...] = grad_up_rows
+    grad_gate_out[0] = grad_gate_rows
+    grad_up_out[0] = grad_up_rows
     sent_grads = (
-        dot_nt(grad_gate_rows, gate_weight[...]) + dot_nt(grad_up_rows, up_weight[...])
+        dot_nt(grad_gate_rows, gate_weight[0]) + dot_nt(grad_up_rows, up_weight[0])
     ).astype(low)
-    result_rows = dot_nn(inner, down_weight[...])
+    result_rows = dot_nn(inner, down_weight[0])
     gate_grad = jnp.sum(result_rows * grad_rows, axis=1, keepdims=True)
     sent_results = (result_rows * gate_col).astype(low)
-    experts = grad_total.shape[1] - tokens
-    for r in range(group):
-        part = slice(r * slots, (r + 1) * slots)
-        grad_sum = dot_tn(hot[r], sent_grads[part])
-        result_sum = dot_tn(hot[r], sent_results[part])
-        token_grad = jnp.sum(jnp.where(places[r], gate_grad[part], 0.0), axis=0, keepdims=True)
+    expert_ids = lax.broadcasted_iota(jnp.int32, (experts, width), 0)
+
+    @pl.when(q == 0)
+    def _():
+        word_sums[...] = jnp.zeros_like(word_sums)
+
+    for r in range(count):
+        grad_all[r, here] = sent_grads[parts[r]]
+        result_all[r, here] = sent_results[parts[r]]
+        token_grad = jnp.sum(
+            jnp.where(places[r], gate_grad[parts[r]], 0.0), axis=0, keepdims=True
+        )
         words = jnp.concatenate(
-            split_words(token_grad) + [jnp.zeros((1, width - 3 * tokens), low)], axis=1
+            [word.astype(full) for word in split_words(token_grad)]
+            + [jnp.zeros((1, width - 3 * tokens), full)],
+            axis=1,
         )
-        expert_ids = lax.broadcasted_iota(jnp.int32, (experts, width), 0)
-        words = jnp.where(expert_ids == place[0], words.astype(full), 0.0)
-        if add:
-            grad_sum = grad_sum + grad_before[r, :tokens].astype(full)
-            result_sum = result_sum + result_before[r].astype(full)
-            words = words + grad_before[r, tokens:].astype(full)
-        grad_total[r, :tokens] = grad_sum.astype(low)
-        grad_total[r, tokens:] = words.astype(low)
-        result_total[r] = result_sum.astype(low)
-
-
-def run_expert(place, rows, grads, slot_rows, gate_rows, weights, before, slots):
-    line, _, width = rows.shape
-    tokens = slot_rows.shape[2]
+        word_sums[r] += jnp.where(expert_ids == numbers[q], words, 0.0)
+
+    @pl.when(q == PLANE - 1)
+    def _():
+        for r in range(count):
+            grad_total[r][:tokens] = dot_tn(hot_all[r], grad_all[r]).astype(low)
+            grad_total[r][tokens:] = word_sums[r].astype(low)
+            result_total[r][...] = dot_tn(hot_all[r], result_all[r]).astype(low)
+
+
+def run_experts(numbers, rows, grads, slot_rows, gate_rows, weights, slots):
+    count = len(rows)
+    extended, width = rows[0].shape
+    tokens = slot_rows[0].shape[2]
     low = jnp.bfloat16
-    hidden_width = weights[0].shape[1]
-    group = 2
-    steps = line // group
-    whole = lambda array: pl.BlockSpec(
-        array.shape, lambda i, place: (0,) * array.ndim, pipeline_mode=pl.Buffered(1)
-    )
-    per_line = lambda size: pl.BlockSpec((group, size, width), lambda i, place: (i, 0, 0))
-    per_token = pl.BlockSpec((group, 1, tokens), lambda i, place: (i, 0, 0))
-    per_row = lambda size: pl.BlockSpec((group * slots, size), lambda i, place: (i, 0))
-    count = line * slots
-    extended = rows.shape[1]
-    return pl.pallas_call(
-        functools.partial(expert_kernel, slots=slots, add=bool(before)),
+    hidden_width = weights[0].shape[2]
+    whole = lambda *shape: pl.BlockSpec(shape, lambda q, numbers: (0,) * len(shape))
+    each = lambda *shape: pl.BlockSpec((1,) + shape, lambda q, numbers: (q, 0, 0))
+    sizes = (width, hidden_width, width, hidden_width, hidden_width)
+    out = pl.pallas_call(
+        functools.partial(expert_kernel, count),
         grid_spec=pltpu.PrefetchScalarGridSpec(
             num_scalar_prefetch=1,
-            grid=(steps,),
-            in_specs=[per_line(extended), per_line(extended), per_token, per_token]
-            + [whole(array) for array in weights]
-            + [per_line(extended), per_line(tokens)][: len(before)],
-            out_specs=[per_line(extended), per_line(tokens)]
-            + [
-                per_row(width),
-                per_row(hidden_width),
-                per_row(width),
-                per_row(hidden_width),
-                per_row(hidden_width),
+            grid=(PLANE,),
+            in_specs=[whole(extended, width)] * (2 * count)
+            + [each(1, tokens)] * (2 * count)
+            + [each(*array.shape[1:]) for array in weights],
+            out_specs=[whole(extended, width)] * count
+            + [whole(tokens, width)] * count
+            + [each(count * slots, size) for size in sizes],
+            scratch_shapes=[
+                pltpu.VMEM((count, PLANE * slots, tokens), low),
+                pltpu.VMEM((count, PLANE * slots, width), low),
+                pltpu.VMEM((count, PLANE * slots, width), low),
+                pltpu.VMEM((count, extended - tokens, width), jnp.float32),
             ],
         ),
-        out_shape=[jax.ShapeDtypeStruct((line, size, width), low) for size in (extended, tokens)]
-        + [
-            jax.ShapeDtypeStruct((count, size), low)
-            for size in (width, hidden_width, width, hidden_width, hidden_width)
-        ],
+        out_shape=[jax.ShapeDtypeStruct((extended, width), low)] * count
+        + [jax.ShapeDtypeStruct((tokens, width), low)] * count
+        + [jax.ShapeDtypeStruct((PLANE, count * slots, size), low) for size in sizes],
         compiler_params=pltpu.CompilerParams(vmem_limit_bytes=62 * 1024 * 1024),
         cost_estimate=pl.CostEstimate(
-            flops=10 * count * width * hidden_width + 8 * line * slots * tokens * width,
-            bytes_accessed=16 * line * tokens * width,
+            flops=count * PLANE * slots * width * (10 * hidden_width + 8 * tokens),
+            bytes_accessed=6 * PLANE * width * hidden_width,
             transcendentals=0,
         ),
-    )(place, rows, grads, slot_rows, gate_rows, *weights, *before)
-
-
-FIRST_ORDERS = (2, 3, 2, 3)
+    )(numbers, *rows, *grads, *slot_rows, *gate_rows, *weights)
+    return out[:count], out[count : 2 * count], out[2 * count :]
+
+
+FIRST_ORDERS = (0, 1, 2, 0, 1, 2)
 
 
 def gather_plan(units, orders):
@@ -1039,22 +972,21 @@
         ]
         return lax.ppermute(block, "expert", pairs)
 
-    def line_sum(self, parts):
+    def swap(self, block, flip):
+        pairs = [(i, (i // PLANE) * PLANE + ((i % PLANE) ^ flip)) for i in range(self.experts)]
+        return lax.ppermute(block, "expert", pairs)
+
+    def line_gather(self, block, rising=None, falling=None):
         half, rest = self.line // 2, (self.line - 1) // 2
-        low = parts[half]
-        for i in range(half, 0, -1):
-            low = self.shift(low, -1)
-            if i > 1:
-                low = add_low(parts[i - 1], low)
-        total = parts[0].astype(jnp.float32) + low.astype(jnp.float32)
+        rising = self.shift(block, 1) if rising is None else rising
+        found = [block, rising] + [None] * (self.line - 2)
+        for i in range(2, half + 1):
+            found[i] = self.shift(found[i - 1], 1)
         if rest:
-            high = parts[self.line - rest]
-            for i in range(rest, 0, -1):
-                high = self.shift(high, 1)
-                if i > 1:
-                    high = add_low(parts[self.line - i + 1], high)
-            total = total + high.astype(jnp.float32)
-        return total
+            found[-1] = self.shift(block, -1) if falling is None else falling
+            for i in range(2, rest + 1):
+                found[-i] = self.shift(found[1 - i], -1)
+        return found
 
 
 def local(
@@ -1129,37 +1061,26 @@
     def widen(rows):
         return jnp.pad(rows, ((0, 0), (0, model_width - rows.shape[1])))
 
-    gate, up, down = (
-        expert_in[0, 0].astype(low),
-        expert_in[0, 1].astype(low),
-        expert_down[0].astype(low),
-    )
+    pair, down = expert_in[0].astype(low), expert_down[0].astype(low)
     plans = (
         gather_plan(pack_one.shape[1] // 128, FIRST_ORDERS),
         gather_plan(model_width // 128, FIRST_ORDERS),
     )
-    (all_one, turned_out), line_grads, gates, up_own, downs = first_exchange(
-        experts,
-        [pack_one, pack_out],
-        plans,
-        jnp.concatenate([cotangent, widen(slot_of.astype(low))], axis=0),
-        gate,
-        up,
-        down,
-    )
-    slot_rows = jnp.stack(
-        [dot_nn(choose, line_grads[r, tokens:, :tokens]) for r in range(grid.line)]
-    )
+    (all_one, turned_out), down_x, down_y = first_exchange(
+        experts, [pack_one, pack_out], plans, down
+    )
+    line_grads, sent = after(
+        (jnp.concatenate([cotangent, widen(slot_of.astype(low))], axis=0), pair), turned_out
+    )
+    line_grads = grid.line_gather(line_grads)
+    pairs = [pair, grid.swap(sent, 1), grid.swap(sent, 2)]
+    downs = [down, down_x, down_y]
     all_one = all_one.reshape(model_width, -1)
     turned_out = turned_out.reshape(model_width, model_width)
     extra = all_one[:, 3 * model_width :]
     router_low = extra[:, :experts]
     gains = extra[:, experts : experts + 2].astype(full).T
     gain_one, gain_two = gains[0], gains[1]
-    pack_shared, _ = lax.optimization_barrier((pack_shared, turned_out))
-    all_shared = lax.all_gather(pack_shared, ("dp", "expert"), axis=0, tiled=True)
-    shared_pair = [all_shared[:, m * hidden_width : (m + 1) * hidden_width] for m in range(2)]
-    turned_down = all_shared[:, 2 * hidden_width :]
     inputs = tokens_in.astype(full)
     rstd_one = lax.rsqrt(jnp.mean(inputs * inputs, axis=-1, keepdims=True) + eps_norm)
     normed_one = (inputs * rstd_one * gain_one).astype(low)
@@ -1178,40 +1099,47 @@
     gating = logit_exps / jnp.sum(logit_exps, axis=0, keepdims=True)
     gating_live = jnp.where(member, gating, 0.0)
     gate_words = jnp.concatenate(split_words(gating_live), axis=1)
-    line_rows, up_x, up_y, *far = second_exchange(
-        experts,
-        jnp.concatenate([normed_two, widen(gate_words)], axis=0),
-        up,
-        gates[1],
-        downs[1],
-        downs[2],
-    )
-    weights = list(zip(gates, (up_own, up_x, up_y), downs)) + [(far[0], far[1], far[2])]
-    weights = [[part.reshape(-1, part.shape[-1]) for part in parts] for parts in weights]
-    gate_rows = []
-    for r in range(grid.line):
-        words = dot_nn(choose, line_rows[r, tokens:, : 3 * tokens])
-        gate_rows.append(
-            words[:, :tokens] + words[:, tokens : 2 * tokens] + words[:, 2 * tokens :]
+    line_rows = jnp.concatenate([normed_two, widen(gate_words)], axis=0)
+    rising, falling, *weights = second_exchange(experts, line_rows, pairs, downs)
+    line_rows = grid.line_gather(line_rows, rising, falling)
+    weights = [part.reshape(PLANE, -1, part.shape[-1]) for part in weights]
+
+    kept, grad_parts, result_parts = [], [], []
+    last = weights
+    for start in range(0, grid.line, 2):
+        group = range(start, start + 2)
+        line_part = [line_rows[r] for r in group], [line_grads[r] for r in group]
+        rows, grads = after(line_part, last)
+        slot_rows, gate_rows = [], []
+        for part in rows:
+            words = dot_nn(choose, part[tokens:, : 3 * tokens])
+            gate_row = words[:, :tokens] + words[:, tokens : 2 * tokens] + words[:, 2 * tokens :]
+            gate_rows.append(gate_row[:, None])
+        for part in grads:
+            slot_rows.append(dot_nn(choose, part[tokens:, :tokens])[:, None])
+        grad_part, result_part, parts = run_experts(
+            wanted, rows, grads, slot_rows, gate_rows, weights, slots
         )
-    gate_rows = jnp.stack(gate_rows)
-
-    before, kept = [], []
-    for q in range(PLANE):
-        *before, rows, inner, gated, grad_gate, grad_up = run_expert(
-            wanted[q : q + 1],
-            line_rows,
-            line_grads,
-            slot_rows[:, q : q + 1],
-            gate_rows[:, q : q + 1],
-            weights[q],
-            before,
-            slots,
-        )
-        kept.append((rows, inner, gated, grad_gate, grad_up))
-    routed_grad, routed_result = before
-    routed_grad, owns, crossed, far = third_exchange(experts, routed_grad, kept)
-    routed_result = grid.line_sum(after(routed_result, routed_grad))
+        kept.append(parts)
+        last = grad_part
+        grad_parts += [grid.shift(part, -r) if r else part for r, part in zip(group, grad_part)]
+        result_parts += result_part
+    routed_grad = sum(part.astype(full) for part in grad_parts)
+    result_parts = after(result_parts, routed_grad)
+    routed_result = sum(
+        (grid.shift(part, -r) if r else part).astype(full) for r, part in enumerate(result_parts)
+    )
+    owns, crossed, far = third_exchange(experts, after(kept, last))
+    near_x = [add_low(*pair) for pair in zip(owns[1], crossed[1])]
+    near_y = [add_low(*pair) for pair in zip(owns[2], crossed[2])]
+    edge = far[2].shape[0]
+    near_x[0] = add_low(near_x[0], far[0])
+    near_y[1] = add_low(near_y[1], far[1])
+    near_x[2] = jnp.concatenate([add_low(near_x[2][:edge], far[2]), near_x[2][edge:]], axis=0)
+    near_y[2] = jnp.concatenate([near_y[2][:edge], add_low(near_y[2][edge:], far[3])], axis=0)
+    arrived = []
+    for (gate, up, down), flip in ((near_x, 1), (near_y, 2)):
+        arrived.append(grid.swap(jnp.stack([gate, up, down.reshape(up.shape)]), flip))
     gate_grads = routed_grad[tokens:]
     routed_grad = routed_grad[:tokens]
     grad_gating = (
@@ -1225,6 +1153,11 @@
         normed_two, grad_logits, (((0,), (1,)), ((), ())), preferred_element_type=full
     )
 
+    all_shared = lax.all_gather(
+        after(pack_shared, weights), ("dp", "expert"), axis=0, tiled=True
+    )
+    shared_pair = [all_shared[:, m * hidden_width : (m + 1) * hidden_width] for m in range(2)]
+    turned_down = all_shared[:, 2 * hidden_width :]
     grad_out = cotangent.astype(full)
     shared_gate = dot_nn(normed_two, shared_pair[0])
     shared_up = dot_nn(normed_two, shared_pair[1])
@@ -1268,13 +1201,6 @@
         cosine,
         sine_table,
     )
-    near_x = [add_low(*pair) for pair in zip(owns[1], crossed[1])]
-    near_y = [add_low(*pair) for pair in zip(owns[2], crossed[2])]
-    edge = far[2].shape[0]
-    near_x[0] = add_low(near_x[0], far[0])
-    near_y[1] = add_low(near_y[1], far[1])
-    near_x[2] = jnp.concatenate([add_low(near_x[2][:edge], far[2]), near_x[2][edge:]], axis=0)
-    near_y[2] = jnp.concatenate([near_y[2][:edge], add_low(near_y[2][edge:], far[3])], axis=0)
     scaled_one = grad_normed_one * gain_one
     grad_gain_one = jnp.sum(grad_normed_one * inputs * rstd_one, axis=0)
     input_grad = (
@@ -1290,8 +1216,8 @@
         ],
         axis=1,
     )
-    cut = 512
-    summed_one, summed_two, *arrived = sum_all(
+    cut = 7 * 128
+    summed_one, summed_two = sum_all(
         experts,
         grads_attention + grads_shared + [grad_extra],
         [
@@ -1306,19 +1232,27 @@
                 [(6, 0, hidden_width)],
             ],
         ],
-        near_x + near_y,
-        ("x",) * 3 + ("y",) * 3,
+        [],
+        (),
     )
     summed_one, summed_two = summed_one.astype(full), summed_two.astype(full)
 
     output = (hidden + shared_result + routed_result).astype(low)
 
-    summed_gate, summed_up, summed_expert_down = [
-        sum(part.astype(full) for part in four)
-        for four in zip(owns[0], crossed[0], arrived[:3], arrived[3:])
-    ]
-    summed_expert_in = jnp.stack([summed_gate, summed_up], axis=0)[None]
-    summed_expert_down = summed_expert_down[None]
+    arrived = after(arrived, summed_one)
+    summed_expert_in = jnp.stack(
+        [
+            sum(
+                part.astype(full)
+                for part in (owns[0][i], crossed[0][i], arrived[0][i], arrived[1][i])
+            )
+            for i in range(2)
+        ]
+    )[None]
+    brought = add_low(arrived[0][2], arrived[1][2]).reshape(owns[0][2].shape)
+    summed_expert_down = sum(
+        part.astype(full) for part in (owns[0][2], crossed[0][2], brought)
+    )[None]
 
     def take(array, start, width):
         return array[:, start : start + width]

time: 841 us -> 672 us (0.80)
  Pallas kernels: 667 us -> 451 us
  other arithmetic: 63.9 us -> 84.1 us
  waiting for transfers between devices: 0.03 us -> 16.7 us
  starting transfers between devices: 5.39 us -> 20.4 us
    pallas_call x7 -> x5, Pallas kernels: 425 us -> 280 us  [the longest x1 88.3 us: first_exchange(): pl.pallas_call(functools.partial(first_kernel, line, plans), out_shape=[j...]
    pallas_call x1, Pallas kernels: 196 us -> 125 us  [sum_all(): pl.pallas_call(functools.partial(sum_kernel, line, tuple(kernel_plans), w...]
    ppermute x0 -> x4, waiting for transfers between devices: none -> 16.7 us  [swap(): return lax.ppermute(block, 'expert', pairs)]
    unnamed x199 -> x175, local copies, waits for them, and re-layouts: 27.8 us -> 15.9 us
    ppermute x3 -> x10, starting transfers between devices: 5.35 us -> 16.2 us  [shift(): return lax.ppermute(block, 'expert', pairs)]
    convert_element_type x1 -> x3, other arithmetic: 0.11 us -> 9.98 us  [the longest x2 6.77 us: local(): pair, down = (expert_in[0].astype(low), expert_down[0].astype(low))]
    another operation x11 -> x9, other arithmetic: 6.13 us -> 15.9 us  [the longest x6 8.92 us: local(): jnp.stack([gate, up, down.reshape(up.shape)])]
  transfers between devices with their start and end apart: 4 -> 15, of which waited for: 0 -> 2; matrix products, arithmetic and copies ran while one was open for 13% -> 20% of each run, Pallas kernels for 63% -> 55%
where the time goes in v3:
time: 672 us; the launch traced here: 664 us
  Pallas kernels  451 us (67%)
  other arithmetic  84.1 us (13%)
  local copies, waits for them, and re-layouts  41.5 us (6%)
  matrix products  34 us (5%)
  starting transfers between devices  20.4 us (3%)
  waiting for transfers between devices  16.7 us (2%)
  between operations  16 us (2%)
    pallas_call x1, Pallas kernels, sum_all(): pl.pallas_call(functools.partial(sum_kernel, line, tuple(kernel_plans), w...  125 us
    pallas_call x1, Pallas kernels, first_exchange(): pl.pallas_call(functools.partial(first_kernel, line, plans), out_shape=[j...  88.3 us
    pallas_call x2, Pallas kernels, run_experts(): pl.pallas_call(functools.partial(expert_kernel, count), grid_spec=pltpu.P...  87.6 us
    pallas_call x1, Pallas kernels, third_exchange(): pl.pallas_call(functools.partial(third_kernel, line, len(kept)), out_shap...  57.2 us
    pallas_call x1, Pallas kernels, second_exchange(): pl.pallas_call(functools.partial(second_kernel, line), out_shape=[jax.Sha...  46.8 us
    pallas_call x1, Pallas kernels, attend_back(): pl.pallas_call(attend_back_kernel, grid=(steps,), in_specs=[whole(tokens,...  27.1 us
    add x8, other arithmetic, advance(): average_new = average + (weight_new - average) / (STEP + 1)  23.8 us
    pallas_call x1, Pallas kernels, attend(): pl.pallas_call(functools.partial(attend_kernel, steps), grid=(steps,), in...  18.8 us
  transfers between devices with their start and end apart: 15, of which 2 were waited for; matrix products, arithmetic and copies ran while one was open for 20% of the time, Pallas kernels for 55%

profile of v3, /device:TPU:0, one launch (start us, length us, event | category | flops | bytes accessed | tf_op | source)
XLA Modules:
  0.0 663.7 jit_solution(4738273922799359454)
XLA Ops:
  11.6 2.8 convert_bitcast_fusion.1.refs_2_.refs_4_
  15.1 4.0 convert_bitcast_fusion.refs_1_
  21.1 88.3 %shard_map.476 = (bf16[2,4,2,2,40,3968]{5,4,3,2,1,0:T(8,128)(2,1)}, bf16[2,4,2,2,40,1280]{5,4,3,2,1,0:T(8,128)(2,1)}, bf16[448,1280]{1,0:T(8,128)(2,1)}, bf16[448,1280]{1,0:T(8,128)(2,1)}) custom-call(bf16[40,3968]{1,0:T(8,128)(2,1)} %concatenate.34.refs_0_, bf16[40,1280]{1,0:T(8,128)(2,1)} %convert_bitcast_fusion.3.refs_1_, ...), custom_call_target="tpu_custom_call" | custom-call | tf_op jit(solution)/shard_map/pallas_call | solution.py:269
  111.9 3.4 collective-permute-start.5
  120.5 18.8 %shard_map.477 = (bf16[384,1280]{1,0:T(8,128)(2,1)S(1)}, bf16[384,1280]{1,0:T(8,128)(2,1)S(1)}, bf16[384,1280]{1,0:T(8,128)(2,1)S(1)}, bf16[384,1280]{1,0:T(8,12...) custom-call(bf16[384,1280]{1,0:T(8,128)(2,1)} %fusion.18.normed, bf16[1280,3968]{1,0:T(8,128)(2,1)} %bitcast.143, ...), custom_call_target="tpu_custom_call" | custom-call | flops 5033164800 | bytes 32768000 | tf_op jit(solution)/shard_map/pallas_call | solution.py:689
  146.4 15.6 %collective-permute-done.refs_2_ = bf16[2,640,896]{2,1,0:T(8,128)(2,1)} collective-permute-done((bf16[2,640,896]{2,1,0:T(8,128)(2,1)}, bf16[2,640,896]{2,1,0:T(8,128)(2,1)}, u32[]{:S(2)}, u32[]{:S(2)}) %collective-permute-start) | collective-permute-done | bytes 2293792 | tf_op jit(solution)/shard_map/ppermute | solution.py:977
  163.0 46.8 %shard_map.478 = (bf16[400,1280]{1,0:T(8,128)(2,1)}, bf16[400,1280]{1,0:T(8,128)(2,1)}, bf16[4,2,640,896]{3,2,1,0:T(8,128)(2,1)}, bf16[4,2,640,896]{3,2,1,0:T(8,128)(2,1)}, bf16[4,2,448,1280]{3,2,1,0:T(8,128)(2,1)}) custom-call(bf16[400,1280]{1,0:T(8,128)(2,1)} %pad_maximum_fusion.4.refs_0_, bf16[2,640,896]{2,1,0:T(8,128)(2,1)} %convert_bitcast_fusion.refs_1_, ...), custom_call_target="tpu_custom_call" | custom-call | tf_op jit(solution)/shard_map/pallas_call | solution.py:329
  216.9 2.6 collective-permute-start.3
  225.6 43.8 %shard_map.479 = (bf16[400,1280]{1,0:T(8,128)(2,1)}, bf16[400,1280]{1,0:T(8,128)(2,1)}, bf16[384,1280]{1,0:T(8,128)(2,1)}, bf16[384,1280]{1,0:T(8,128)(2,1)}, bf...) custom-call(s32[4]{0:T(128)} %copy-done.80, ...), custom_call_target="tpu_custom_call" | custom-call | flops 23655874560 | bytes 27525120 | tf_op jit(solution)/shard_map/pallas_call | solution.py:903
  277.6 43.8 %shard_map.480 = (bf16[400,1280]{1,0:T(8,128)(2,1)}, bf16[400,1280]{1,0:T(8,128)(2,1)}, bf16[384,1280]{1,0:T(8,128)(2,1)}, bf16[384,1280]{1,0:T(8,128)(2,1)}, bf...) custom-call(s32[4]{0:T(128)} %copy-done.80, ...), custom_call_target="tpu_custom_call" | custom-call | flops 23655874560 | bytes 27525120 | tf_op jit(solution)/shard_map/pallas_call | solution.py:903
  323.7 57.2 %shard_map.483 = (bf16[640,896]{1,0:T(8,128)(2,1)}, bf16[640,896]{1,0:T(8,128)(2,1)}, bf16[448,1280]{1,0:T(8,128)(2,1)}, bf16[640,896]{1,0:T(8,128)(2,1)}, bf16[...) custom-call(bf16[4,384,1280]{2,1,0:T(8,128)(2,1)} %get-tuple-element, ...), custom_call_target="tpu_custom_call" | custom-call | tf_op jit(solution)/shard_map/pallas_call | solution.py:432
  384.1 2.7 stack_reshape.6
  395.7 2.4 stack_reshape.7
  403.8 2.3 convert_add_fusion.4
  406.1 2.5 collective-permute-start.11
  411.6 3.0 fusion.14
  420.8 2.7 multiply_reduce_fusion
  427.3 27.1 %shard_map.481 = (bf16[1280,1280]{1,0:T(8,128)(2,1)}, bf16[1280,1280]{1,0:T(8,128)(2,1)}, bf16[1280,1280]{1,0:T(8,128)(2,1)}, bf16[1280,1280]{1,0:T(8,128)(2,1)}, f32[384,1280]{1,0:T(8,128)}) custom-call(bf16[384,1280]{1,0:T(8,128)(2,1)S(1)} %get-tuple-element.338.grad_branch, bf16[384,1280]{1,0:T(8,128)(2,1)S(1)} %copy-done, ...), custom_call_target="tpu_custom_call" | custom-call | flops 10066329600 | bytes 65536000 | tf_op jit(solution)/shard_map/pallas_call | solution.py:783
  454.4 2.1 fusion.23
  456.7 2.8 fusion
  459.5 4.3 copy.129
  463.8 4.0 convolution_convert_fusion.2
  467.8 2.9 convolution_convert_fusion.1
  471.8 125.2 %shard_map.482 = (bf16[40,3968]{1,0:T(8,128)(2,1)}, bf16[40,3968]{1,0:T(8,128)(2,1)}) custom-call(bf16[2,4,2,2,40,1280]{5,4,3,2,1,0:T(8,128)(2,1)} %bitcast.156, bf16[2,4,2,2,40,1280]{5,4,3,2,1,0:T(8,128)(2,1)} %bitcast.153, bf16[2,4,2,2,40,1280]{5,4,3,2,1,0:T(8,128)(2,1)} %bitcast.157, bf16[2,4,2,2,40,128]{5,4,3,2,1,0:T(8,128)(2,1)} %bitcast.161, ...), custom_call_target="tpu_custom_call" | custom-call | tf_op jit(solution)/shard_map/pallas_call | solution.py:604
  603.1 3.2 fusion.32
  606.3 3.0 reshape.189
  614.3 3.5 fusion.20
  619.8 5.8 fusion.2
  628.4 3.7 multiply_add_fusion.2
  632.1 4.2 convolution_add_fusion.2
  641.0 12.2 %multiply_add_fusion = (f32[1,2,640,896]{3,2,1,0:T(8,128)}, f32[1,2,640,896]{3,2,1,0:T(8,128)}, f32[1,2,640,896]{3,2,1,0:T(8,128)}) fusion(f32[1,2,640,896]{3,2,1,0:T(8,128)} %param.54, f32[1,2,640,896]{3,2,1,0:T(8,128)} %param.52, f32[1,640,896]{2,1,0:T(8,128)} %get-tuple-element.341, f32[1,640,896]{2,1,0:T(8,128)} %get-tuple-element.340, ...), kind=kLoop, calls=%fused_computation.1 | loop fusion | flops 11468800 | bytes 32112640 | tf_op jit(solution)/shard_map/add | solution.py:55
  653.3 3.4 add_convert_fusion.9
  (301 shorter events, 97.8 us)
Async XLA Ops:
  7.2 404.4 %all-gather.2.cloned.1.call-start = ((), (), s32[]{:S(2)}) async-start(), calls=%async_computation | async-start | bytes 7096320 | tf_op jit(solution)/shard_map/all_gather | solution.py:1156
  21.1 96.0 %copy-start.10 = (bf16[384,1280]{1,0:T(8,128)(2,1)S(1)}, bf16[384,1280]{1,0:T(8,128)(2,1)}, u32[]{:S(2)}) copy-start(bf16[384,1280]{1,0:T(8,128)(2,1)} %inputs.1) | copy-start | bytes 2949124
  109.4 52.5 %collective-permute-start = (bf16[2,640,896]{2,1,0:T(8,128)(2,1)}, bf16[2,640,896]{2,1,0:T(8,128)(2,1)}, u32[]{:S(2)}, u32[]{:S(2)}) collective-permute-start(bf16[2,640,896]{2,1,0:T(8,128)(2,1)} %convert_bitcast_fusion.refs_1_), channel_id=1, source_target_pairs={{0,1},{1,0},{2,3},{3,2},{4,5},{5,4},{6,7},{7,6},{8,9},{9,8},{10,11... | collective-permute-start | bytes 6881288 | tf_op jit(solution)/shard_map/ppermute | solution.py:977
  110.9 52.1 %collective-permute-start.1 = (bf16[2,640,896]{2,1,0:T(8,128)(2,1)}, bf16[2,640,896]{2,1,0:T(8,128)(2,1)}, u32[]{:S(2)}, u32[]{:S(2)}) collective-permute-start(bf16[2,640,896]{2,1,0:T(8,128)(2,1)} %convert_bitcast_fusion.refs_1_), channel_id=1, source_target_pairs={{0,2},{1,3},{2,0},{3,1},{4,6},{5,7},{6,4},{7,5},{8,10},{9,11},{10,... | collective-permute-start | bytes 6881288 | tf_op jit(solution)/shard_map/ppermute | solution.py:977
  111.5 104.8 %collective-permute-start.2 = (bf16[400,1280]{1,0:T(8,128)(2,1)}, bf16[400,1280]{1,0:T(8,128)(2,1)}, u32[]{:S(2)}, u32[]{:S(2)}) collective-permute-start(bf16[400,1280]{1,0:T(8,128)(2,1)} %fusion.34.refs_2_), channel_id=1, source_target_pairs={{0,4},{1,5},{2,6},{3,7},{4,8},{5,9},{6,10},{7,11},{8,12},{9,13},{1... | collective-permute-start | bytes 3072008 | tf_op jit(solution)/shard_map/ppermute | solution.py:973
  111.9 159.5 %collective-permute-start.5 = (bf16[400,1280]{1,0:T(8,128)(2,1)}, bf16[400,1280]{1,0:T(8,128)(2,1)}, u32[]{:S(2)}, u32[]{:S(2)}) collective-permute-start(bf16[400,1280]{1,0:T(8,128)(2,1)} %fusion.34.refs_2_), channel_id=1, source_target_pairs={{0,12},{1,13},{2,14},{3,15},{4,0},{5,1},{6,2},{7,3},{8,4},{9,5},{1... | collective-permute-start | bytes 3072008 | tf_op jit(solution)/shard_map/ppermute | solution.py:973
  120.5 24.1 %copy-start.54 = (f32[896,40]{0,1:T(8,128)S(1)}, f32[896,40]{0,1:T(8,128)}, u32[]{:S(2)}) copy-start(f32[896,40]{0,1:T(8,128)} %param.43) | copy-start | bytes 430084
  144.5 65.3 %copy-start.64 = (f32[384]{0:T(512)}, f32[384]{0:T(512)S(1)}, u32[]{:S(2)}) copy-start(f32[384]{0:T(512)S(1)} %fusion.60) | copy-start | bytes 4612
  163.0 46.8 %copy-start.76 = (f32[2,40]{1,0:T(2,128)S(1)}, f32[2,40]{1,0:T(2,128)}, u32[]{:S(2)}) copy-start(f32[2,40]{1,0:T(2,128)} %param.50) | copy-start | bytes 964
  163.0 46.9 %copy-start.66 = (f32[40,16]{0,1:T(8,128)S(1)}, f32[40,16]{0,1:T(8,128)}, u32[]{:S(2)}) copy-start(f32[40,16]{0,1:T(8,128)} %param.46) | copy-start | bytes 7684
  163.0 47.0 %copy-start.77 = (f32[2,40]{1,0:T(2,128)S(1)}, f32[2,40]{1,0:T(2,128)}, u32[]{:S(2)}) copy-start(f32[2,40]{1,0:T(2,128)} %param.49) | copy-start | bytes 964
  163.0 47.6 %copy-start.73 = (f32[40,16]{0,1:T(8,128)S(1)}, f32[40,16]{0,1:T(8,128)}, u32[]{:S(2)}) copy-start(f32[40,16]{0,1:T(8,128)} %param.48) | copy-start | bytes 7684
  163.0 48.3 %copy-start.74 = (f32[40,16]{0,1:T(8,128)S(1)}, f32[40,16]{0,1:T(8,128)}, u32[]{:S(2)}) copy-start(f32[40,16]{0,1:T(8,128)} %param.47) | copy-start | bytes 7684
  163.0 49.0 %copy-start.78 = (f32[2,40]{1,0:T(2,128)S(1)}, f32[2,40]{1,0:T(2,128)}, u32[]{:S(2)}) copy-start(f32[2,40]{1,0:T(2,128)} %param.51) | copy-start | bytes 964
  214.0 11.0 %copy-start.80 = (s32[4]{0:T(128)}, s32[4]{0:T(128)S(1)}, u32[]{:S(2)}) copy-start(s32[4]{0:T(128)S(1)} %xor_add_fusion.numbers) | copy-start | bytes 52
  216.4 55.1 %collective-permute-start.4 = (bf16[400,1280]{1,0:T(8,128)(2,1)}, bf16[400,1280]{1,0:T(8,128)(2,1)}, u32[]{:S(2)}, u32[]{:S(2)}) collective-permute-start(bf16[400,1280]{1,0:T(8,128)(2,1)} %collective-permute-done.2.refs_3_), channel_id=1, source_target_pairs={{0,4},{1,5},{2,6},{3,7},{4,8},{5,9},{6,10},{7,11},{8,12},{9,13},{1... | collective-permute-start | bytes 3072008 | tf_op jit(solution)/shard_map/ppermute | solution.py:973
  216.9 54.6 %collective-permute-start.3 = (bf16[400,1280]{1,0:T(8,128)(2,1)}, bf16[400,1280]{1,0:T(8,128)(2,1)}, u32[]{:S(2)}, u32[]{:S(2)}) collective-permute-start(bf16[400,1280]{1,0:T(8,128)(2,1)} %get-tuple-element.129.refs_1_), channel_id=1, source_target_pairs={{0,4},{1,5},{2,6},{3,7},{4,8},{5,9},{6,10},{7,11},{8,12},{9,13},{1... | collective-permute-start | bytes 3072008 | tf_op jit(solution)/shard_map/ppermute | solution.py:973
  269.4 134.3 %collective-permute-start.6 = (bf16[400,1280]{1,0:T(8,128)(2,1)}, bf16[400,1280]{1,0:T(8,128)(2,1)}, u32[]{:S(2)}, u32[]{:S(2)}) collective-permute-start(bf16[400,1280]{1,0:T(8,128)(2,1)} %get-tuple-element.136), channel_id=1, source_target_pairs={{0,12},{1,13},{2,14},{3,15},{4,0},{5,1},{6,2},{7,3},{8,4},{9,5},{1... | collective-permute-start | bytes 3072008 | tf_op jit(solution)/shard_map/ppermute | solution.py:973
  321.4 82.3 %collective-permute-start.8 = (bf16[400,1280]{1,0:T(8,128)(2,1)}, bf16[400,1280]{1,0:T(8,128)(2,1)}, u32[]{:S(2)}, u32[]{:S(2)}) collective-permute-start(bf16[400,1280]{1,0:T(8,128)(2,1)} %get-tuple-element.144), channel_id=1, source_target_pairs={{0,4},{1,5},{2,6},{3,7},{4,8},{5,9},{6,10},{7,11},{8,12},{9,13},{1... | collective-permute-start | bytes 3072008 | tf_op jit(solution)/shard_map/ppermute | solution.py:973
  322.2 81.5 %collective-permute-start.7 = (bf16[400,1280]{1,0:T(8,128)(2,1)}, bf16[400,1280]{1,0:T(8,128)(2,1)}, u32[]{:S(2)}, u32[]{:S(2)}) collective-permute-start(bf16[400,1280]{1,0:T(8,128)(2,1)} %get-tuple-element.143), channel_id=1, source_target_pairs={{0,8},{1,9},{2,10},{3,11},{4,12},{5,13},{6,14},{7,15},{8,0},{9,1},... | collective-permute-start | bytes 3072008 | tf_op jit(solution)/shard_map/ppermute | solution.py:973
  392.0 211.1 %collective-permute-start.12 = (bf16[3,640,896]{2,1,0:T(8,128)(2,1)}, bf16[3,640,896]{2,1,0:T(8,128)(2,1)}, u32[]{:S(2)}, u32[]{:S(2)}) collective-permute-start(bf16[3,640,896]{2,1,0:T(8,128)(2,1)} %pad_maximum_fusion), channel_id=1, source_target_pairs={{0,1},{1,0},{2,3},{3,2},{4,5},{5,4},{6,7},{7,6},{8,9},{9,8},{10,11... | collective-permute-start | bytes 10321928 | tf_op jit(solution)/shard_map/ppermute | solution.py:977
  403.2 7.9 %copy-start.65 = (f32[384]{0:T(512)S(1)}, f32[384]{0:T(512)}, u32[]{:S(2)}) copy-start(f32[384]{0:T(512)} %copy-done.64) | copy-start | bytes 4612
  403.2 200.0 %collective-permute-start.13 = (bf16[3,640,896]{2,1,0:T(8,128)(2,1)}, bf16[3,640,896]{2,1,0:T(8,128)(2,1)}, u32[]{:S(2)}, u32[]{:S(2)}) collective-permute-start(bf16[3,640,896]{2,1,0:T(8,128)(2,1)} %pad_maximum_fusion.1), channel_id=1, source_target_pairs={{0,2},{1,3},{2,0},{3,1},{4,6},{5,7},{6,4},{7,5},{8,10},{9,11},{10,... | collective-permute-start | bytes 10321928 | tf_op jit(solution)/shard_map/ppermute | solution.py:977
  406.1 247.1 %collective-permute-start.11 = (bf16[384,1280]{1,0:T(8,128)(2,1)}, bf16[384,1280]{1,0:T(8,128)(2,1)}, u32[]{:S(2)}, u32[]{:S(2)}) collective-permute-start(bf16[384,1280]{1,0:T(8,128)(2,1)} %get-tuple-element.148), channel_id=1, source_target_pairs={{0,4},{1,5},{2,6},{3,7},{4,8},{5,9},{6,10},{7,11},{8,12},{9,13},{1... | collective-permute-start | bytes 2949128 | tf_op jit(solution)/shard_map/ppermute | solution.py:973
  408.6 244.7 %collective-permute-start.10 = (bf16[384,1280]{1,0:T(8,128)(2,1)}, bf16[384,1280]{1,0:T(8,128)(2,1)}, u32[]{:S(2)}, u32[]{:S(2)}) collective-permute-start(bf16[384,1280]{1,0:T(8,128)(2,1)} %get-tuple-element.147), channel_id=1, source_target_pairs={{0,8},{1,9},{2,10},{3,11},{4,12},{5,13},{6,14},{7,15},{8,0},{9,1},... | collective-permute-start | bytes 2949128 | tf_op jit(solution)/shard_map/ppermute | solution.py:973
  409.2 244.0 %collective-permute-start.9 = (bf16[384,1280]{1,0:T(8,128)(2,1)}, bf16[384,1280]{1,0:T(8,128)(2,1)}, u32[]{:S(2)}, u32[]{:S(2)}) collective-permute-start(bf16[384,1280]{1,0:T(8,128)(2,1)} %get-tuple-element.146), channel_id=1, source_target_pairs={{0,12},{1,13},{2,14},{3,15},{4,0},{5,1},{6,2},{7,3},{8,4},{9,5},{1... | collective-permute-start | bytes 2949128 | tf_op jit(solution)/shard_map/ppermute | solution.py:973
  418.0 38.7 %copy-start.46 = (bf16[384,896]{1,0:T(8,128)(2,1)}, bf16[384,896]{1,0:T(8,128)(2,1)S(1)}, u32[]{:S(2)}) copy-start(bf16[384,896]{1,0:T(8,128)(2,1)S(1)} %get-tuple-element.344) | copy-start | bytes 2064388
  427.3 27.1 %copy-start.11 = (bf16[384,1280]{1,0:T(8,128)(2,1)S(1)}, bf16[384,1280]{1,0:T(8,128)(2,1)}, u32[]{:S(2)}) copy-start(bf16[384,1280]{1,0:T(8,128)(2,1)} %inputs.1) | copy-start | bytes 2949124
  427.3 27.1 %copy-start.68 = (f32[384]{0:T(512)S(1)}, f32[384]{0:T(512)}, u32[]{:S(2)}) copy-start(f32[384]{0:T(512)} %copy-done.67) | copy-start | bytes 4612
  619.8 7.3 %copy-start.13 = (f32[448,1280]{1,0:T(8,128)S(1)}, f32[448,1280]{1,0:T(8,128)}, u32[]{:S(2)}) copy-start(f32[448,1280]{1,0:T(8,128)} %reshape.189) | copy-start | bytes 6881284
  641.0 12.2 %copy-start.15 = (f32[384,1280]{1,0:T(8,128)S(1)}, f32[384,1280]{1,0:T(8,128)}, u32[]{:S(2)}) copy-start(f32[384,1280]{1,0:T(8,128)} %convolution_add_fusion.2) | copy-start | bytes 5898244
  641.0 12.2 %copy-start.43 = (bf16[384,1280]{1,0:T(8,128)(2,1)S(1)}, bf16[384,1280]{1,0:T(8,128)(2,1)}, u32[]{:S(2)}) copy-start(bf16[384,1280]{1,0:T(8,128)(2,1)} %get-tuple-element.145) | copy-start | bytes 2949124
  (65 other events, 230.7 us)
Sparse Core Ops, SparseCore 0:
  210.0 169.9 all-gather.1

commit v4 on v3

--- a/solution.py
+++ b/solution.py
@@ -339,24 +339,40 @@
     )(rows, *pairs, *downs)
 
 
+def packed(half, hidden_width, down_half, width):
+    edge, more = down_half // 2, width - hidden_width
+    below = 2 * half + down_half
+    full = slice(0, hidden_width)
+    rest = slice(hidden_width, width)
+    places = [
+        (0, slice(0, half), full, slice(0, half), full),
+        (1, slice(half, 2 * half), full, slice(0, half), full),
+        (2, slice(2 * half, 2 * half + edge), full, slice(0, edge), full),
+        (2, slice(2 * half + edge, below), full, slice(edge, down_half), full),
+        (2, slice(below, below + edge), slice(0, more), slice(0, edge), rest),
+        (2, slice(below, below + edge), slice(more, 2 * more), slice(edge, down_half), rest),
+    ]
+    return places, below + edge, 2 * more
+
+
 def third_kernel(line, groups, *refs):
     low, full = jnp.bfloat16, jnp.float32
     kept = [refs[5 * r : 5 * r + 5] for r in range(groups)]
     refs = refs[5 * groups :]
-    owns = [refs[3 * q : 3 + 3 * q] for q in range(PLANE - 1)]
-    refs = refs[3 * (PLANE - 1) :]
-    crossed = [refs[3 * q : 3 + 3 * q] for q in range(PLANE - 1)]
-    refs = refs[3 * (PLANE - 1) :]
-    far_in, refs = refs[:4], refs[4:]
+    owns, crossed, nears, refs = refs[:3], refs[3:6], refs[6:8], refs[8:]
     loaded, refs = [refs[:5], refs[5:10]], refs[10:]
     results, refs = [refs[:6], refs[6:12]], refs[12:]
-    far_box, down_grad, refs = refs[:3], refs[3], refs[4:]
+    far_box, far_in, near_box, down_grad, refs = refs[:3], refs[3:7], refs[7:9], refs[9], refs[10:]
     spot = Spot(line)
     meet(spot)
     moves = Moves(spot, *refs)
     order = (3, 1, 2, 0)
     slots = kept[0][0].shape[1]
     loads = {}
+    rows_half, hidden_width = results[0][0].shape
+    down_half, width = results[0][2].shape
+    edge = down_half // 2
+    places, _, used = packed(rows_half, hidden_width, down_half, width)
 
     def load(n):
         loads[n] = [
@@ -369,8 +385,9 @@
         target[...] = (target[...].astype(full) + source[...].astype(full)).astype(low)
 
     load(0)
-    rows_half = results[0][0].shape[0]
-    down_half = results[0][2].shape[0]
+    for box in near_box:
+        spare = (slice(2 * rows_half + down_half, box.shape[0]), slice(used, hidden_width))
+        box[spare] = jnp.zeros((edge, hidden_width - used), low)
     sent = {}
 
     def weights(n):
@@ -380,10 +397,8 @@
             copy.wait()
         rows, inner, gated, grad_gate, grad_up = loaded[n % 2]
         buffers = results[n % 2]
-        if n == 3:
-            for copy in sent[1]:
-                copy.wait()
         down_grad[...] = dot_tn(inner[...], gated[...]).astype(low)
+        q = order[n]
         for which in (1, 0):
             place = jnp.bitwise_xor(spot.core, which)
             gate_out, up_out, down_out = buffers[3 * which : 3 * which + 3]
@@ -391,12 +406,20 @@
             gate_out[...] = dot_tn(part, grad_gate[...]).astype(low)
             up_out[...] = dot_tn(part, grad_up[...]).astype(low)
             down_out[...] = down_grad[pl.ds(pl.multiple_of(place * down_half, 16), down_half), :]
-            q = order[n]
-            targets = far_box if q == PLANE - 1 else crossed[q]
-            if which:
+            if which and q in (0, 3):
+                targets = crossed if q == 0 else far_box
                 sent[n] = [moves.start(buffers[3 + i], targets[i], "core") for i in range(3)]
-            elif q < PLANE - 1:
-                sent[n] += [moves.keep(buffers[i], owns[q][i]) for i in range(3)]
+            elif which:
+                sent[n] = [
+                    moves.start(
+                        buffers[3 + i].at[rows_at, columns_at],
+                        near_box[q - 1].at[to_rows, to_columns],
+                        "core",
+                    )
+                    for i, to_rows, to_columns, rows_at, columns_at in places
+                ]
+            elif q == 0:
+                sent[n] += [moves.keep(buffers[i], owns[i]) for i in range(3)]
 
     def far():
         for copy in sent[0]:
@@ -404,21 +427,41 @@
         mine = results[0][:3]
         for i in range(3):
             add(far_box[i], mine[i])
-        edge = down_half // 2
-        moves.start(far_box[0], far_in[0], "y", later=True)
-        moves.start(far_box[1], far_in[1], "x", later=True)
-        moves.start(far_box[2].at[pl.ds(0, edge)], far_in[2], "y", later=True)
-        moves.start(far_box[2].at[pl.ds(edge, edge)], far_in[3], "x", later=True)
+        upper, lower = pl.ds(0, edge), pl.ds(edge, edge)
+        return [
+            moves.start(far_box[0], far_in[0], "y"),
+            moves.start(far_box[1], far_in[1], "x"),
+            moves.start(far_box[2].at[upper], far_in[2], "y"),
+            moves.start(far_box[2].at[lower], far_in[3], "x"),
+        ]
+
+    def near(n):
+        for copy in sent[n]:
+            copy.wait()
+        box = near_box[order[n] - 1]
+        for i, to_rows, to_columns, rows_at, columns_at in places:
+            add(box.at[to_rows, to_columns], results[n % 2][i].at[rows_at, columns_at])
 
     weights(0)
     weights(1)
-    far()
+    across = far()
     weights(2)
+    near(1)
     weights(3)
-    for n in (2, 3):
-        for copy in sent[n]:
-            copy.wait()
-    moves.finish()
+    near(2)
+    for copy in across:
+        copy.wait()
+    rest, full_width = slice(hidden_width, width), slice(0, hidden_width)
+    for box, i, source in ((near_box[0], 0, far_in[0]), (near_box[1], 1, far_in[1])):
+        _, to_rows, to_columns, _, _ = places[i]
+        add(box.at[to_rows, to_columns], source)
+    for box, i, source in ((near_box[0], 0, far_in[2]), (near_box[1], 1, far_in[3])):
+        for index, columns_at in ((2 + i, full_width), (4 + i, rest)):
+            _, to_rows, to_columns, _, _ = places[index]
+            add(box.at[to_rows, to_columns], source.at[:, columns_at])
+    stores = [moves.keep(box, target) for box, target in zip(near_box, nears)]
+    for copy in sent[3] + stores:
+        copy.wait()
 
 
 def third_exchange(experts, kept):
@@ -429,36 +472,115 @@
     half, down_half = width // 2, hidden_width // 2
     pieces = [(half, hidden_width), (half, hidden_width), (down_half, width)]
     far = pieces[:2] + [(down_half // 2, width)] * 2
+    package = (packed(half, hidden_width, down_half, width)[1], hidden_width)
     out = pl.pallas_call(
         functools.partial(third_kernel, line, len(kept)),
-        out_shape=[
-            jax.ShapeDtypeStruct(size, low) for size in pieces * (2 * (PLANE - 1)) + far
-        ],
+        out_shape=[jax.ShapeDtypeStruct(size, low) for size in pieces * 2 + [package] * 2],
         in_specs=hbm(5 * len(kept)),
-        out_specs=hbm(6 * (PLANE - 1) + 4),
+        out_specs=hbm(8),
         scratch_shapes=[
             pltpu.VMEM((len(kept) * slots, array.shape[2]), low) for array in list(kept[0]) * 2
         ]
         + [pltpu.VMEM(size, low) for size in pieces * 4]
-        + [pltpu.VMEM(size, low) for size in pieces]
+        + [pltpu.VMEM(size, low) for size in pieces + far + [package] * 2]
         + [pltpu.VMEM((hidden_width, width), low)]
-        + semaphores(3 * PLANE + 4, 5 * PLANE * len(kept) + 3 * PLANE),
+        + semaphores(2 * 3 + 2 * 6 + 4, 5 * PLANE * len(kept) + 3 + 2),
         compiler_params=pltpu.CompilerParams(
             collective_id=4, has_side_effects=True, vmem_limit_bytes=62 * 1024 * 1024
         ),
     )(*[array for parts in kept for array in parts])
-    count = 3 * (PLANE - 1)
-    triples = lambda arrays: [arrays[3 * q : 3 * q + 3] for q in range(PLANE - 1)]
-    return triples(out[:count]), triples(out[count : 2 * count]), out[2 * count :]
-
-
-def sum_kernel(line, plans, ways, *refs):
+    return out[:3], out[3:6], out[6:]
+
+
+def sum_plans(width, hidden_width, extra_width):
+    edge = width * 8 // 10
+    half = width // 2
+    gate_edge = hidden_width * 5 // 7
+    return (
+        (((0, 0, edge),), ((1, 0, half),), ((0, edge, width - edge),)),
+        (((2, 0, edge),), ((1, half, width - half),), ((2, edge, width - edge),)),
+        (
+            ((3, 0, width - 128),),
+            ((4, 0, gate_edge),),
+            ((3, width - 128, 128), (7, 0, extra_width)),
+        ),
+        (
+            ((5, 0, hidden_width), (4, gate_edge, hidden_width - gate_edge)),
+            ((6, 0, gate_edge),),
+            ((6, gate_edge, hidden_width - gate_edge),),
+        ),
+    )
+
+
+def total_chain(moves, owns, crossed, arrived, totals, buffers):
+    full = jnp.float32
+    half, hidden_width = owns[0].shape
+    down_half, width = owns[2].shape
+    edge = down_half // 2
+    places, _, _ = packed(half, hidden_width, down_half, width)
+    jobs = []
+    for i in range(2):
+        for rows in range(0, half, half // 4):
+            jobs.append((i, rows, half // 4))
+    for rows in range(0, down_half, edge // 2):
+        jobs.append((2, rows, edge // 2))
+    loads, stores = {}, {}
+
+    def box(n, i):
+        wide = jobs[n][0] == 2
+        return buffers[10 * (n % 2) + 5 * wide + i]
+
+    def load(n):
+        which, start, rows = jobs[n]
+        at = pl.ds(start, rows)
+        copies = [(owns[which].at[at], box(n, 0)), (crossed[which].at[at], box(n, 1))]
+        for k, package in enumerate(arrived):
+            for part, to_rows, to_columns, rows_at, columns_at in places:
+                inside = rows_at.start <= start < rows_at.stop
+                if part == which and inside:
+                    copies.append(
+                        (
+                            package.at[
+                                pl.ds(to_rows.start + start - rows_at.start, rows), to_columns
+                            ],
+                            box(n, 2 + k).at[:, columns_at],
+                        )
+                    )
+        loads[n] = [moves.keep(source, target) for source, target in copies]
+
+    load(0)
+    for n, (which, start, rows) in enumerate(jobs):
+        if n + 1 < len(jobs):
+            load(n + 1)
+        for copy in loads[n]:
+            copy.wait()
+        if n >= 2:
+            for copy in stores[n - 2]:
+                copy.wait()
+        total = box(n, 4)
+        total[...] = sum(box(n, i)[...].astype(full) for i in range(4)).astype(total.dtype)
+        at = pl.ds(start, rows)
+        target = totals[0].at[which, at] if which < 2 else totals[1].at[at]
+        stores[n] = [moves.keep(total, target)]
+        if n % 2:
+            yield
+    for n in (len(jobs) - 2, len(jobs) - 1):
+        for copy in stores[n]:
+            copy.wait()
+
+
+def total_buffers(half, hidden_width, down_half, width, dtype):
+    shapes = [(half // 4, hidden_width)] * 5 + [(down_half // 4, width)] * 5
+    return [pltpu.VMEM(shape, dtype) for shape in shapes * 2]
+
+
+def sum_kernel(line, plans, arrays, *refs):
     count = len(plans)
-    given = sum(len(order) for plan in plans for order in plan)
-    grads, refs = refs[:given], refs[given:]
-    moved, refs = refs[: len(ways)], refs[len(ways) :]
-    sums, refs = refs[:count], refs[count:]
-    arrived, refs = refs[: len(ways)], refs[len(ways) :]
+    grads, refs = refs[:arrays], refs[arrays:]
+    owns, crossed, arrived, refs = refs[:3], refs[3:6], refs[6:8], refs[8:]
+    sums, refs = refs[:arrays], refs[arrays:]
+    totals, refs = refs[:2], refs[2:]
+    buffers, refs = refs[:20], refs[20:]
     kept, refs = refs[: 3 * count], refs[3 * count :]
     core_in, refs = refs[: 3 * count], refs[3 * count :]
     first_in, refs = refs[: 3 * count], refs[3 * count :]
@@ -477,8 +599,8 @@
         for o, pieces in enumerate(plan):
             mine, theirs = [], []
             start = 0
-            for first, width in pieces:
-                ref = grads[at]
+            for which, first, width in pieces:
+                ref = grads[which]
                 source = slice(first, first + width)
                 target = slice(start, start + width)
                 mine.append(
@@ -498,9 +620,6 @@
                 start += width
             loads.append(mine)
             swaps.append(theirs)
-
-    for way, source, target in zip(ways, moved, arrived):
-        moves.start(source, target, way, later=True)
 
     def add(target, source):
         lead = target.shape[:-2]
@@ -558,33 +677,32 @@
                 copy.wait()
                 held[dim] = own
                 add(region(), box)
-        start = sum(sum(width for _, width in pieces) for pieces in plans[n][:o])
-        width = sum(width for _, width in plans[n][o])
-        result = moves.keep(region(), sums[n].at[:, slice(start, start + width)])
+        results, start = [], 0
+        for which, first, width in plans[n][o]:
+            source = region().at[:, slice(start, start + width)]
+            results.append(moves.keep(source, sums[which].at[:, slice(first, first + width)]))
+            start += width
         yield
-        result.wait()
-
-    in_turn([chain(n, o) for n in range(count) for o in range(3)])
-    moves.finish()
-
-
-def sum_all(experts, grads, plans, moved, ways):
+        for result in results:
+            result.wait()
+
+    chains = [chain(n, o) for n in range(count) for o in range(3)]
+    chains.append(total_chain(moves, owns, crossed, arrived, totals, buffers))
+    in_turn(chains)
+
+
+def sum_all(experts, grads, plans, owns, crossed, arrived):
     line = experts // PLANE
     half, rest = line // 2, (line - 1) // 2
     rows = grads[0].shape[0] // (2 * experts)
     dtype = grads[0].dtype
-    operands, kernel_plans, shapes = [], [], []
+    operands = [array.reshape(2, line, 2, 2, rows, array.shape[1]) for array in grads]
+    shapes = [jax.ShapeDtypeStruct((rows, array.shape[1]), dtype) for array in grads]
     boxes = [[], [], [], [], []]
     for plan in plans:
-        kernel_plan = []
         for o, pieces in enumerate(plan):
-            for which, _, _ in pieces:
-                array = grads[which]
-                operands.append(array.reshape(2, line, 2, 2, rows, array.shape[1]))
-            kernel_plan.append(tuple((first, width) for _, first, width in pieces))
-            width = sum(width for _, _, width in pieces)
             steps = half + rest
-            block = (rows, width)
+            block = (rows, sum(width for _, _, width in pieces))
             boxes[0].append((line, 2, 2) + block)
             boxes[1].append((line, 2, 2) + block)
             if o == 0:
@@ -595,23 +713,26 @@
                 inboxes = [(steps, 2, 2), (2,), ()]
             for i, lead in enumerate(inboxes):
                 boxes[2 + i].append(lead + block)
-        kernel_plans.append(tuple(kernel_plan))
-        total = sum(width for pieces in kernel_plan for _, width in pieces)
-        shapes.append(jax.ShapeDtypeStruct((rows, total), dtype))
     count = len(plans)
-    number = len(operands) + 3 * count * (line + 1) + len(moved)
-    shapes += [jax.ShapeDtypeStruct(array.shape, array.dtype) for array in moved]
+    given = sum(len(pieces) for plan in plans for pieces in plan)
+    number = given + 3 * count * (line + 1)
+    others = list(owns) + list(crossed) + list(arrived)
+    shapes += [
+        jax.ShapeDtypeStruct((2,) + owns[0].shape, dtype),
+        jax.ShapeDtypeStruct(owns[2].shape, dtype),
+    ]
     return pl.pallas_call(
-        functools.partial(sum_kernel, line, tuple(kernel_plans), ways),
+        functools.partial(sum_kernel, line, plans, len(grads)),
         out_shape=shapes,
-        in_specs=hbm(len(operands) + len(moved)),
-        out_specs=hbm(count + len(moved)),
-        scratch_shapes=[pltpu.VMEM(shape, dtype) for kind in boxes for shape in kind]
-        + semaphores(number, len(operands) + 3 * count),
+        in_specs=hbm(len(operands) + len(others)),
+        out_specs=hbm(len(grads) + 2),
+        scratch_shapes=total_buffers(*owns[0].shape, *owns[2].shape, dtype)
+        + [pltpu.VMEM(shape, dtype) for kind in boxes for shape in kind]
+        + semaphores(number, 2 * given + 12 * 7),
         compiler_params=pltpu.CompilerParams(
             collective_id=2, has_side_effects=True, vmem_limit_bytes=60 * 1024 * 1024
         ),
-    )(*operands, *moved)
+    )(*operands, *others)
 
 
 def turn(values, cosine, sine_table):
@@ -1100,6 +1221,7 @@
     gating_live = jnp.where(member, gating, 0.0)
     gate_words = jnp.concatenate(split_words(gating_live), axis=1)
     line_rows = jnp.concatenate([normed_two, widen(gate_words)], axis=0)
+    line_rows = after(line_rows, [line_grads[1], line_grads[-1]])
     rising, falling, *weights = second_exchange(experts, line_rows, pairs, downs)
     line_rows = grid.line_gather(line_rows, rising, falling)
     weights = [part.reshape(PLANE, -1, part.shape[-1]) for part in weights]
@@ -1129,17 +1251,8 @@
     routed_result = sum(
         (grid.shift(part, -r) if r else part).astype(full) for r, part in enumerate(result_parts)
     )
-    owns, crossed, far = third_exchange(experts, after(kept, last))
-    near_x = [add_low(*pair) for pair in zip(owns[1], crossed[1])]
-    near_y = [add_low(*pair) for pair in zip(owns[2], crossed[2])]
-    edge = far[2].shape[0]
-    near_x[0] = add_low(near_x[0], far[0])
-    near_y[1] = add_low(near_y[1], far[1])
-    near_x[2] = jnp.concatenate([add_low(near_x[2][:edge], far[2]), near_x[2][edge:]], axis=0)
-    near_y[2] = jnp.concatenate([near_y[2][:edge], add_low(near_y[2][edge:], far[3])], axis=0)
-    arrived = []
-    for (gate, up, down), flip in ((near_x, 1), (near_y, 2)):
-        arrived.append(grid.swap(jnp.stack([gate, up, down.reshape(up.shape)]), flip))
+    owns, crossed, nears = third_exchange(experts, after(kept, last))
+    arrived = [grid.swap(part, flip) for part, flip in zip(nears, (1, 2))]
     gate_grads = routed_grad[tokens:]
     routed_grad = routed_grad[:tokens]
     grad_gating = (
@@ -1216,68 +1329,23 @@
         ],
         axis=1,
     )
-    cut = 7 * 128
-    summed_one, summed_two = sum_all(
+    *sums, total_in, total_down = sum_all(
         experts,
         grads_attention + grads_shared + [grad_extra],
-        [
-            [
-                [(0, 0, model_width), (2, 0, cut)],
-                [(1, 0, model_width), (7, 0, extra_width)],
-                [(2, cut, model_width - cut)],
-            ],
-            [
-                [(4, 0, hidden_width), (5, 0, hidden_width)],
-                [(3, 0, model_width)],
-                [(6, 0, hidden_width)],
-            ],
-        ],
-        [],
-        (),
-    )
-    summed_one, summed_two = summed_one.astype(full), summed_two.astype(full)
-
+        sum_plans(model_width, hidden_width, extra_width),
+        owns,
+        crossed,
+        arrived,
+    )
     output = (hidden + shared_result + routed_result).astype(low)
 
-    arrived = after(arrived, summed_one)
-    summed_expert_in = jnp.stack(
-        [
-            sum(
-                part.astype(full)
-                for part in (owns[0][i], crossed[0][i], arrived[0][i], arrived[1][i])
-            )
-            for i in range(2)
-        ]
-    )[None]
-    brought = add_low(arrived[0][2], arrived[1][2]).reshape(owns[0][2].shape)
-    summed_expert_down = sum(
-        part.astype(full) for part in (owns[0][2], crossed[0][2], brought)
-    )[None]
-
-    def take(array, start, width):
-        return array[:, start : start + width]
-
-    at = model_width + cut
-    summed_value = jnp.concatenate(
-        [
-            take(summed_one, model_width, cut),
-            take(summed_one, at + model_width + extra_width, model_width - cut),
-        ],
-        axis=1,
-    )
-    summed_in = jnp.stack(
-        [take(summed_one, 0, model_width).T, take(summed_one, at, model_width).T, summed_value.T],
-        axis=0,
-    )
-    at = at + model_width
-    summed_router = take(summed_one, at, experts)
-    summed_gains = take(summed_one, at + experts, 2).T
-    summed_shared_in = jnp.stack(
-        [take(summed_two, 0, hidden_width), take(summed_two, hidden_width, hidden_width)], axis=0
-    )
-    at = 2 * hidden_width
-    summed_out = take(summed_two, at, model_width).T
-    summed_shared_down = take(summed_two, at + model_width, hidden_width).T
+    sums = [part.astype(full) for part in sums]
+    summed_in = jnp.stack([part.T for part in sums[:3]], axis=0)
+    summed_out = sums[3].T
+    summed_shared_in = jnp.stack(sums[4:6], axis=0)
+    summed_shared_down = sums[6].T
+    summed_router = sums[7][:, :experts]
+    summed_gains = sums[7][:, experts : experts + 2].T
     upd_attn_in = advance(
         attention_in, attention_in_momentum, attention_in_average, summed_in, rate_attention_in
     )
@@ -1295,10 +1363,18 @@
         norm_gains, norm_gains_momentum, norm_gains_average, summed_gains, rate_gains
     )
     upd_expert_in = advance(
-        expert_in, expert_in_momentum, expert_in_average, summed_expert_in, rate_expert_in
+        expert_in,
+        expert_in_momentum,
+        expert_in_average,
+        total_in.astype(full)[None],
+        rate_expert_in,
     )
     upd_expert_down = advance(
-        expert_down, expert_down_momentum, expert_down_average, summed_expert_down, rate_expert_down
+        expert_down,
+        expert_down_momentum,
+        expert_down_average,
+        total_down.astype(full)[None],
+        rate_expert_down,
     )
     return (
         output,

time: 672 us -> 644 us (0.958)
  other arithmetic: 84.1 us -> 55.5 us
  local copies, waits for them, and re-layouts: 41.5 us -> 31 us
  waiting for transfers between devices: 16.7 us -> 25.4 us
    another operation x10 -> x2, other arithmetic: 16.9 us -> 1.13 us  [the longest x6 8.92 us: local(): jnp.stack([gate, up, down.reshape(up.shape)])]
    ppermute x10, waiting for transfers between devices: 0.03 us -> 10.4 us  [shift(): return lax.ppermute(block, 'expert', pairs)]
    convert_element_type x7 -> x1, other arithmetic: 7.92 us -> 0.71 us  [local(): sums = [part.astype(full) for part in sums]]
    unnamed x175 -> x137, local copies, waits for them, and re-layouts: 15.9 us -> 18.1 us
  transfers between devices with their start and end apart: 15 -> 15, of which waited for: 2 -> 5; matrix products, arithmetic and copies ran while one was open for 20% -> 15% of each run, Pallas kernels for 55% -> 50%
where the time goes in v4:
time: 644 us; the launch traced here: 636 us
  Pallas kernels  453 us (70%)
  other arithmetic  55.5 us (9%)
  matrix products  34.2 us (5%)
  local copies, waits for them, and re-layouts  31 us (5%)
  waiting for transfers between devices  25.4 us (4%)
  starting transfers between devices  21 us (3%)
  between operations  15.8 us (2%)
    pallas_call x1, Pallas kernels, sum_all(): pl.pallas_call(functools.partial(sum_kernel, line, plans, len(grads)), ou...  125 us
    pallas_call x1, Pallas kernels, first_exchange(): pl.pallas_call(functools.partial(first_kernel, line, plans), out_shape=[j...  88.3 us
    pallas_call x2, Pallas kernels, run_experts(): pl.pallas_call(functools.partial(expert_kernel, count), grid_spec=pltpu.P...  87.5 us
    pallas_call x1, Pallas kernels, third_exchange(): pl.pallas_call(functools.partial(third_kernel, line, len(kept)), out_shap...  60.7 us
    pallas_call x1, Pallas kernels, second_exchange(): pl.pallas_call(functools.partial(second_kernel, line), out_shape=[jax.Sha...  46 us
    pallas_call x1, Pallas kernels, attend_back(): pl.pallas_call(attend_back_kernel, grid=(steps,), in_specs=[whole(tokens,...  26.9 us
    add x8, other arithmetic, advance(): average_new = average + (weight_new - average) / (STEP + 1)  22 us
    pallas_call x1, Pallas kernels, attend(): pl.pallas_call(functools.partial(attend_kernel, steps), grid=(steps,), in...  18.8 us
  transfers between devices with their start and end apart: 15, of which 5 were waited for; matrix products, arithmetic and copies ran while one was open for 15% of the time, Pallas kernels for 50%

profile of v4, /device:TPU:0, one launch (start us, length us, event | category | flops | bytes accessed | tf_op | source)
XLA Modules:
  0.0 635.8 jit_solution(17806694529332236918)
XLA Ops:
  10.1 2.8 convert_bitcast_fusion.1.refs_2_.refs_4_
  14.2 4.0 convert_bitcast_fusion.refs_1_
  20.2 88.3 %shard_map.476 = (bf16[2,4,2,2,40,3968]{5,4,3,2,1,0:T(8,128)(2,1)}, bf16[2,4,2,2,40,1280]{5,4,3,2,1,0:T(8,128)(2,1)}, bf16[448,1280]{1,0:T(8,128)(2,1)}, bf16[448,1280]{1,0:T(8,128)(2,1)}) custom-call(bf16[40,3968]{1,0:T(8,128)(2,1)} %concatenate.25.refs_0_, bf16[40,1280]{1,0:T(8,128)(2,1)} %convert_bitcast_fusion.3.refs_1_, ...), custom_call_target="tpu_custom_call" | custom-call | tf_op jit(solution)/shard_map/pallas_call | solution.py:269
  109.1 3.4 collective-permute-start.1
  119.6 18.8 %shard_map.477 = (bf16[384,1280]{1,0:T(8,128)(2,1)S(1)}, bf16[384,1280]{1,0:T(8,128)(2,1)S(1)}, bf16[384,1280]{1,0:T(8,128)(2,1)S(1)}, bf16[384,1280]{1,0:T(8,12...) custom-call(bf16[384,1280]{1,0:T(8,128)(2,1)} %fusion.18.normed, bf16[1280,3968]{1,0:T(8,128)(2,1)} %bitcast.111, ...), custom_call_target="tpu_custom_call" | custom-call | flops 5033164800 | bytes 32768000 | tf_op jit(solution)/shard_map/pallas_call | solution.py:810
  145.6 10.4 %collective-permute-done.1.refs_3_ = bf16[400,1280]{1,0:T(8,128)(2,1)} collective-permute-done((bf16[400,1280]{1,0:T(8,128)(2,1)}, bf16[400,1280]{1,0:T(8,128)(2,1)}, u32[]{:S(2)}, u32[]{:S(2)}) %collective-permute-start.1) | collective-permute-done | bytes 1024032 | tf_op jit(solution)/shard_map/ppermute | solution.py:1094
  155.9 8.4 %collective-permute-done.2.refs_2_ = bf16[2,640,896]{2,1,0:T(8,128)(2,1)} collective-permute-done((bf16[2,640,896]{2,1,0:T(8,128)(2,1)}, bf16[2,640,896]{2,1,0:T(8,128)(2,1)}, u32[]{:S(2)}, u32[]{:S(2)}) %collective-permute-start.2) | collective-permute-done | bytes 2293792 | tf_op jit(solution)/shard_map/ppermute | solution.py:1098
  165.4 46.0 %shard_map.478 = (bf16[400,1280]{1,0:T(8,128)(2,1)}, bf16[400,1280]{1,0:T(8,128)(2,1)}, bf16[4,2,640,896]{3,2,1,0:T(8,128)(2,1)}, bf16[4,2,640,896]{3,2,1,0:T(8,128)(2,1)}, bf16[4,2,448,1280]{3,2,1,0:T(8,128)(2,1)}) custom-call(bf16[400,1280]{1,0:T(8,128)(2,1)} %pad_maximum_fusion.refs_0_, bf16[2,640,896]{2,1,0:T(8,128)(2,1)} %convert_bitcast_fusion.refs_1_, ...), custom_call_target="tpu_custom_call" | custom-call | tf_op jit(solution)/shard_map/pallas_call | solution.py:329
  211.5 3.2 collective-permute-start.4
  220.9 43.7 %shard_map.479 = (bf16[400,1280]{1,0:T(8,128)(2,1)}, bf16[400,1280]{1,0:T(8,128)(2,1)}, bf16[384,1280]{1,0:T(8,128)(2,1)}, bf16[384,1280]{1,0:T(8,128)(2,1)}, bf...) custom-call(s32[4]{0:T(128)} %copy-done.61, ...), custom_call_target="tpu_custom_call" | custom-call | flops 23655874560 | bytes 27525120 | tf_op jit(solution)/shard_map/pallas_call | solution.py:1024
  264.6 1.8 collective-permute-start.6
  272.6 43.8 %shard_map.480 = (bf16[400,1280]{1,0:T(8,128)(2,1)}, bf16[400,1280]{1,0:T(8,128)(2,1)}, bf16[384,1280]{1,0:T(8,128)(2,1)}, bf16[384,1280]{1,0:T(8,128)(2,1)}, bf...) custom-call(s32[4]{0:T(128)} %copy-done.61, ...), custom_call_target="tpu_custom_call" | custom-call | flops 23655874560 | bytes 27525120 | tf_op jit(solution)/shard_map/pallas_call | solution.py:1024
  316.4 2.4 collective-permute-start.7
  329.7 60.7 %shard_map.482 = (bf16[640,896]{1,0:T(8,128)(2,1)}, bf16[640,896]{1,0:T(8,128)(2,1)}, bf16[448,1280]{1,0:T(8,128)(2,1)}, bf16[640,896]{1,0:T(8,128)(2,1)}, bf16[...) custom-call(bf16[4,384,1280]{2,1,0:T(8,128)(2,1)} %get-tuple-element.162, ...), custom_call_target="tpu_custom_call" | custom-call | tf_op jit(solution)/shard_map/pallas_call | solution.py:476
  390.4 2.1 collective-permute-start.12
  392.5 2.6 convert_add_fusion.4
  398.4 2.8 collective-permute-start.11
  402.2 3.0 fusion.10
  411.5 2.7 multiply_reduce_fusion
  414.2 1.9 fusion.91
  417.0 26.9 %shard_map.481 = (bf16[1280,1280]{1,0:T(8,128)(2,1)}, bf16[1280,1280]{1,0:T(8,128)(2,1)}, bf16[1280,1280]{1,0:T(8,128)(2,1)}, bf16[1280,1280]{1,0:T(8,128)(2,1)}, f32[384,1280]{1,0:T(8,128)}) custom-call(bf16[384,1280]{1,0:T(8,128)(2,1)S(1)} %get-tuple-element.324.grad_branch, bf16[384,1280]{1,0:T(8,128)(2,1)S(1)} %copy-done, ...), custom_call_target="tpu_custom_call" | custom-call | flops 10066329600 | bytes 65536000 | tf_op jit(solution)/shard_map/pallas_call | solution.py:904
  443.9 2.1 fusion.23
  446.5 2.8 fusion.2
  449.2 4.3 copy.126
  453.5 4.0 convolution_convert_fusion.2
  457.6 2.9 convolution_convert_fusion.1
  461.5 4.0 collective-permute-done.12.refs_14_
  467.0 124.7 %shard_map.483 = (bf16[40,1280]{1,0:T(8,128)(2,1)}, bf16[40,1280]{1,0:T(8,128)(2,1)}, bf16[40,1280]{1,0:T(8,128)(2,1)}, bf16[40,1280]{1,0:T(8,128)(2,1)}, bf16[4...) custom-call(bf16[2,4,2,2,40,1280]{5,4,3,2,1,0:T(8,128)(2,1)} %bitcas, ...), custom_call_target="tpu_custom_call" | custom-call | tf_op jit(solution)/shard_map/pallas_call | solution.py:724
  592.5 7.0 %multiply_add_fusion.1 = (f32[1,448,1280]{2,1,0:T(8,128)}, f32[1,448,1280]{2,1,0:T(8,128)}, f32[1,448,1280]{2,1,0:T(8,128)}) fusion(f32[1,448,1280]{2,1,0:T(8,128)} %param.57, f32[1,448,1280]{2,1,0:T(8,128)} %param.55, bf16[448,1280]{1,0:T(8,128)(2,1)} %get-tuple-element.189, f32[1,448,1280]{2,1,0:T(8,128)} %param.56), kind=kLoop, calls=%fused_computation.21 | loop fusion | flops 5734400 | bytes 14909440 | tf_op jit(solution)/shard_map/add | solution.py:55
  606.3 4.3 convolution_add_fusion.2
  614.6 10.8 %multiply_add_fusion = (f32[1,2,640,896]{3,2,1,0:T(8,128)}, f32[1,2,640,896]{3,2,1,0:T(8,128)}, f32[1,2,640,896]{3,2,1,0:T(8,128)}) fusion(f32[1,2,640,896]{3,2,1,0:T(8,128)} %param.54, f32[1,2,640,896]{3,2,1,0:T(8,128)} %param.52, bf16[2,640,896]{2,1,0:T(8,128)(2,1)} %get-tuple-element.188, f32[1,2,640,896]{3,2,1,0:T(8,128)} %param.53), kind=kLoop, calls=%fused_computation.4 | loop fusion | flops 11468800 | bytes 29818880 | tf_op jit(solution)/shard_map/add | solution.py:55
  625.5 3.3 add_convert_fusion
  (238 shorter events, 70.3 us)
Async XLA Ops:
  7.2 395.0 %all-gather.2.cloned.1.call-start = ((), (), s32[]{:S(2)}) async-start(), calls=%async_computation | async-start | bytes 7096320 | tf_op jit(solution)/shard_map/all_gather | solution.py:1269
  20.2 96.0 %copy-start.10 = (bf16[384,1280]{1,0:T(8,128)(2,1)S(1)}, bf16[384,1280]{1,0:T(8,128)(2,1)}, u32[]{:S(2)}) copy-start(bf16[384,1280]{1,0:T(8,128)(2,1)} %inputs.1) | copy-start | bytes 2949124
  108.6 37.0 %collective-permute-start = (bf16[400,1280]{1,0:T(8,128)(2,1)}, bf16[400,1280]{1,0:T(8,128)(2,1)}, u32[]{:S(2)}, u32[]{:S(2)}) collective-permute-start(bf16[400,1280]{1,0:T(8,128)(2,1)} %fusion.29.refs_2_), channel_id=1, source_target_pairs={{0,4},{1,5},{2,6},{3,7},{4,8},{5,9},{6,10},{7,11},{8,12},{9,13},{1... | collective-permute-start | bytes 3072008 | tf_op jit(solution)/shard_map/ppermute | solution.py:1094
  109.1 46.9 %collective-permute-start.1 = (bf16[400,1280]{1,0:T(8,128)(2,1)}, bf16[400,1280]{1,0:T(8,128)(2,1)}, u32[]{:S(2)}, u32[]{:S(2)}) collective-permute-start(bf16[400,1280]{1,0:T(8,128)(2,1)} %fusion.29.refs_2_), channel_id=1, source_target_pairs={{0,12},{1,13},{2,14},{3,15},{4,0},{5,1},{6,2},{7,3},{8,4},{9,5},{1... | collective-permute-start | bytes 3072008 | tf_op jit(solution)/shard_map/ppermute | solution.py:1094
  112.4 51.9 %collective-permute-start.2 = (bf16[2,640,896]{2,1,0:T(8,128)(2,1)}, bf16[2,640,896]{2,1,0:T(8,128)(2,1)}, u32[]{:S(2)}, u32[]{:S(2)}) collective-permute-start(bf16[2,640,896]{2,1,0:T(8,128)(2,1)} %convert_bitcast_fusion.refs_1_), channel_id=1, source_target_pairs={{0,1},{1,0},{2,3},{3,2},{4,5},{5,4},{6,7},{7,6},{8,9},{9,8},{10,11... | collective-permute-start | bytes 6881288 | tf_op jit(solution)/shard_map/ppermute | solution.py:1098
  113.8 51.6 %collective-permute-start.3 = (bf16[2,640,896]{2,1,0:T(8,128)(2,1)}, bf16[2,640,896]{2,1,0:T(8,128)(2,1)}, u32[]{:S(2)}, u32[]{:S(2)}) collective-permute-start(bf16[2,640,896]{2,1,0:T(8,128)(2,1)} %convert_bitcast_fusion.refs_1_), channel_id=1, source_target_pairs={{0,2},{1,3},{2,0},{3,1},{4,6},{5,7},{6,4},{7,5},{8,10},{9,11},{10,... | collective-permute-start | bytes 6881288 | tf_op jit(solution)/shard_map/ppermute | solution.py:1098
  119.6 24.2 %copy-start.31 = (f32[896,40]{0,1:T(8,128)S(1)}, f32[896,40]{0,1:T(8,128)}, u32[]{:S(2)}) copy-start(f32[896,40]{0,1:T(8,128)} %param.43) | copy-start | bytes 430084
  143.7 67.7 %copy-start.51 = (f32[384]{0:T(512)}, f32[384]{0:T(512)S(1)}, u32[]{:S(2)}) copy-start(f32[384]{0:T(512)S(1)} %fusion.63) | copy-start | bytes 4612
  211.5 9.4 %copy-start.61 = (s32[4]{0:T(128)}, s32[4]{0:T(128)S(1)}, u32[]{:S(2)}) copy-start(s32[4]{0:T(128)S(1)} %xor_add_fusion.numbers) | copy-start | bytes 52
  211.5 55.0 %collective-permute-start.5 = (bf16[400,1280]{1,0:T(8,128)(2,1)}, bf16[400,1280]{1,0:T(8,128)(2,1)}, u32[]{:S(2)}, u32[]{:S(2)}) collective-permute-start(bf16[400,1280]{1,0:T(8,128)(2,1)} %collective-permute-done.refs_3_), channel_id=1, source_target_pairs={{0,4},{1,5},{2,6},{3,7},{4,8},{5,9},{6,10},{7,11},{8,12},{9,13},{1... | collective-permute-start | bytes 3072008 | tf_op jit(solution)/shard_map/ppermute | solution.py:1094
  211.5 54.9 %collective-permute-start.4 = (bf16[400,1280]{1,0:T(8,128)(2,1)}, bf16[400,1280]{1,0:T(8,128)(2,1)}, u32[]{:S(2)}, u32[]{:S(2)}) collective-permute-start(bf16[400,1280]{1,0:T(8,128)(2,1)} %get-tuple-element.123.refs_1_), channel_id=1, source_target_pairs={{0,4},{1,5},{2,6},{3,7},{4,8},{5,9},{6,10},{7,11},{8,12},{9,13},{1... | collective-permute-start | bytes 3072008 | tf_op jit(solution)/shard_map/ppermute | solution.py:1094
  264.6 127.9 %collective-permute-start.6 = (bf16[400,1280]{1,0:T(8,128)(2,1)}, bf16[400,1280]{1,0:T(8,128)(2,1)}, u32[]{:S(2)}, u32[]{:S(2)}) collective-permute-start(bf16[400,1280]{1,0:T(8,128)(2,1)} %get-tuple-element.130), channel_id=1, source_target_pairs={{0,12},{1,13},{2,14},{3,15},{4,0},{5,1},{6,2},{7,3},{8,4},{9,5},{1... | collective-permute-start | bytes 3072008 | tf_op jit(solution)/shard_map/ppermute | solution.py:1094
  316.4 76.1 %collective-permute-start.7 = (bf16[400,1280]{1,0:T(8,128)(2,1)}, bf16[400,1280]{1,0:T(8,128)(2,1)}, u32[]{:S(2)}, u32[]{:S(2)}) collective-permute-start(bf16[400,1280]{1,0:T(8,128)(2,1)} %get-tuple-element.137), channel_id=1, source_target_pairs={{0,8},{1,9},{2,10},{3,11},{4,12},{5,13},{6,14},{7,15},{8,0},{9,1},... | collective-permute-start | bytes 3072008 | tf_op jit(solution)/shard_map/ppermute | solution.py:1094
  318.9 73.7 %collective-permute-start.8 = (bf16[400,1280]{1,0:T(8,128)(2,1)}, bf16[400,1280]{1,0:T(8,128)(2,1)}, u32[]{:S(2)}, u32[]{:S(2)}) collective-permute-start(bf16[400,1280]{1,0:T(8,128)(2,1)} %get-tuple-element.138), channel_id=1, source_target_pairs={{0,4},{1,5},{2,6},{3,7},{4,8},{5,9},{6,10},{7,11},{8,12},{9,13},{1... | collective-permute-start | bytes 3072008 | tf_op jit(solution)/shard_map/ppermute | solution.py:1094
  390.4 75.2 %collective-permute-start.12 = (bf16[1952,896]{1,0:T(8,128)(2,1)}, bf16[1952,896]{1,0:T(8,128)(2,1)}, u32[]{:S(2)}, u32[]{:S(2)}) collective-permute-start(bf16[1952,896]{1,0:T(8,128)(2,1)} %get-tuple-element.178), channel_id=1, source_target_pairs={{0,1},{1,0},{2,3},{3,2},{4,5},{5,4},{6,7},{7,6},{8,9},{9,8},{10,11... | collective-permute-start | bytes 10493960 | tf_op jit(solution)/shard_map/ppermute | solution.py:1098
  392.4 74.6 %collective-permute-start.13 = (bf16[1952,896]{1,0:T(8,128)(2,1)}, bf16[1952,896]{1,0:T(8,128)(2,1)}, u32[]{:S(2)}, u32[]{:S(2)}) collective-permute-start(bf16[1952,896]{1,0:T(8,128)(2,1)} %get-tuple-element.179), channel_id=1, source_target_pairs={{0,2},{1,3},{2,0},{3,1},{4,6},{5,7},{6,4},{7,5},{8,10},{9,11},{10,... | collective-permute-start | bytes 10493960 | tf_op jit(solution)/shard_map/ppermute | solution.py:1098
  397.1 228.3 %collective-permute-start.10 = (bf16[384,1280]{1,0:T(8,128)(2,1)}, bf16[384,1280]{1,0:T(8,128)(2,1)}, u32[]{:S(2)}, u32[]{:S(2)}) collective-permute-start(bf16[384,1280]{1,0:T(8,128)(2,1)} %get-tuple-element.141), channel_id=1, source_target_pairs={{0,8},{1,9},{2,10},{3,11},{4,12},{5,13},{6,14},{7,15},{8,0},{9,1},... | collective-permute-start | bytes 2949128 | tf_op jit(solution)/shard_map/ppermute | solution.py:1094
  398.4 227.0 %collective-permute-start.11 = (bf16[384,1280]{1,0:T(8,128)(2,1)}, bf16[384,1280]{1,0:T(8,128)(2,1)}, u32[]{:S(2)}, u32[]{:S(2)}) collective-permute-start(bf16[384,1280]{1,0:T(8,128)(2,1)} %get-tuple-element.142), channel_id=1, source_target_pairs={{0,4},{1,5},{2,6},{3,7},{4,8},{5,9},{6,10},{7,11},{8,12},{9,13},{1... | collective-permute-start | bytes 2949128 | tf_op jit(solution)/shard_map/ppermute | solution.py:1094
  401.2 224.3 %collective-permute-start.9 = (bf16[384,1280]{1,0:T(8,128)(2,1)}, bf16[384,1280]{1,0:T(8,128)(2,1)}, u32[]{:S(2)}, u32[]{:S(2)}) collective-permute-start(bf16[384,1280]{1,0:T(8,128)(2,1)} %get-tuple-element.140), channel_id=1, source_target_pairs={{0,12},{1,13},{2,14},{3,15},{4,0},{5,1},{6,2},{7,3},{8,4},{9,5},{1... | collective-permute-start | bytes 2949128 | tf_op jit(solution)/shard_map/ppermute | solution.py:1094
  408.7 37.8 %copy-start.25 = (bf16[384,896]{1,0:T(8,128)(2,1)}, bf16[384,896]{1,0:T(8,128)(2,1)S(1)}, u32[]{:S(2)}) copy-start(bf16[384,896]{1,0:T(8,128)(2,1)S(1)} %get-tuple-element.328) | copy-start | bytes 2064388
  417.0 26.9 %copy-start.11 = (bf16[384,1280]{1,0:T(8,128)(2,1)S(1)}, bf16[384,1280]{1,0:T(8,128)(2,1)}, u32[]{:S(2)}) copy-start(bf16[384,1280]{1,0:T(8,128)(2,1)} %inputs.1) | copy-start | bytes 2949124
  417.0 26.9 %copy-start.54 = (f32[384]{0:T(512)S(1)}, f32[384]{0:T(512)}, u32[]{:S(2)}) copy-start(f32[384]{0:T(512)} %copy-done.53) | copy-start | bytes 4612
  592.4 7.1 %copy-start.35 = (f32[1280,40]{0,1:T(8,128)S(1)}, f32[1280,40]{0,1:T(8,128)}, u32[]{:S(2)}) copy-start(f32[1280,40]{0,1:T(8,128)} %param.39) | copy-start | bytes 614404
  592.4 7.1 %copy-start.36 = (f32[1280,40]{0,1:T(8,128)S(1)}, f32[1280,40]{0,1:T(8,128)}, u32[]{:S(2)}) copy-start(f32[1280,40]{0,1:T(8,128)} %param.38) | copy-start | bytes 614404
  592.4 7.1 %copy-start.42 = (bf16[40,1280]{1,0:T(8,128)(2,1)S(1)}, bf16[40,1280]{1,0:T(8,128)(2,1)}, u32[]{:S(2)}) copy-start(bf16[40,1280]{1,0:T(8,128)(2,1)} %get-tuple-element.183) | copy-start | bytes 307204
  592.4 8.0 %copy-start.32 = (f32[896,40]{0,1:T(8,128)S(1)}, f32[896,40]{0,1:T(8,128)}, u32[]{:S(2)}) copy-start(f32[896,40]{0,1:T(8,128)} %param.43) | copy-start | bytes 430084
  592.4 8.0 %copy-start.37 = (f32[896,40]{0,1:T(8,128)S(1)}, f32[896,40]{0,1:T(8,128)}, u32[]{:S(2)}) copy-start(f32[896,40]{0,1:T(8,128)} %param.45) | copy-start | bytes 430084
  592.5 8.0 %copy-start.38 = (f32[896,40]{0,1:T(8,128)S(1)}, f32[896,40]{0,1:T(8,128)}, u32[]{:S(2)}) copy-start(f32[896,40]{0,1:T(8,128)} %param.44) | copy-start | bytes 430084
  592.5 8.0 %copy-start.50 = (bf16[40,896]{1,0:T(8,128)(2,1)S(1)}, bf16[40,896]{1,0:T(8,128)(2,1)}, u32[]{:S(2)}) copy-start(bf16[40,896]{1,0:T(8,128)(2,1)} %get-tuple-element.186) | copy-start | bytes 215044
  592.5 8.8 %copy-start.13 = (f32[384,1280]{1,0:T(8,128)S(1)}, f32[384,1280]{1,0:T(8,128)}, u32[]{:S(2)}) copy-start(f32[384,1280]{1,0:T(8,128)} %get-tuple-element.147) | copy-start | bytes 5898244
  614.6 10.8 %copy-start.14 = (f32[384,1280]{1,0:T(8,128)S(1)}, f32[384,1280]{1,0:T(8,128)}, u32[]{:S(2)}) copy-start(f32[384,1280]{1,0:T(8,128)} %convolution_add_fusion.2) | copy-start | bytes 5898244
  614.6 10.9 %copy-start.22 = (bf16[384,1280]{1,0:T(8,128)(2,1)S(1)}, bf16[384,1280]{1,0:T(8,128)(2,1)}, u32[]{:S(2)}) copy-start(bf16[384,1280]{1,0:T(8,128)(2,1)} %get-tuple-element.139) | copy-start | bytes 2949124
  (46 other events, 115.2 us)
Sparse Core Ops, SparseCore 0:
  211.6 164.7 all-gather.1

commit v5 on v4

--- a/solution.py
+++ b/solution.py
@@ -493,21 +493,21 @@
 
 
 def sum_plans(width, hidden_width, extra_width):
-    edge = width * 8 // 10
-    half = width // 2
-    gate_edge = hidden_width * 5 // 7
+    edge, half = width * 6 // 10, width // 2
+    out_edge = width * 7 // 10
+    gate_edge, down_edge = hidden_width * 5 // 7, hidden_width * 4 // 7
     return (
         (((0, 0, edge),), ((1, 0, half),), ((0, edge, width - edge),)),
         (((2, 0, edge),), ((1, half, width - half),), ((2, edge, width - edge),)),
         (
-            ((3, 0, width - 128),),
+            ((3, 0, out_edge),),
             ((4, 0, gate_edge),),
-            ((3, width - 128, 128), (7, 0, extra_width)),
+            ((3, out_edge, width - out_edge), (7, 0, extra_width)),
         ),
         (
             ((5, 0, hidden_width), (4, gate_edge, hidden_width - gate_edge)),
-            ((6, 0, gate_edge),),
-            ((6, gate_edge, hidden_width - gate_edge),),
+            ((6, 0, down_edge),),
+            ((6, down_edge, hidden_width - down_edge),),
         ),
     )
 
@@ -1057,8 +1057,36 @@
 
 def gather_plan(units, orders):
     least, more = divmod(units, len(orders))
-    count = len(orders)
-    return tuple((order, 128 * (least + (i >= count - more))) for i, order in enumerate(orders))
+    widths = [least] * len(orders)
+    for i in sorted(range(len(orders)), key=lambda i: (-orders[i], -i))[:more]:
+        widths[i] += 1
+    if least > 2:
+        for i, order in enumerate(orders):
+            widths[i] += order - 1
+    return tuple((order, 128 * width) for order, width in zip(orders, widths))
+
+
+def shared_grads_kernel(rows, grad_gate, grad_up, grads, inner, gate_out, up_out, down_out):
+    low = jnp.bfloat16
+    gate_out[...] = dot_tn(rows[...], grad_gate[...]).astype(low)
+    up_out[...] = dot_tn(rows[...], grad_up[...]).astype(low)
+    down_out[...] = dot_tn(grads[...], inner[...]).astype(low)
+
+
+def shared_grads(rows, grad_gate, grad_up, grads, inner):
+    shape = jax.ShapeDtypeStruct((rows.shape[1], inner.shape[1]), jnp.bfloat16)
+    return pl.pallas_call(
+        shared_grads_kernel,
+        in_specs=[pl.BlockSpec(memory_space=pltpu.VMEM)] * 5,
+        out_specs=[pl.BlockSpec(memory_space=pltpu.VMEM)] * 3,
+        out_shape=[shape] * 3,
+        compiler_params=pltpu.CompilerParams(vmem_limit_bytes=32 * 1024 * 1024),
+        cost_estimate=pl.CostEstimate(
+            flops=6 * rows.size * inner.shape[1],
+            bytes_accessed=4 * rows.size + 6 * rows.shape[1] * inner.shape[1],
+            transcendentals=0,
+        ),
+    )(rows, grad_gate, grad_up, grads, inner)
 
 
 def split_words(values):
@@ -1296,11 +1324,9 @@
         - hidden * rstd_two**3 * jnp.mean(scaled_two * hidden, axis=-1, keepdims=True)
     )
     grad_branch = grad_hidden.astype(low)
-    grads_shared = [
-        dot_tn(normed_two, grad_shared_gate).astype(low),
-        dot_tn(normed_two, grad_shared_up).astype(low),
-        dot_tn(cotangent, shared_hidden).astype(low),
-    ]
+    grads_shared = shared_grads(
+        normed_two, grad_shared_gate, grad_shared_up, cotangent, shared_hidden
+    )
     *grads_attention, grad_normed_one = attend_back(
         grad_branch,
         normed_one,
@@ -1331,7 +1357,7 @@
     )
     *sums, total_in, total_down = sum_all(
         experts,
-        grads_attention + grads_shared + [grad_extra],
+        grads_attention + list(grads_shared) + [grad_extra],
         sum_plans(model_width, hidden_width, extra_width),
         owns,
         crossed,

time: 644 us -> 627 us (0.974)
  Pallas kernels: 453 us -> 442 us
  matrix products: 34.2 us -> 24.3 us
    pallas_call x1, Pallas kernels: 125 us -> 110 us  [sum_all(): pl.pallas_call(functools.partial(sum_kernel, line, plans, len(grads)), ou...]
    dot_general x3 -> x0, matrix products: 9.72 us -> none  [dot_tn(): lax.dot_general(a, b, (((0,), (0,)), ((), ())), preferred_element_type=jn...]
    unnamed x137 -> x133, local copies, waits for them, and re-layouts: 18.1 us -> 22.3 us
  transfers between devices with their start and end apart: 15 -> 15, of which waited for: 5 -> 5; matrix products, arithmetic and copies ran while one was open for 15% -> 13% of each run, Pallas kernels for 50% -> 50%
where the time goes in v5:
time: 627 us; the launch traced here: 618 us
  Pallas kernels  442 us (70%)
  other arithmetic  55.5 us (9%)
  local copies, waits for them, and re-layouts  30.9 us (5%)
  waiting for transfers between devices  30.2 us (5%)
  matrix products  24.3 us (4%)
  starting transfers between devices  19.7 us (3%)
  between operations  15.8 us (3%)
    pallas_call x1, Pallas kernels, sum_all(): pl.pallas_call(functools.partial(sum_kernel, line, plans, len(grads)), ou...  110 us
    pallas_call x2, Pallas kernels, run_experts(): pl.pallas_call(functools.partial(expert_kernel, count), grid_spec=pltpu.P...  87.5 us
    pallas_call x1, Pallas kernels, first_exchange(): pl.pallas_call(functools.partial(first_kernel, line, plans), out_shape=[j...  86.8 us
    pallas_call x1, Pallas kernels, third_exchange(): pl.pallas_call(functools.partial(third_kernel, line, len(kept)), out_shap...  62.3 us
    pallas_call x1, Pallas kernels, second_exchange(): pl.pallas_call(functools.partial(second_kernel, line), out_shape=[jax.Sha...  46.1 us
    pallas_call x1, Pallas kernels, attend_back(): pl.pallas_call(attend_back_kernel, grid=(steps,), in_specs=[whole(tokens,...  26.9 us
    unnamed x133, local copies, waits for them, and re-layouts  22.3 us
    add x8, other arithmetic, advance(): average_new = average + (weight_new - average) / (STEP + 1)  22 us
  transfers between devices with their start and end apart: 15, of which 5 were waited for; matrix products, arithmetic and copies ran while one was open for 13% of the time, Pallas kernels for 50%

profile of v5, /device:TPU:0, one launch (start us, length us, event | category | flops | bytes accessed | tf_op | source)
XLA Modules:
  0.0 618.5 jit_solution(7349183473421351290)
XLA Ops:
  10.1 2.8 convert_bitcast_fusion.1.refs_2_.refs_4_
  14.2 4.0 convert_bitcast_fusion.refs_1_
  20.2 86.8 %shard_map.476 = (bf16[2,4,2,2,40,3968]{5,4,3,2,1,0:T(8,128)(2,1)}, bf16[2,4,2,2,40,1280]{5,4,3,2,1,0:T(8,128)(2,1)}, bf16[448,1280]{1,0:T(8,128)(2,1)}, bf16[448,1280]{1,0:T(8,128)(2,1)}) custom-call(bf16[40,3968]{1,0:T(8,128)(2,1)} %concatenate.25.refs_0_, bf16[40,1280]{1,0:T(8,128)(2,1)} %convert_bitcast_fusion.3.refs_1_, ...), custom_call_target="tpu_custom_call" | custom-call | tf_op jit(solution)/shard_map/pallas_call | solution.py:269
  107.1 3.8 collective-permute-start.1
  117.5 18.9 %shard_map.477 = (bf16[384,1280]{1,0:T(8,128)(2,1)S(1)}, bf16[384,1280]{1,0:T(8,128)(2,1)S(1)}, bf16[384,1280]{1,0:T(8,128)(2,1)S(1)}, bf16[384,1280]{1,0:T(8,12...) custom-call(bf16[384,1280]{1,0:T(8,128)(2,1)} %fusion.17.normed, bf16[1280,3968]{1,0:T(8,128)(2,1)} %bitcast.106, ...), custom_call_target="tpu_custom_call" | custom-call | flops 5033164800 | bytes 32768000 | tf_op jit(solution)/shard_map/pallas_call | solution.py:810
  143.5 10.8 %collective-permute-done.1.refs_3_ = bf16[400,1280]{1,0:T(8,128)(2,1)} collective-permute-done((bf16[400,1280]{1,0:T(8,128)(2,1)}, bf16[400,1280]{1,0:T(8,128)(2,1)}, u32[]{:S(2)}, u32[]{:S(2)}) %collective-permute-start.1) | collective-permute-done | bytes 1024032 | tf_op jit(solution)/shard_map/ppermute | solution.py:1122
  154.3 8.5 %collective-permute-done.2.refs_2_ = bf16[2,640,896]{2,1,0:T(8,128)(2,1)} collective-permute-done((bf16[2,640,896]{2,1,0:T(8,128)(2,1)}, bf16[2,640,896]{2,1,0:T(8,128)(2,1)}, u32[]{:S(2)}, u32[]{:S(2)}) %collective-permute-start.2) | collective-permute-done | bytes 2293792 | tf_op jit(solution)/shard_map/ppermute | solution.py:1126
  163.1 46.1 %shard_map.478 = (bf16[400,1280]{1,0:T(8,128)(2,1)}, bf16[400,1280]{1,0:T(8,128)(2,1)}, bf16[4,2,640,896]{3,2,1,0:T(8,128)(2,1)}, bf16[4,2,640,896]{3,2,1,0:T(8,128)(2,1)}, bf16[4,2,448,1280]{3,2,1,0:T(8,128)(2,1)}) custom-call(bf16[400,1280]{1,0:T(8,128)(2,1)} %pad_maximum_fusion.refs_0_, bf16[2,640,896]{2,1,0:T(8,128)(2,1)} %convert_bitcast_fusion.refs_1_, ...), custom_call_target="tpu_custom_call" | custom-call | tf_op jit(solution)/shard_map/pallas_call | solution.py:329
  209.3 3.2 collective-permute-start.4
  218.6 43.7 %shard_map.479 = (bf16[400,1280]{1,0:T(8,128)(2,1)}, bf16[400,1280]{1,0:T(8,128)(2,1)}, bf16[384,1280]{1,0:T(8,128)(2,1)}, bf16[384,1280]{1,0:T(8,128)(2,1)}, bf...) custom-call(s32[4]{0:T(128)} %copy-done.60, ...), custom_call_target="tpu_custom_call" | custom-call | flops 23655874560 | bytes 27525120 | tf_op jit(solution)/shard_map/pallas_call | solution.py:1024
  262.4 1.8 collective-permute-start.6
  270.4 43.8 %shard_map.480 = (bf16[400,1280]{1,0:T(8,128)(2,1)}, bf16[400,1280]{1,0:T(8,128)(2,1)}, bf16[384,1280]{1,0:T(8,128)(2,1)}, bf16[384,1280]{1,0:T(8,128)(2,1)}, bf...) custom-call(s32[4]{0:T(128)} %copy-done.60, ...), custom_call_target="tpu_custom_call" | custom-call | flops 23655874560 | bytes 27525120 | tf_op jit(solution)/shard_map/pallas_call | solution.py:1024
  314.2 2.3 collective-permute-start.7
  325.0 1.8 multiply_reduce_fusion.2
  327.4 62.3 %shard_map.483 = (bf16[640,896]{1,0:T(8,128)(2,1)}, bf16[640,896]{1,0:T(8,128)(2,1)}, bf16[448,1280]{1,0:T(8,128)(2,1)}, bf16[640,896]{1,0:T(8,128)(2,1)}, bf16[...) custom-call(bf16[4,384,1280]{2,1,0:T(8,128)(2,1)} %get-tuple-element.168, ...), custom_call_target="tpu_custom_call" | custom-call | tf_op jit(solution)/shard_map/pallas_call | solution.py:476
  389.7 2.0 collective-permute-start.13
  391.8 2.6 convert_add_fusion.4
  397.0 2.6 collective-permute-start.11
  400.8 3.0 fusion.9
  405.7 1.5 multiply_convert_fusion
  410.0 2.6 multiply_reduce_fusion
  412.7 1.9 fusion.90
  415.4 26.9 %shard_map.481 = (bf16[1280,1280]{1,0:T(8,128)(2,1)}, bf16[1280,1280]{1,0:T(8,128)(2,1)}, bf16[1280,1280]{1,0:T(8,128)(2,1)}, bf16[1280,1280]{1,0:T(8,128)(2,1)}, f32[384,1280]{1,0:T(8,128)}) custom-call(bf16[384,1280]{1,0:T(8,128)(2,1)S(1)} %get-tuple-element.330.grad_branch, bf16[384,1280]{1,0:T(8,128)(2,1)S(1)} %copy-done, ...), custom_call_target="tpu_custom_call" | custom-call | flops 10066329600 | bytes 65536000 | tf_op jit(solution)/shard_map/pallas_call | solution.py:904
  442.4 2.1 fusion.22
  445.0 4.0 shard_map.482
  454.2 10.6 %collective-permute-done.12.refs_14_ = bf16[1952,896]{1,0:T(8,128)(2,1)} collective-permute-done((bf16[1952,896]{1,0:T(8,128)(2,1)}, bf16[1952,896]{1,0:T(8,128)(2,1)}, u32[]{:S(2)}, u32[]{:S(2)}) %collective-permute-start.12) | collective-permute-done | bytes 3498016 | tf_op jit(solution)/shard_map/ppermute | solution.py:1126
  464.9 109.6 %shard_map.484 = (bf16[40,1280]{1,0:T(8,128)(2,1)}, bf16[40,1280]{1,0:T(8,128)(2,1)}, bf16[40,1280]{1,0:T(8,128)(2,1)}, bf16[40,1280]{1,0:T(8,128)(2,1)}, bf16[4...) custom-call(bf16[2,4,2,2,40,1280]{5,4,3,2,1,0:T(8,128)(2,1)} %bitcas, ...), custom_call_target="tpu_custom_call" | custom-call | tf_op jit(solution)/shard_map/pallas_call | solution.py:724
  575.2 7.0 %multiply_add_fusion.1 = (f32[1,448,1280]{2,1,0:T(8,128)}, f32[1,448,1280]{2,1,0:T(8,128)}, f32[1,448,1280]{2,1,0:T(8,128)}) fusion(f32[1,448,1280]{2,1,0:T(8,128)} %param.57, f32[1,448,1280]{2,1,0:T(8,128)} %param.55, bf16[448,1280]{1,0:T(8,128)(2,1)} %get-tuple-element.195, f32[1,448,1280]{2,1,0:T(8,128)} %param.56), kind=kLoop, calls=%fused_computation.17 | loop fusion | flops 5734400 | bytes 14909440 | tf_op jit(solution)/shard_map/add | solution.py:55
  584.1 1.8 fusion.19
  589.0 4.2 convolution_add_fusion.2
  597.3 10.8 %multiply_add_fusion = (f32[1,2,640,896]{3,2,1,0:T(8,128)}, f32[1,2,640,896]{3,2,1,0:T(8,128)}, f32[1,2,640,896]{3,2,1,0:T(8,128)}) fusion(f32[1,2,640,896]{3,2,1,0:T(8,128)} %param.54, f32[1,2,640,896]{3,2,1,0:T(8,128)} %param.52, bf16[2,640,896]{2,1,0:T(8,128)(2,1)} %get-tuple-element.194, f32[1,2,640,896]{3,2,1,0:T(8,128)} %param.53), kind=kLoop, calls=%fused_computation.4 | loop fusion | flops 11468800 | bytes 29818880 | tf_op jit(solution)/shard_map/add | solution.py:55
  608.1 3.3 add_convert_fusion
  (231 shorter events, 65.8 us)
Async XLA Ops:
  7.2 393.6 %all-gather.2.cloned.1.call-start = ((), (), s32[]{:S(2)}) async-start(), calls=%async_computation | async-start | bytes 7096320 | tf_op jit(solution)/shard_map/all_gather | solution.py:1297
  20.2 93.9 %copy-start.15 = (bf16[384,1280]{1,0:T(8,128)(2,1)S(1)}, bf16[384,1280]{1,0:T(8,128)(2,1)}, u32[]{:S(2)}) copy-start(bf16[384,1280]{1,0:T(8,128)(2,1)} %inputs.1) | copy-start | bytes 2949124
  107.0 36.5 %collective-permute-start = (bf16[400,1280]{1,0:T(8,128)(2,1)}, bf16[400,1280]{1,0:T(8,128)(2,1)}, u32[]{:S(2)}, u32[]{:S(2)}) collective-permute-start(bf16[400,1280]{1,0:T(8,128)(2,1)} %fusion.28.refs_2_), channel_id=1, source_target_pairs={{0,4},{1,5},{2,6},{3,7},{4,8},{5,9},{6,10},{7,11},{8,12},{9,13},{1... | collective-permute-start | bytes 3072008 | tf_op jit(solution)/shard_map/ppermute | solution.py:1122
  107.1 47.2 %collective-permute-start.1 = (bf16[400,1280]{1,0:T(8,128)(2,1)}, bf16[400,1280]{1,0:T(8,128)(2,1)}, u32[]{:S(2)}, u32[]{:S(2)}) collective-permute-start(bf16[400,1280]{1,0:T(8,128)(2,1)} %fusion.28.refs_2_), channel_id=1, source_target_pairs={{0,12},{1,13},{2,14},{3,15},{4,0},{5,1},{6,2},{7,3},{8,4},{9,5},{1... | collective-permute-start | bytes 3072008 | tf_op jit(solution)/shard_map/ppermute | solution.py:1122
  110.9 51.9 %collective-permute-start.2 = (bf16[2,640,896]{2,1,0:T(8,128)(2,1)}, bf16[2,640,896]{2,1,0:T(8,128)(2,1)}, u32[]{:S(2)}, u32[]{:S(2)}) collective-permute-start(bf16[2,640,896]{2,1,0:T(8,128)(2,1)} %convert_bitcast_fusion.refs_1_), channel_id=1, source_target_pairs={{0,1},{1,0},{2,3},{3,2},{4,5},{5,4},{6,7},{7,6},{8,9},{9,8},{10,11... | collective-permute-start | bytes 6881288 | tf_op jit(solution)/shard_map/ppermute | solution.py:1126
  111.5 51.6 %collective-permute-start.3 = (bf16[2,640,896]{2,1,0:T(8,128)(2,1)}, bf16[2,640,896]{2,1,0:T(8,128)(2,1)}, u32[]{:S(2)}, u32[]{:S(2)}) collective-permute-start(bf16[2,640,896]{2,1,0:T(8,128)(2,1)} %convert_bitcast_fusion.refs_1_), channel_id=1, source_target_pairs={{0,2},{1,3},{2,0},{3,1},{4,6},{5,7},{6,4},{7,5},{8,10},{9,11},{10,... | collective-permute-start | bytes 6881288 | tf_op jit(solution)/shard_map/ppermute | solution.py:1126
  117.5 24.2 %copy-start.30 = (f32[896,40]{0,1:T(8,128)S(1)}, f32[896,40]{0,1:T(8,128)}, u32[]{:S(2)}) copy-start(f32[896,40]{0,1:T(8,128)} %param.43) | copy-start | bytes 430084
  141.7 67.4 %copy-start.50 = (f32[384]{0:T(512)}, f32[384]{0:T(512)S(1)}, u32[]{:S(2)}) copy-start(f32[384]{0:T(512)S(1)} %fusion.62) | copy-start | bytes 4612
  209.2 9.4 %copy-start.60 = (s32[4]{0:T(128)}, s32[4]{0:T(128)S(1)}, u32[]{:S(2)}) copy-start(s32[4]{0:T(128)S(1)} %xor_add_fusion.numbers) | copy-start | bytes 52
  209.2 55.0 %collective-permute-start.5 = (bf16[400,1280]{1,0:T(8,128)(2,1)}, bf16[400,1280]{1,0:T(8,128)(2,1)}, u32[]{:S(2)}, u32[]{:S(2)}) collective-permute-start(bf16[400,1280]{1,0:T(8,128)(2,1)} %collective-permute-done.refs_3_), channel_id=1, source_target_pairs={{0,4},{1,5},{2,6},{3,7},{4,8},{5,9},{6,10},{7,11},{8,12},{9,13},{1... | collective-permute-start | bytes 3072008 | tf_op jit(solution)/shard_map/ppermute | solution.py:1122
  209.3 54.9 %collective-permute-start.4 = (bf16[400,1280]{1,0:T(8,128)(2,1)}, bf16[400,1280]{1,0:T(8,128)(2,1)}, u32[]{:S(2)}, u32[]{:S(2)}) collective-permute-start(bf16[400,1280]{1,0:T(8,128)(2,1)} %get-tuple-element.126.refs_1_), channel_id=1, source_target_pairs={{0,4},{1,5},{2,6},{3,7},{4,8},{5,9},{6,10},{7,11},{8,12},{9,13},{1... | collective-permute-start | bytes 3072008 | tf_op jit(solution)/shard_map/ppermute | solution.py:1122
  262.4 129.4 %collective-permute-start.6 = (bf16[400,1280]{1,0:T(8,128)(2,1)}, bf16[400,1280]{1,0:T(8,128)(2,1)}, u32[]{:S(2)}, u32[]{:S(2)}) collective-permute-start(bf16[400,1280]{1,0:T(8,128)(2,1)} %get-tuple-element.133), channel_id=1, source_target_pairs={{0,12},{1,13},{2,14},{3,15},{4,0},{5,1},{6,2},{7,3},{8,4},{9,5},{1... | collective-permute-start | bytes 3072008 | tf_op jit(solution)/shard_map/ppermute | solution.py:1122
  314.2 77.6 %collective-permute-start.7 = (bf16[400,1280]{1,0:T(8,128)(2,1)}, bf16[400,1280]{1,0:T(8,128)(2,1)}, u32[]{:S(2)}, u32[]{:S(2)}) collective-permute-start(bf16[400,1280]{1,0:T(8,128)(2,1)} %get-tuple-element.140), channel_id=1, source_target_pairs={{0,8},{1,9},{2,10},{3,11},{4,12},{5,13},{6,14},{7,15},{8,0},{9,1},... | collective-permute-start | bytes 3072008 | tf_op jit(solution)/shard_map/ppermute | solution.py:1122
  316.5 75.3 %collective-permute-start.8 = (bf16[400,1280]{1,0:T(8,128)(2,1)}, bf16[400,1280]{1,0:T(8,128)(2,1)}, u32[]{:S(2)}, u32[]{:S(2)}) collective-permute-start(bf16[400,1280]{1,0:T(8,128)(2,1)} %get-tuple-element.141), channel_id=1, source_target_pairs={{0,4},{1,5},{2,6},{3,7},{4,8},{5,9},{6,10},{7,11},{8,12},{9,13},{1... | collective-permute-start | bytes 3072008 | tf_op jit(solution)/shard_map/ppermute | solution.py:1122
  389.6 75.1 %collective-permute-start.12 = (bf16[1952,896]{1,0:T(8,128)(2,1)}, bf16[1952,896]{1,0:T(8,128)(2,1)}, u32[]{:S(2)}, u32[]{:S(2)}) collective-permute-start(bf16[1952,896]{1,0:T(8,128)(2,1)} %get-tuple-element.184), channel_id=1, source_target_pairs={{0,1},{1,0},{2,3},{3,2},{4,5},{5,4},{6,7},{7,6},{8,9},{9,8},{10,11... | collective-permute-start | bytes 10493960 | tf_op jit(solution)/shard_map/ppermute | solution.py:1126
  389.7 75.1 %collective-permute-start.13 = (bf16[1952,896]{1,0:T(8,128)(2,1)}, bf16[1952,896]{1,0:T(8,128)(2,1)}, u32[]{:S(2)}, u32[]{:S(2)}) collective-permute-start(bf16[1952,896]{1,0:T(8,128)(2,1)} %get-tuple-element.185), channel_id=1, source_target_pairs={{0,2},{1,3},{2,0},{3,1},{4,6},{5,7},{6,4},{7,5},{8,10},{9,11},{10,... | collective-permute-start | bytes 10493960 | tf_op jit(solution)/shard_map/ppermute | solution.py:1126
  396.3 211.7 %collective-permute-start.10 = (bf16[384,1280]{1,0:T(8,128)(2,1)}, bf16[384,1280]{1,0:T(8,128)(2,1)}, u32[]{:S(2)}, u32[]{:S(2)}) collective-permute-start(bf16[384,1280]{1,0:T(8,128)(2,1)} %get-tuple-element.144), channel_id=1, source_target_pairs={{0,8},{1,9},{2,10},{3,11},{4,12},{5,13},{6,14},{7,15},{8,0},{9,1},... | collective-permute-start | bytes 2949128 | tf_op jit(solution)/shard_map/ppermute | solution.py:1122
  397.0 211.1 %collective-permute-start.11 = (bf16[384,1280]{1,0:T(8,128)(2,1)}, bf16[384,1280]{1,0:T(8,128)(2,1)}, u32[]{:S(2)}, u32[]{:S(2)}) collective-permute-start(bf16[384,1280]{1,0:T(8,128)(2,1)} %get-tuple-element.145), channel_id=1, source_target_pairs={{0,4},{1,5},{2,6},{3,7},{4,8},{5,9},{6,10},{7,11},{8,12},{9,13},{1... | collective-permute-start | bytes 2949128 | tf_op jit(solution)/shard_map/ppermute | solution.py:1122
  399.6 208.5 %collective-permute-start.9 = (bf16[384,1280]{1,0:T(8,128)(2,1)}, bf16[384,1280]{1,0:T(8,128)(2,1)}, u32[]{:S(2)}, u32[]{:S(2)}) collective-permute-start(bf16[384,1280]{1,0:T(8,128)(2,1)} %get-tuple-element.143), channel_id=1, source_target_pairs={{0,12},{1,13},{2,14},{3,15},{4,0},{5,1},{6,2},{7,3},{8,4},{9,5},{1... | collective-permute-start | bytes 2949128 | tf_op jit(solution)/shard_map/ppermute | solution.py:1122
  415.4 26.9 %copy-start.16 = (bf16[384,1280]{1,0:T(8,128)(2,1)S(1)}, bf16[384,1280]{1,0:T(8,128)(2,1)}, u32[]{:S(2)}) copy-start(bf16[384,1280]{1,0:T(8,128)(2,1)} %inputs.1) | copy-start | bytes 2949124
  415.4 26.9 %copy-start.53 = (f32[384]{0:T(512)S(1)}, f32[384]{0:T(512)}, u32[]{:S(2)}) copy-start(f32[384]{0:T(512)} %copy-done.52) | copy-start | bytes 4612
  444.9 8.2 %copy-start.59 = (bf16[128]{0:T(256)(128)(2,1)S(1)}, bf16[128]{0:T(256)(128)(2,1)}, u32[]{:S(2)}) copy-start(bf16[128]{0:T(256)(128)(2,1)} %pad.18.clone) | copy-start | bytes 772
  575.1 7.1 %copy-start.34 = (f32[1280,40]{0,1:T(8,128)S(1)}, f32[1280,40]{0,1:T(8,128)}, u32[]{:S(2)}) copy-start(f32[1280,40]{0,1:T(8,128)} %param.39) | copy-start | bytes 614404
  575.1 7.1 %copy-start.35 = (f32[1280,40]{0,1:T(8,128)S(1)}, f32[1280,40]{0,1:T(8,128)}, u32[]{:S(2)}) copy-start(f32[1280,40]{0,1:T(8,128)} %param.38) | copy-start | bytes 614404
  575.1 7.1 %copy-start.41 = (bf16[40,1280]{1,0:T(8,128)(2,1)S(1)}, bf16[40,1280]{1,0:T(8,128)(2,1)}, u32[]{:S(2)}) copy-start(bf16[40,1280]{1,0:T(8,128)(2,1)} %get-tuple-element.189) | copy-start | bytes 307204
  575.2 8.0 %copy-start.31 = (f32[896,40]{0,1:T(8,128)S(1)}, f32[896,40]{0,1:T(8,128)}, u32[]{:S(2)}) copy-start(f32[896,40]{0,1:T(8,128)} %param.43) | copy-start | bytes 430084
  575.2 8.0 %copy-start.36 = (f32[896,40]{0,1:T(8,128)S(1)}, f32[896,40]{0,1:T(8,128)}, u32[]{:S(2)}) copy-start(f32[896,40]{0,1:T(8,128)} %param.45) | copy-start | bytes 430084
  575.2 8.0 %copy-start.37 = (f32[896,40]{0,1:T(8,128)S(1)}, f32[896,40]{0,1:T(8,128)}, u32[]{:S(2)}) copy-start(f32[896,40]{0,1:T(8,128)} %param.44) | copy-start | bytes 430084
  575.2 8.0 %copy-start.49 = (bf16[40,896]{1,0:T(8,128)(2,1)S(1)}, bf16[40,896]{1,0:T(8,128)(2,1)}, u32[]{:S(2)}) copy-start(bf16[40,896]{1,0:T(8,128)(2,1)} %get-tuple-element.192) | copy-start | bytes 215044
  575.2 8.8 %copy-start.18 = (f32[384,1280]{1,0:T(8,128)S(1)}, f32[384,1280]{1,0:T(8,128)}, u32[]{:S(2)}) copy-start(f32[384,1280]{1,0:T(8,128)} %get-tuple-element.150) | copy-start | bytes 5898244
  597.2 10.8 %copy-start.19 = (f32[384,1280]{1,0:T(8,128)S(1)}, f32[384,1280]{1,0:T(8,128)}, u32[]{:S(2)}) copy-start(f32[384,1280]{1,0:T(8,128)} %convolution_add_fusion.2) | copy-start | bytes 5898244
  597.2 10.9 %copy-start.25 = (bf16[384,1280]{1,0:T(8,128)(2,1)S(1)}, bf16[384,1280]{1,0:T(8,128)(2,1)}, u32[]{:S(2)}) copy-start(bf16[384,1280]{1,0:T(8,128)(2,1)} %get-tuple-element.142) | copy-start | bytes 2949124
  (44 other events, 109.5 us)
Sparse Core Ops, SparseCore 0:
  209.3 163.5 all-gather.1

commit v6 on v5

--- a/solution.py
+++ b/solution.py
@@ -512,12 +512,11 @@
     )
 
 
-def total_chain(moves, owns, crossed, arrived, totals, buffers):
+def total_chain(moves, owns, crossed, totals, buffers):
     full = jnp.float32
     half, hidden_width = owns[0].shape
     down_half, width = owns[2].shape
     edge = down_half // 2
-    places, _, _ = packed(half, hidden_width, down_half, width)
     jobs = []
     for i in range(2):
         for rows in range(0, half, half // 4):
@@ -534,18 +533,6 @@
         which, start, rows = jobs[n]
         at = pl.ds(start, rows)
         copies = [(owns[which].at[at], box(n, 0)), (crossed[which].at[at], box(n, 1))]
-        for k, package in enumerate(arrived):
-            for part, to_rows, to_columns, rows_at, columns_at in places:
-                inside = rows_at.start <= start < rows_at.stop
-                if part == which and inside:
-                    copies.append(
-                        (
-                            package.at[
-                                pl.ds(to_rows.start + start - rows_at.start, rows), to_columns
-                            ],
-                            box(n, 2 + k).at[:, columns_at],
-                        )
-                    )
         loads[n] = [moves.keep(source, target) for source, target in copies]
 
     load(0)
@@ -558,7 +545,7 @@
             for copy in stores[n - 2]:
                 copy.wait()
         total = box(n, 4)
-        total[...] = sum(box(n, i)[...].astype(full) for i in range(4)).astype(total.dtype)
+        total[...] = sum(box(n, i)[...].astype(full) for i in range(2)).astype(total.dtype)
         at = pl.ds(start, rows)
         target = totals[0].at[which, at] if which < 2 else totals[1].at[at]
         stores[n] = [moves.keep(total, target)]
@@ -577,7 +564,7 @@
 def sum_kernel(line, plans, arrays, *refs):
     count = len(plans)
     grads, refs = refs[:arrays], refs[arrays:]
-    owns, crossed, arrived, refs = refs[:3], refs[3:6], refs[6:8], refs[8:]
+    owns, crossed, refs = refs[:3], refs[3:6], refs[6:]
     sums, refs = refs[:arrays], refs[arrays:]
     totals, refs = refs[:2], refs[2:]
     buffers, refs = refs[:20], refs[20:]
@@ -687,11 +674,11 @@
             result.wait()
 
     chains = [chain(n, o) for n in range(count) for o in range(3)]
-    chains.append(total_chain(moves, owns, crossed, arrived, totals, buffers))
+    chains.append(total_chain(moves, owns, crossed, totals, buffers))
     in_turn(chains)
 
 
-def sum_all(experts, grads, plans, owns, crossed, arrived):
+def sum_all(experts, grads, plans, owns, crossed):
     line = experts // PLANE
     half, rest = line // 2, (line - 1) // 2
     rows = grads[0].shape[0] // (2 * experts)
@@ -716,7 +703,7 @@
     count = len(plans)
     given = sum(len(pieces) for plan in plans for pieces in plan)
     number = given + 3 * count * (line + 1)
-    others = list(owns) + list(crossed) + list(arrived)
+    others = list(owns) + list(crossed)
     shapes += [
         jax.ShapeDtypeStruct((2,) + owns[0].shape, dtype),
         jax.ShapeDtypeStruct(owns[2].shape, dtype),
@@ -1276,9 +1263,7 @@
         result_parts += result_part
     routed_grad = sum(part.astype(full) for part in grad_parts)
     result_parts = after(result_parts, routed_grad)
-    routed_result = sum(
-        (grid.shift(part, -r) if r else part).astype(full) for r, part in enumerate(result_parts)
-    )
+    result_parts = [grid.shift(part, -r) if r else part for r, part in enumerate(result_parts)]
     owns, crossed, nears = third_exchange(experts, after(kept, last))
     arrived = [grid.swap(part, flip) for part, flip in zip(nears, (1, 2))]
     gate_grads = routed_grad[tokens:]
@@ -1361,8 +1346,18 @@
         sum_plans(model_width, hidden_width, extra_width),
         owns,
         crossed,
-        arrived,
-    )
+    )
+    half, down_half = model_width // 2, hidden_width // 2
+    more = model_width - hidden_width
+    total_in, total_down = total_in.astype(full), total_down.astype(full)
+    for package in after(arrived, total_in):
+        total_in = total_in + package[: 2 * half].reshape(2, half, hidden_width).astype(full)
+        below = package[2 * half + down_half :]
+        below = jnp.concatenate([below[:, :more], below[:, more : 2 * more]], axis=0)
+        down = package[2 * half : 2 * half + down_half]
+        total_down = total_down + jnp.concatenate([down, below], axis=1).astype(full)
+    result_parts = after(result_parts, total_in)
+    routed_result = sum(part.astype(full) for part in result_parts)
     output = (hidden + shared_result + routed_result).astype(low)
 
     sums = [part.astype(full) for part in sums]
@@ -1392,14 +1387,14 @@
         expert_in,
         expert_in_momentum,
         expert_in_average,
-        total_in.astype(full)[None],
+        total_in[None],
         rate_expert_in,
     )
     upd_expert_down = advance(
         expert_down,
         expert_down_momentum,
         expert_down_average,
-        total_down.astype(full)[None],
+        total_down[None],
         rate_expert_down,
     )
     return (

time: 627 us -> 703 us (1.12)
  waiting for transfers between devices: 30.2 us -> 97.8 us
  local copies, waits for them, and re-layouts: 30.9 us -> 43.7 us
    ppermute x10, waiting for transfers between devices: 10.8 us -> 89.1 us  [shift(): return lax.ppermute(block, 'expert', pairs)]
    slice x0 -> x6, local copies, waits for them, and re-layouts: none -> 13.4 us  [the longest x2 6.55 us: local(): package[:2 * half].reshape(2, half, hidden_width).astype(full)]
    ppermute x4, waiting for transfers between devices: 19.4 us -> 8.72 us  [swap(): return lax.ppermute(block, 'expert', pairs)]
    unnamed x133 -> x153, local copies, waits for them, and re-layouts: 22.3 us -> 20.9 us
  transfers between devices with their start and end apart: 15 -> 15, of which waited for: 5 -> 5; matrix products, arithmetic and copies ran while one was open for 13% -> 11% of each run, Pallas kernels for 50% -> 44%
where the time goes in v6:
time: 703 us; the launch traced here: 695 us
  Pallas kernels  439 us (62%)
  waiting for transfers between devices  97.8 us (14%)
  other arithmetic  57 us (8%)
  local copies, waits for them, and re-layouts  43.7 us (6%)
  matrix products  23 us (3%)
  starting transfers between devices  18.4 us (3%)
  between operations  16 us (2%)
    pallas_call x1, Pallas kernels, sum_all(): pl.pallas_call(functools.partial(sum_kernel, line, plans, len(grads)), ou...  106 us
    ppermute x10, waiting for transfers between devices, shift(): return lax.ppermute(block, 'expert', pairs)  89.1 us
    pallas_call x2, Pallas kernels, run_experts(): pl.pallas_call(functools.partial(expert_kernel, count), grid_spec=pltpu.P...  88.2 us
    pallas_call x1, Pallas kernels, first_exchange(): pl.pallas_call(functools.partial(first_kernel, line, plans), out_shape=[j...  86.8 us
    pallas_call x1, Pallas kernels, third_exchange(): pl.pallas_call(functools.partial(third_kernel, line, len(kept)), out_shap...  61.7 us
    pallas_call x1, Pallas kernels, second_exchange(): pl.pallas_call(functools.partial(second_kernel, line), out_shape=[jax.Sha...  46.1 us
    pallas_call x1, Pallas kernels, attend_back(): pl.pallas_call(attend_back_kernel, grid=(steps,), in_specs=[whole(tokens,...  27 us
    add x8, other arithmetic, advance(): average_new = average + (weight_new - average) / (STEP + 1)  21.9 us
  transfers between devices with their start and end apart: 15, of which 5 were waited for; matrix products, arithmetic and copies ran while one was open for 11% of the time, Pallas kernels for 44%

profile of v6, /device:TPU:0, one launch (start us, length us, event | category | flops | bytes accessed | tf_op | source)
XLA Modules:
  0.0 694.7 jit_solution(365075274251021621)
XLA Ops:
  10.1 2.8 convert_bitcast_fusion.1.refs_2_.refs_4_
  14.2 4.0 convert_bitcast_fusion.refs_1_
  20.2 86.8 %shard_map.476 = (bf16[2,4,2,2,40,3968]{5,4,3,2,1,0:T(8,128)(2,1)}, bf16[2,4,2,2,40,1280]{5,4,3,2,1,0:T(8,128)(2,1)}, bf16[448,1280]{1,0:T(8,128)(2,1)}, bf16[448,1280]{1,0:T(8,128)(2,1)}) custom-call(bf16[40,3968]{1,0:T(8,128)(2,1)} %concatenate.37.refs_0_, bf16[40,1280]{1,0:T(8,128)(2,1)} %convert_bitcast_fusion.3.refs_1_, ...), custom_call_target="tpu_custom_call" | custom-call | tf_op jit(solution)/shard_map/pallas_call | solution.py:269
  107.1 3.8 collective-permute-start.1
  117.6 18.8 %shard_map.477 = (bf16[384,1280]{1,0:T(8,128)(2,1)S(1)}, bf16[384,1280]{1,0:T(8,128)(2,1)S(1)}, bf16[384,1280]{1,0:T(8,128)(2,1)S(1)}, bf16[384,1280]{1,0:T(8,12...) custom-call(bf16[384,1280]{1,0:T(8,128)(2,1)} %fusion.17.normed, bf16[1280,3968]{1,0:T(8,128)(2,1)} %bitcast.116, ...), custom_call_target="tpu_custom_call" | custom-call | flops 5033164800 | bytes 32768000 | tf_op jit(solution)/shard_map/pallas_call | solution.py:797
  143.5 10.9 %collective-permute-done.1.refs_3_ = bf16[400,1280]{1,0:T(8,128)(2,1)} collective-permute-done((bf16[400,1280]{1,0:T(8,128)(2,1)}, bf16[400,1280]{1,0:T(8,128)(2,1)}, u32[]{:S(2)}, u32[]{:S(2)}) %collective-permute-start.1) | collective-permute-done | bytes 1024032 | tf_op jit(solution)/shard_map/ppermute | solution.py:1109
  154.4 8.5 %collective-permute-done.2.refs_2_ = bf16[2,640,896]{2,1,0:T(8,128)(2,1)} collective-permute-done((bf16[2,640,896]{2,1,0:T(8,128)(2,1)}, bf16[2,640,896]{2,1,0:T(8,128)(2,1)}, u32[]{:S(2)}, u32[]{:S(2)}) %collective-permute-start.2) | collective-permute-done | bytes 2293792 | tf_op jit(solution)/shard_map/ppermute | solution.py:1113
  163.1 46.1 %shard_map.478 = (bf16[400,1280]{1,0:T(8,128)(2,1)}, bf16[400,1280]{1,0:T(8,128)(2,1)}, bf16[4,2,640,896]{3,2,1,0:T(8,128)(2,1)}, bf16[4,2,640,896]{3,2,1,0:T(8,128)(2,1)}, bf16[4,2,448,1280]{3,2,1,0:T(8,128)(2,1)}) custom-call(bf16[400,1280]{1,0:T(8,128)(2,1)} %pad_maximum_fusion.refs_0_, bf16[2,640,896]{2,1,0:T(8,128)(2,1)} %convert_bitcast_fusion.refs_1_, ...), custom_call_target="tpu_custom_call" | custom-call | tf_op jit(solution)/shard_map/pallas_call | solution.py:329
  209.3 3.2 collective-permute-start.4
  218.6 43.7 %shard_map.479 = (bf16[400,1280]{1,0:T(8,128)(2,1)}, bf16[400,1280]{1,0:T(8,128)(2,1)}, bf16[384,1280]{1,0:T(8,128)(2,1)}, bf16[384,1280]{1,0:T(8,128)(2,1)}, bf...) custom-call(s32[4]{0:T(128)} %copy-done.70, ...), custom_call_target="tpu_custom_call" | custom-call | flops 23655874560 | bytes 27525120 | tf_op jit(solution)/shard_map/pallas_call | solution.py:1011
  268.6 44.4 %shard_map.480 = (bf16[400,1280]{1,0:T(8,128)(2,1)}, bf16[400,1280]{1,0:T(8,128)(2,1)}, bf16[384,1280]{1,0:T(8,128)(2,1)}, bf16[384,1280]{1,0:T(8,128)(2,1)}, bf...) custom-call(s32[4]{0:T(128)} %copy-done.70, ...), custom_call_target="tpu_custom_call" | custom-call | flops 23655874560 | bytes 27525120 | tf_op jit(solution)/shard_map/pallas_call | solution.py:1011
  313.0 61.7 %shard_map.483 = (bf16[640,896]{1,0:T(8,128)(2,1)}, bf16[640,896]{1,0:T(8,128)(2,1)}, bf16[448,1280]{1,0:T(8,128)(2,1)}, bf16[640,896]{1,0:T(8,128)(2,1)}, bf16[...) custom-call(bf16[4,384,1280]{2,1,0:T(8,128)(2,1)} %get-tuple-element.174, ...), custom_call_target="tpu_custom_call" | custom-call | tf_op jit(solution)/shard_map/pallas_call | solution.py:476
  389.3 12.5 %collective-permute-done.6 = bf16[400,1280]{1,0:T(8,128)(2,1)} collective-permute-done((bf16[400,1280]{1,0:T(8,128)(2,1)}, bf16[400,1280]{1,0:T(8,128)(2,1)}, u32[]{:S(2)}, u32[]{:S(2)}) %collective-permute-start.6) | collective-permute-done | bytes 1024032 | tf_op jit(solution)/shard_map/ppermute | solution.py:1109
  401.8 65.7 %collective-permute-done.7 = bf16[400,1280]{1,0:T(8,128)(2,1)} collective-permute-done((bf16[400,1280]{1,0:T(8,128)(2,1)}, bf16[400,1280]{1,0:T(8,128)(2,1)}, u32[]{:S(2)}, u32[]{:S(2)}) %collective-permute-start.7) | collective-permute-done | bytes 1024032 | tf_op jit(solution)/shard_map/ppermute | solution.py:1109
  467.5 2.3 convert_add_fusion.3
  472.3 3.8 collective-permute-start.9
  477.3 3.3 slice.192
  480.6 2.1 slice.199
  482.7 3.2 slice.193
  487.7 1.8 fusion.92
  489.5 3.0 fusion.9
  498.7 2.6 multiply_reduce_fusion
  501.3 1.9 fusion.90
  504.1 27.0 %shard_map.481 = (bf16[1280,1280]{1,0:T(8,128)(2,1)}, bf16[1280,1280]{1,0:T(8,128)(2,1)}, bf16[1280,1280]{1,0:T(8,128)(2,1)}, bf16[1280,1280]{1,0:T(8,128)(2,1)}, f32[384,1280]{1,0:T(8,128)}) custom-call(bf16[384,1280]{1,0:T(8,128)(2,1)S(1)} %get-tuple-element.343.grad_branch, bf16[384,1280]{1,0:T(8,128)(2,1)S(1)} %copy-done, ...), custom_call_target="tpu_custom_call" | custom-call | flops 10066329600 | bytes 65536000 | tf_op jit(solution)/shard_map/pallas_call | solution.py:891
  531.1 2.1 fusion.22
  533.7 4.0 shard_map.482
  543.0 106.3 %shard_map.484 = (bf16[40,1280]{1,0:T(8,128)(2,1)}, bf16[40,1280]{1,0:T(8,128)(2,1)}, bf16[40,1280]{1,0:T(8,128)(2,1)}, bf16[40,1280]{1,0:T(8,128)(2,1)}, bf16[4...) custom-call(bf16[2,4,2,2,40,1280]{5,4,3,2,1,0:T(8,128)(2,1)} %bitcas, ...), custom_call_target="tpu_custom_call" | custom-call | tf_op jit(solution)/shard_map/pallas_call | solution.py:711
  649.4 13.2 %multiply_add_fusion = (f32[1,2,640,896]{3,2,1,0:T(8,128)}, f32[1,2,640,896]{3,2,1,0:T(8,128)}, f32[1,2,640,896]{3,2,1,0:T(8,128)}) fusion(f32[1,2,640,896]{3,2,1,0:T(8,128)} %param.54, f32[1,2,640,896]{3,2,1,0:T(8,128)} %param.52, f32[1,2,640,896]{3,2,1,0:T(8,128)} %param.53, bf16[2,640,896]{2,1,0:T(8,128)(2,1)} %bitcast.127, ...), kind=kLoop, calls=%fused_computation.6 | loop fusion | flops 16056320 | bytes 34406400 | tf_op jit(solution)/shard_map/add | solution.py:55
  666.8 4.1 fusion.21
  675.9 3.0 convolution_add_fusion.2
  679.0 3.5 add_convert_fusion
  683.1 4.6 multiply_add_fusion.1
  (257 shorter events, 74.1 us)
Async XLA Ops:
  7.2 482.3 %all-gather.2.cloned.1.call-start = ((), (), s32[]{:S(2)}) async-start(), calls=%async_computation | async-start | bytes 7096320 | tf_op jit(solution)/shard_map/all_gather | solution.py:1282
  20.2 93.9 %copy-start.15 = (bf16[384,1280]{1,0:T(8,128)(2,1)S(1)}, bf16[384,1280]{1,0:T(8,128)(2,1)}, u32[]{:S(2)}) copy-start(bf16[384,1280]{1,0:T(8,128)(2,1)} %inputs.1) | copy-start | bytes 2949124
  107.1 36.4 %collective-permute-start = (bf16[400,1280]{1,0:T(8,128)(2,1)}, bf16[400,1280]{1,0:T(8,128)(2,1)}, u32[]{:S(2)}, u32[]{:S(2)}) collective-permute-start(bf16[400,1280]{1,0:T(8,128)(2,1)} %fusion.28.refs_2_), channel_id=1, source_target_pairs={{0,4},{1,5},{2,6},{3,7},{4,8},{5,9},{6,10},{7,11},{8,12},{9,13},{1... | collective-permute-start | bytes 3072008 | tf_op jit(solution)/shard_map/ppermute | solution.py:1109
  107.1 47.2 %collective-permute-start.1 = (bf16[400,1280]{1,0:T(8,128)(2,1)}, bf16[400,1280]{1,0:T(8,128)(2,1)}, u32[]{:S(2)}, u32[]{:S(2)}) collective-permute-start(bf16[400,1280]{1,0:T(8,128)(2,1)} %fusion.28.refs_2_), channel_id=1, source_target_pairs={{0,12},{1,13},{2,14},{3,15},{4,0},{5,1},{6,2},{7,3},{8,4},{9,5},{1... | collective-permute-start | bytes 3072008 | tf_op jit(solution)/shard_map/ppermute | solution.py:1109
  111.0 51.9 %collective-permute-start.2 = (bf16[2,640,896]{2,1,0:T(8,128)(2,1)}, bf16[2,640,896]{2,1,0:T(8,128)(2,1)}, u32[]{:S(2)}, u32[]{:S(2)}) collective-permute-start(bf16[2,640,896]{2,1,0:T(8,128)(2,1)} %convert_bitcast_fusion.refs_1_), channel_id=1, source_target_pairs={{0,1},{1,0},{2,3},{3,2},{4,5},{5,4},{6,7},{7,6},{8,9},{9,8},{10,11... | collective-permute-start | bytes 6881288 | tf_op jit(solution)/shard_map/ppermute | solution.py:1113
  111.5 51.6 %collective-permute-start.3 = (bf16[2,640,896]{2,1,0:T(8,128)(2,1)}, bf16[2,640,896]{2,1,0:T(8,128)(2,1)}, u32[]{:S(2)}, u32[]{:S(2)}) collective-permute-start(bf16[2,640,896]{2,1,0:T(8,128)(2,1)} %convert_bitcast_fusion.refs_1_), channel_id=1, source_target_pairs={{0,2},{1,3},{2,0},{3,1},{4,6},{5,7},{6,4},{7,5},{8,10},{9,11},{10,... | collective-permute-start | bytes 6881288 | tf_op jit(solution)/shard_map/ppermute | solution.py:1113
  117.5 24.2 %copy-start.39 = (f32[896,40]{0,1:T(8,128)S(1)}, f32[896,40]{0,1:T(8,128)}, u32[]{:S(2)}) copy-start(f32[896,40]{0,1:T(8,128)} %param.43) | copy-start | bytes 430084
  141.6 67.5 %copy-start.58 = (f32[384]{0:T(512)}, f32[384]{0:T(512)S(1)}, u32[]{:S(2)}) copy-start(f32[384]{0:T(512)S(1)} %fusion.62) | copy-start | bytes 4612
  209.2 9.4 %copy-start.70 = (s32[4]{0:T(128)}, s32[4]{0:T(128)S(1)}, u32[]{:S(2)}) copy-start(s32[4]{0:T(128)S(1)} %xor_add_fusion.numbers) | copy-start | bytes 52
  209.2 53.1 %collective-permute-start.5 = (bf16[400,1280]{1,0:T(8,128)(2,1)}, bf16[400,1280]{1,0:T(8,128)(2,1)}, u32[]{:S(2)}, u32[]{:S(2)}) collective-permute-start(bf16[400,1280]{1,0:T(8,128)(2,1)} %collective-permute-done.refs_3_), channel_id=1, source_target_pairs={{0,4},{1,5},{2,6},{3,7},{4,8},{5,9},{6,10},{7,11},{8,12},{9,13},{1... | collective-permute-start | bytes 3072008 | tf_op jit(solution)/shard_map/ppermute | solution.py:1109
  209.3 53.1 %collective-permute-start.4 = (bf16[400,1280]{1,0:T(8,128)(2,1)}, bf16[400,1280]{1,0:T(8,128)(2,1)}, u32[]{:S(2)}, u32[]{:S(2)}) collective-permute-start(bf16[400,1280]{1,0:T(8,128)(2,1)} %get-tuple-element.132.refs_1_), channel_id=1, source_target_pairs={{0,4},{1,5},{2,6},{3,7},{4,8},{5,9},{6,10},{7,11},{8,12},{9,13},{1... | collective-permute-start | bytes 3072008 | tf_op jit(solution)/shard_map/ppermute | solution.py:1109
  313.0 67.7 %copy-start.60 = (f32[40,16]{0,1:T(8,128)S(1)}, f32[40,16]{0,1:T(8,128)}, u32[]{:S(2)}) copy-start(f32[40,16]{0,1:T(8,128)} %param.46) | copy-start | bytes 7684
  313.0 67.8 %copy-start.68 = (f32[2,40]{1,0:T(2,128)S(1)}, f32[2,40]{1,0:T(2,128)}, u32[]{:S(2)}) copy-start(f32[2,40]{1,0:T(2,128)} %param.49) | copy-start | bytes 964
  374.7 92.7 %copy-start.29 = (bf16[400,1280]{1,0:T(8,128)(2,1)S(1)}, bf16[400,1280]{1,0:T(8,128)(2,1)}, u32[]{:S(2)}) copy-start(bf16[400,1280]{1,0:T(8,128)(2,1)} %get-tuple-element.138) | copy-start | bytes 3072004
  374.8 101.3 %collective-permute-start.12 = (bf16[1952,896]{1,0:T(8,128)(2,1)}, bf16[1952,896]{1,0:T(8,128)(2,1)}, u32[]{:S(2)}, u32[]{:S(2)}) collective-permute-start(bf16[1952,896]{1,0:T(8,128)(2,1)} %get-tuple-element.191), channel_id=1, source_target_pairs={{0,1},{1,0},{2,3},{3,2},{4,5},{5,4},{6,7},{7,6},{8,9},{9,8},{10,11... | collective-permute-start | bytes 10493960 | tf_op jit(solution)/shard_map/ppermute | solution.py:1113
  375.1 101.0 %collective-permute-start.13 = (bf16[1952,896]{1,0:T(8,128)(2,1)}, bf16[1952,896]{1,0:T(8,128)(2,1)}, u32[]{:S(2)}, u32[]{:S(2)}) collective-permute-start(bf16[1952,896]{1,0:T(8,128)(2,1)} %get-tuple-element.192), channel_id=1, source_target_pairs={{0,2},{1,3},{2,0},{3,1},{4,6},{5,7},{6,4},{7,5},{8,10},{9,11},{10,... | collective-permute-start | bytes 10493960 | tf_op jit(solution)/shard_map/ppermute | solution.py:1113
  376.9 25.0 %collective-permute-start.6 = (bf16[400,1280]{1,0:T(8,128)(2,1)}, bf16[400,1280]{1,0:T(8,128)(2,1)}, u32[]{:S(2)}, u32[]{:S(2)}) collective-permute-start(bf16[400,1280]{1,0:T(8,128)(2,1)} %get-tuple-element.139), channel_id=1, source_target_pairs={{0,12},{1,13},{2,14},{3,15},{4,0},{5,1},{6,2},{7,3},{8,4},{9,5},{1... | collective-permute-start | bytes 3072008 | tf_op jit(solution)/shard_map/ppermute | solution.py:1109
  378.4 89.1 %collective-permute-start.7 = (bf16[400,1280]{1,0:T(8,128)(2,1)}, bf16[400,1280]{1,0:T(8,128)(2,1)}, u32[]{:S(2)}, u32[]{:S(2)}) collective-permute-start(bf16[400,1280]{1,0:T(8,128)(2,1)} %get-tuple-element.146), channel_id=1, source_target_pairs={{0,8},{1,9},{2,10},{3,11},{4,12},{5,13},{6,14},{7,15},{8,0},{9,1},... | collective-permute-start | bytes 3072008 | tf_op jit(solution)/shard_map/ppermute | solution.py:1109
  380.1 87.4 %collective-permute-start.8 = (bf16[400,1280]{1,0:T(8,128)(2,1)}, bf16[400,1280]{1,0:T(8,128)(2,1)}, u32[]{:S(2)}, u32[]{:S(2)}) collective-permute-start(bf16[400,1280]{1,0:T(8,128)(2,1)} %get-tuple-element.147), channel_id=1, source_target_pairs={{0,4},{1,5},{2,6},{3,7},{4,8},{5,9},{6,10},{7,11},{8,12},{9,13},{1... | collective-permute-start | bytes 3072008 | tf_op jit(solution)/shard_map/ppermute | solution.py:1109
  389.3 80.5 %copy-start.59 = (f32[384]{0:T(512)S(1)}, f32[384]{0:T(512)}, u32[]{:S(2)}) copy-start(f32[384]{0:T(512)} %copy-done.58) | copy-start | bytes 4612
  472.3 190.3 %collective-permute-start.10 = (bf16[384,1280]{1,0:T(8,128)(2,1)}, bf16[384,1280]{1,0:T(8,128)(2,1)}, u32[]{:S(2)}, u32[]{:S(2)}) collective-permute-start(bf16[384,1280]{1,0:T(8,128)(2,1)} %get-tuple-element.150), channel_id=1, source_target_pairs={{0,8},{1,9},{2,10},{3,11},{4,12},{5,13},{6,14},{7,15},{8,0},{9,1},... | collective-permute-start | bytes 2949128 | tf_op jit(solution)/shard_map/ppermute | solution.py:1109
  472.3 190.3 %collective-permute-start.11 = (bf16[384,1280]{1,0:T(8,128)(2,1)}, bf16[384,1280]{1,0:T(8,128)(2,1)}, u32[]{:S(2)}, u32[]{:S(2)}) collective-permute-start(bf16[384,1280]{1,0:T(8,128)(2,1)} %get-tuple-element.151), channel_id=1, source_target_pairs={{0,4},{1,5},{2,6},{3,7},{4,8},{5,9},{6,10},{7,11},{8,12},{9,13},{1... | collective-permute-start | bytes 2949128 | tf_op jit(solution)/shard_map/ppermute | solution.py:1109
  472.3 190.4 %collective-permute-start.9 = (bf16[384,1280]{1,0:T(8,128)(2,1)}, bf16[384,1280]{1,0:T(8,128)(2,1)}, u32[]{:S(2)}, u32[]{:S(2)}) collective-permute-start(bf16[384,1280]{1,0:T(8,128)(2,1)} %get-tuple-element.149), channel_id=1, source_target_pairs={{0,12},{1,13},{2,14},{3,15},{4,0},{5,1},{6,2},{7,3},{8,4},{9,5},{1... | collective-permute-start | bytes 2949128 | tf_op jit(solution)/shard_map/ppermute | solution.py:1109
  504.1 27.0 %copy-start.16 = (bf16[384,1280]{1,0:T(8,128)(2,1)S(1)}, bf16[384,1280]{1,0:T(8,128)(2,1)}, u32[]{:S(2)}) copy-start(bf16[384,1280]{1,0:T(8,128)(2,1)} %inputs.1) | copy-start | bytes 2949124
  504.1 27.0 %copy-start.62 = (f32[384]{0:T(512)S(1)}, f32[384]{0:T(512)}, u32[]{:S(2)}) copy-start(f32[384]{0:T(512)} %copy-done.61) | copy-start | bytes 4612
  649.3 13.3 %copy-start.64 = (bf16[40,128]{1,0:T(8,128)(2,1)S(1)}, bf16[40,128]{1,0:T(8,128)(2,1)}, u32[]{:S(2)}) copy-start(bf16[40,128]{1,0:T(8,128)(2,1)} %get-tuple-element.206) | copy-start | bytes 30724
  649.3 13.4 %copy-start.51 = (f32[40,16]{1,0:T(8,128)S(1)}, f32[40,16]{1,0:T(8,128)}, u32[]{:S(2)}) copy-start(f32[40,16]{1,0:T(8,128)} %copy.131) | copy-start | bytes 7684
  649.3 15.4 %copy-start.52 = (f32[2,40]{0,1:T(8,128)S(1)}, f32[2,40]{0,1:T(8,128)}, u32[]{:S(2)}) copy-start(f32[2,40]{0,1:T(8,128)} %copy.134) | copy-start | bytes 964
  649.3 15.4 %copy-start.53 = (f32[2,40]{0,1:T(8,128)S(1)}, f32[2,40]{0,1:T(8,128)}, u32[]{:S(2)}) copy-start(f32[2,40]{0,1:T(8,128)} %copy.132) | copy-start | bytes 964
  649.3 15.4 %copy-start.54 = (f32[2,40]{0,1:T(8,128)S(1)}, f32[2,40]{0,1:T(8,128)}, u32[]{:S(2)}) copy-start(f32[2,40]{0,1:T(8,128)} %copy.136) | copy-start | bytes 964
  649.4 17.4 %copy-start.17 = (bf16[384,1280]{1,0:T(8,128)(2,1)S(1)}, bf16[384,1280]{1,0:T(8,128)(2,1)}, u32[]{:S(2)}) copy-start(bf16[384,1280]{1,0:T(8,128)(2,1)} %inputs.1) | copy-start | bytes 2949124
  649.4 17.3 %copy-start.65 = (f32[384]{0:T(512)S(1)}, f32[384]{0:T(512)}, u32[]{:S(2)}) copy-start(f32[384]{0:T(512)} %get-tuple-element.361) | copy-start | bytes 4612
  (54 other events, 177.9 us)
Sparse Core Ops, SparseCore 0:
  209.3 102.1 all-gather.1
